TPU v7x, 32 devices: a whole 2x2x4 slice. The times are simulated.
32 devices in a mesh: seq: 8 (over z, x), head: 4 (over y, core).
Axes of the slice: x: 2, y: 2, z: 4, core: 2. Of those that a mesh axis runs over, the one named last changes fastest.
Arguments:
- queries: bfloat16 [768, 8192], P('head', 'seq'), may hold values from -6 to 6
- keys: bfloat16 [768, 8192], P('head', 'seq'), may hold values from -6 to 6
- values: bfloat16 [768, 8192], P('head', 'seq'), may hold values from -36 to 36
- slide_lengths: int32 [8], replicated, may hold values from 1 to 4096, 8192 in all
- norm_gain: float32 [768], P('head'), may hold values from 0.1 to 1.9
- norm_bias: float32 [768], P('head'), may hold values from -3 to 3
Outputs:
- encoded: bfloat16 [768, 8192], P('head', 'seq')
Inputs may be any that keep to these rules, and one draw needn't show every extreme that they name: `slide_lengths`: positive slide lengths that sum to 8192; the longest is exactly 4096.
All inputs are finite; a program needn't handle non-finite values.
Results may differ from a plain program's by a relative error of at most 0.0041.
Values may be sent and summed in bfloat16 or wider, within the bound.
No kernel may reach another device: no remote copies, remote signals or barrier semaphores. Data moves between devices by JAX's collectives and lax.ppermute only.
A program may use at most 128 MiB of HBM per device.

v0:
```python
import math

import jax
import jax.numpy as jnp
from jax import lax
from jax.sharding import PartitionSpec as P

D = 768
HD = 48
SEG = 1024


def partner_2(value, axis, distance):
    mask = 2**distance
    pairs = [(source, source ^ mask) for source in range(lax.axis_size(axis))]
    return lax.ppermute(value, axis, pairs)


def slide_of(positions, slide_ends):
    return jnp.sum((positions[..., None] >= slide_ends).astype(jnp.int32), axis=-1)


def attend(query_rows, key_rows, value_rows, query_slide, key_slide):
    score_scale = 1.0 / math.sqrt(HD)
    scores = (
        jnp.einsum("nhd,khd->hnk", query_rows, key_rows, preferred_element_type=jnp.float32)
        * score_scale
    )
    same_slide = query_slide.T[:, :, None] == key_slide.T[:, None, :]
    scores = jnp.where(same_slide, scores, -1e30)
    row_peak = jnp.max(scores, axis=-1)
    probabilities = jnp.exp(scores - row_peak[..., None])
    totals = jnp.sum(probabilities, axis=-1)
    weighted = jnp.einsum(
        "hnk,khd->nhd",
        probabilities.astype(jnp.bfloat16),
        value_rows,
        preferred_element_type=jnp.float32,
    )
    return (row_peak.T, totals.T, weighted)


def attend_segment(segment_items):
    return attend(*segment_items)


def pick_rows(shaped, dilation, chosen):
    leading = shaped.shape[:-3]
    row_count, head_count, head_size = shaped.shape[-3:]
    split = shaped.reshape(leading + (row_count // dilation, dilation, head_count, head_size))
    return jnp.sum(jnp.where(chosen[:, :, None], split, jnp.zeros((), shaped.dtype)), axis=-3)


def spread(compact, dilation, chosen, filler):
    extra = compact.ndim - 2
    widened = chosen.reshape(chosen.shape + (1,) * extra)
    full = jnp.where(widened[None], compact[:, None], filler)
    return full.reshape((compact.shape[0] * dilation,) + compact.shape[1:])


def collect(flat_pairs, first_bit, last_bit, seq_place):
    for bit_index in range(first_bit, last_bit):
        partner = partner_2(flat_pairs, "seq", bit_index)
        is_upper = seq_place // 2**bit_index % 2 == 1
        flat_pairs = jnp.where(
            is_upper,
            jnp.concatenate([partner, flat_pairs], axis=1),
            jnp.concatenate([flat_pairs, partner], axis=1),
        )
    return flat_pairs


def per_device(queries, keys, values, slide_lengths, norm_gain, norm_bias):
    queries = queries.T
    keys = keys.T
    values = values.T
    row_count, col_count = queries.shape
    head_count = col_count // HD
    seq_place = lax.axis_index("seq")
    total_rows = row_count * lax.axis_size("seq")
    slide_ends = jnp.cumsum(slide_lengths)
    head_ids = lax.axis_index("head") * head_count + jnp.arange(head_count, dtype=jnp.int32)
    row_start = seq_place * row_count
    q_shaped = queries.reshape(row_count, head_count, HD)
    kv_shaped = jnp.stack(
        [keys.reshape(row_count, head_count, HD), values.reshape(row_count, head_count, HD)]
    )
    running_peak = None
    weight = None
    accumulated = None
    for branch in range(4):
        dilation = 4**branch
        seg_span = min(SEG * dilation, total_rows)
        seg_keys = seg_span // dilation
        local_rows = row_count // dilation
        offsets = head_ids % dilation
        chosen = jnp.arange(dilation, dtype=jnp.int32)[:, None] == offsets[None, :]
        query_rows = pick_rows(q_shaped, dilation, chosen)
        query_pos = (
            row_start
            + dilation * jnp.arange(local_rows, dtype=jnp.int32)[:, None]
            + offsets[None, :]
        )
        query_slide = slide_of(query_pos, slide_ends)
        if seg_span <= row_count:
            key_value = pick_rows(kv_shaped, dilation, chosen)
            segment_count = row_count // seg_span
            items = (
                query_rows.reshape(segment_count, seg_keys, head_count, HD),
                key_value[0].reshape(segment_count, seg_keys, head_count, HD),
                key_value[1].reshape(segment_count, seg_keys, head_count, HD),
                query_slide.reshape(segment_count, seg_keys, head_count),
                query_slide.reshape(segment_count, seg_keys, head_count),
            )
            row_peak, totals, weighted = lax.map(attend_segment, items)
            row_peak = row_peak.reshape(local_rows, head_count)
            totals = totals.reshape(local_rows, head_count)
            weighted = weighted.reshape(local_rows, head_count, HD)
        else:
            group_size = seg_span // row_count
            bit_count = group_size.bit_length() - 1
            source = pick_rows(kv_shaped, dilation, chosen)
            first_bit = 0
            source_rows = source.shape[1]
            flat_pairs = collect(
                source.reshape(2, source_rows, col_count), first_bit, bit_count, seq_place
            )
            key_value = flat_pairs.reshape(2, seg_keys, head_count, HD)
            group_start = seq_place // group_size * seg_span
            key_pos = (
                group_start
                + dilation * jnp.arange(seg_keys, dtype=jnp.int32)[:, None]
                + offsets[None, :]
            )
            key_slide = slide_of(key_pos, slide_ends)
            row_peak, totals, weighted = attend(
                query_rows, key_value[0], key_value[1], query_slide, key_slide
            )
        peak_full = spread(row_peak, dilation, chosen, jnp.float32(-1e30))
        total_full = spread(totals, dilation, chosen, jnp.float32(0.0))
        mixed_full = spread(weighted, dilation, chosen, jnp.float32(0.0))
        if running_peak is None:
            running_peak, weight, accumulated = (peak_full, total_full, mixed_full)
        else:
            newest = jnp.maximum(running_peak, peak_full)
            keep_old = jnp.exp(running_peak - newest)
            keep_new = jnp.exp(peak_full - newest)
            weight = weight * keep_old + total_full * keep_new
            accumulated = accumulated * keep_old[..., None] + mixed_full * keep_new[..., None]
            running_peak = newest
    attended = (accumulated / weight[..., None]).reshape(row_count, col_count)
    feature_sums = lax.psum(
        (jnp.sum(attended, axis=1), jnp.sum(attended * attended, axis=1)), "head"
    )
    row_mean = feature_sums[0] / D
    variance = feature_sums[1] / D - row_mean * row_mean
    normed = (attended - row_mean[:, None]) * lax.rsqrt(variance + 1e-05)[:, None]
    return (normed * norm_gain + norm_bias).astype(jnp.bfloat16).T


def solution(mesh):
    placed = (P("head", "seq"), P("head", "seq"), P("head", "seq"), P(), P("head"), P("head"))
    return jax.shard_map(
        per_device, mesh=mesh, in_specs=placed, out_specs=P("head", "seq"), check_vma=False
    )
```

profile of v0, /device:TPU:0, one launch (start us, length us, event | category | flops | bytes accessed | tf_op | source)
XLA Modules:
  0.0 109.1 jit_solution(11684068147152647410)
XLA Ops:
  0.1 1.7 %stack.25 = bf16[1,16,64,4,48]{2,1,4,3,0:T(8,128)(2,1)S(1)} reshape(bf16[1024,192]{0,1:T(8,128)(2,1)} %bitcast.166) | data formatting | bytes 786432 | tf_op jit(solution)/shard_map/stack | solution.py:85
  1.8 1.6 %stack.26 = bf16[1,16,64,4,48]{2,1,4,3,0:T(8,128)(2,1)S(1)} reshape(bf16[1024,192]{0,1:T(8,128)(2,1)} %bitcast.172) | data formatting | bytes 786432 | tf_op jit(solution)/shard_map/stack | solution.py:85
  3.5 0.9 fusion.11
  5.1 2.9 %collective-permute-start.5 = (bf16[2,16,192]{2,1,0:T(8,128)(2,1)}, bf16[2,16,192]{2,1,0:T(8,128)(2,1)}, u32[]{:S(2)}, u32[]{:S(2)}) collective-permute-start(bf16[2,16,192]{2,1,0:T(8,128)(2,1)} %copy.249), channel_id=1, source_target_pairs={{0,4},{4,0},{8,12},{12,8},{16,20},{20,16},{24,28},{28,24},{1,5},{5... | collective-permute-start | bytes 36872 | tf_op jit(solution)/shard_map/ppermute | solution.py:16
  9.5 3.0 %fusion.8 = bf16[2,64,4,48]{3,2,1,0:T(4,128)(2,1)} fusion(bf16[1,64,16,4,48]{4,3,2,1,0:T(4,128)(2,1)S(1)} %stack.23, bf16[1,64,16,4,48]{4,3,2,1,0:T(4,128)(2,1)S(1)} %stack.22, pred[16,4]{1,0:T(8,128)(4,1)S(1)} %iota_compare_fusion), kind=kLoop, calls=%fused_computation.12 | loop fusion | flops 1155072 | bytes 835648 | tf_op jit(solution)/shard_map/reduce_sum | solution.py:51
  12.6 1.7 %copy.244 = bf16[2,64,4,48]{1,3,2,0:T(8,128)(2,1)} copy(bf16[2,64,4,48]{3,2,1,0:T(4,128)(2,1)} %fusion.8) | data formatting | bytes 98304 | tf_op jit(solution)/shard_map/reduce_sum | solution.py:51
  19.0 2.0 %collective-permute-start = (bf16[2,256,192]{1,2,0:T(8,128)(2,1)}, bf16[2,256,192]{1,2,0:T(8,128)(2,1)}, u32[]{:S(2)}, u32[]{:S(2)}) collective-permute-start(bf16[2,256,192]{1,2,0:T(8,128)(2,1)} %bitcast.13), channel_id=1, source_target_pairs={{0,4},{4,0},{8,12},{12,8},{16,20},{20,16},{24,28},{28,24},{1,5},{5... | collective-permute-start | bytes 589832 | tf_op jit(solution)/shard_map/ppermute | solution.py:16
  24.1 1.6 %reshape_reshape.12 = bf16[16,64,4,48]{1,0,3,2:T(8,128)(2,1)S(1)} reshape(bf16[1024,192]{0,1:T(8,128)(2,1)} %bitcast.169) | data formatting | bytes 786432 | tf_op jit(solution)/shard_map/reshape;reshape | solution.py:50
  33.4 1.6 %select_reduce_fusion.1 = bf16[256,4,48]{2,1,0:T(4,128)(2,1)} fusion(bf16[256,4,4,48]{3,2,1,0:T(4,128)(2,1)S(1)} %reshape_reshape.10, pred[4,4]{1,0:T(4,128)(4,1)S(1)} %copy-done.24), kind=kLoop, calls=%fused_computation.26 | loop fusion | flops 344064 | bytes 491536 | tf_op jit(solution)/shard_map/reduce_sum | solution.py:51
  35.7 4.8 %fusion.2 = (f32[4,1024]{1,0:T(4,128)S(1)}, f32[4,1024,1024]{1,2,0:T(8,128)S(1)}) fusion(s32[4,1024]{1,0:T(4,128)S(1)} %bitcast.182, bf16[1024,4,48]{0,2,1:T(8,128)(2,1)} %bitcast.170, bf16[1024,4,48]{0,2,1:T(8,128)(2,1)} %bitcast.167), kind=kOutput, calls=%fused_computation.4 | convolution fusion | flops 419426304 | bytes 17596416 | tf_op jit(solution)/shard_map/while/body/eval_jaxpr/nhd,khd->hnk/dot_general | solution.py:26
  40.6 5.6 %fusion = f32[4,1024]{1,0:T(4,128)} fusion(f32[4,1024,1024]{1,2,0:T(8,128)S(1)} %get-tuple-element.76, f32[4,1024]{1,0:T(4,128)S(1)} %get-tuple-element.75, s32[4,1024]{1,0:T(4,128)S(1)} %bitcast.183), kind=kLoop, calls=%fused_computation.2 | loop fusion | flops 20967424 | bytes 16826368 | tf_op jit(solution)/shard_map/while/body/eval_jaxpr/reduce_sum | solution.py:33
  47.2 1.6 %collective-permute-start.6 = (bf16[2,32,192]{2,1,0:T(8,128)(2,1)S(1)}, bf16[2,32,192]{2,1,0:T(8,128)(2,1)S(1)}, u32[]{:S(2)}, u32[]{:S(2)}) collective-permute-start(bf16[2,32,192]{2,1,0:T(8,128)(2,1)S(1)} %maximum_select_fusion.10), channel_id=1, source_target_pairs={{0,8},{4,12},{8,0},{12,4},{16,24},{20,28},{24,16},{28,20},{1,9},{5... | collective-permute-start | bytes 73736 | tf_op jit(solution)/shard_map/ppermute | solution.py:16
  50.6 0.9 broadcast_in_dim.405
  51.5 2.6 %collective-permute-start.7 = (bf16[2,64,192]{2,1,0:T(8,128)(2,1)S(1)}, bf16[2,64,192]{2,1,0:T(8,128)(2,1)S(1)}, u32[]{:S(2)}, u32[]{:S(2)}) collective-permute-start(bf16[2,64,192]{2,1,0:T(8,128)(2,1)S(1)} %maximum_select_fusion.9), channel_id=1, source_target_pairs={{0,16},{4,20},{8,24},{12,28},{16,0},{20,4},{24,8},{28,12},{1,17},{... | collective-permute-start | bytes 147464 | tf_op jit(solution)/shard_map/ppermute | solution.py:16
  54.2 1.2 %maximum_select_fusion.8 = bf16[2,128,192]{1,2,0:T(8,128)(2,1)S(1)} fusion(bf16[2,64,192]{1,2,0:T(8,128)(2,1)} %bitcast.23, bf16[2,64,192]{1,2,0:T(8,128)(2,1)} %collective-permute-done.2, pred[]{:T(512)S(6)} %eq.170), kind=kLoop, calls=%fused_computation.59 | loop fusion | flops 442368 | bytes 196609 | tf_op jit(solution)/shard_map/jit(_where)/select_n | solution.py:65
  55.4 1.3 %collective-permute-start.3 = (bf16[2,128,192]{1,2,0:T(8,128)(2,1)S(1)}, bf16[2,128,192]{1,2,0:T(8,128)(2,1)S(1)}, u32[]{:S(2)}, u32[]{:S(2)}) collective-permute-start(bf16[2,128,192]{1,2,0:T(8,128)(2,1)S(1)} %maximum_select_fusion.8), channel_id=1, source_target_pairs={{0,8},{4,12},{8,0},{12,4},{16,24},{20,28},{24,16},{28,20},{1,9},{5... | collective-permute-start | bytes 294920 | tf_op jit(solution)/shard_map/ppermute | solution.py:16
  58.2 1.3 %broadcast_in_dim.455 = f32[1024,4,48]{0,2,1:T(8,128)} reshape(f32[16,64,4,48]{1,0,3,2:T(8,128)S(1)} %broadcast_in_dim.443) | data formatting | bytes 1572864 | tf_op jit(solution)/shard_map/jit(_where)/broadcast_in_dim | solution.py:57
  59.5 1.3 %broadcast_in_dim.444 = f32[1024,192]{0,1:T(8,128)} reshape(f32[16,64,4,48]{1,0,3,2:T(8,128)S(1)} %broadcast_in_dim.443) | data formatting | bytes 1572864 | tf_op jit(solution)/shard_map/jit(_where)/broadcast_in_dim | solution.py:57
  60.9 2.8 %collective-permute-start.4 = (bf16[2,256,192]{1,2,0:T(8,128)(2,1)S(1)}, bf16[2,256,192]{1,2,0:T(8,128)(2,1)S(1)}, u32[]{:S(2)}, u32[]{:S(2)}) collective-permute-start(bf16[2,256,192]{1,2,0:T(8,128)(2,1)S(1)} %maximum_select_fusion.6), channel_id=1, source_target_pairs={{0,16},{4,20},{8,24},{12,28},{16,0},{20,4},{24,8},{28,12},{1,17},{... | collective-permute-start | bytes 589832 | tf_op jit(solution)/shard_map/ppermute | solution.py:16
  65.4 1.3 %maximum_select_fusion.4 = bf16[2,512,192]{1,2,0:T(8,128)(2,1)S(1)} fusion(bf16[2,256,192]{1,2,0:T(8,128)(2,1)} %bitcast.13, bf16[2,256,192]{1,2,0:T(8,128)(2,1)} %collective-permute-done, pred[]{:T(512)S(6)} %eq.170), kind=kLoop, calls=%fused_computation.50 | loop fusion | flops 1769472 | bytes 786433 | tf_op jit(solution)/shard_map/jit(_where)/select_n | solution.py:65
  66.7 1.9 %collective-permute-start.1 = (bf16[2,512,192]{1,2,0:T(8,128)(2,1)S(1)}, bf16[2,512,192]{1,2,0:T(8,128)(2,1)}, u32[]{:S(2)}, u32[]{:S(2)}) collective-permute-start(bf16[2,512,192]{1,2,0:T(8,128)(2,1)S(1)} %maximum_select_fusion.4), channel_id=1, source_target_pairs={{0,8},{4,12},{8,0},{12,4},{16,24},{20,28},{24,16},{28,20},{1,9},{5... | collective-permute-start | bytes 1179656 | tf_op jit(solution)/shard_map/ppermute | solution.py:16
  68.6 2.4 %collective-permute-done.4 = bf16[2,256,192]{1,2,0:T(8,128)(2,1)S(1)} collective-permute-done((bf16[2,256,192]{1,2,0:T(8,128)(2,1)S(1)}, bf16[2,256,192]{1,2,0:T(8,128)(2,1)S(1)}, u32[]{:S(2)}, u32[]{:S(2)}) %collective-permute-start.4) | collective-permute-done | bytes 196640 | tf_op jit(solution)/shard_map/ppermute | solution.py:16
  74.0 1.5 %copy.257 = f32[1024,4,48]{0,2,1:T(8,128)} copy(f32[1024,4,48]{2,0,1:T(8,128)S(1)} %bitcast.165) | data formatting | bytes 1572864 | tf_op jit(solution)/shard_map/jit(_where)/broadcast_in_dim | solution.py:57
  76.7 1.2 %copy.248 = f32[1024,192]{0,1:T(8,128)} copy(f32[1024,192]{1,0:T(8,128)S(1)} %broadcast_in_dim.431) | data formatting | bytes 1572864 | tf_op jit(solution)/shard_map/jit(_where)/broadcast_in_dim | solution.py:57
  77.9 1.3 %maximum_select_fusion.3 = bf16[2,1024,192]{1,2,0:T(8,128)(2,1)S(1)} fusion(bf16[2,512,192]{1,2,0:T(8,128)(2,1)S(1)} %maximum_select_fusion.4, bf16[2,512,192]{1,2,0:T(8,128)(2,1)} %collective-permute-done.1, pred[]{:T(512)S(6)} %eq.169), kind=kLoop, calls=%fused_computation.29 | loop fusion | flops 3538944 | bytes 1572865 | tf_op jit(solution)/shard_map/jit(_where)/select_n | solution.py:65
  79.3 1.1 fusion.7
  80.4 1.3 %fusion.5 = f32[4,256]{1,0:T(4,128)S(1)} fusion(f32[4,256,1024]{2,1,0:T(8,128)S(1)} %get-tuple-element.74, f32[4,256]{1,0:T(4,128)S(1)} %get-tuple-element.73, s32[4,1024]{1,0:T(4,128)S(1)} %bitcast.186, s32[4,256]{1,0:T(4,128)S(1)} %bitcast.199), kind=kLoop, calls=%fused_computation.8 | loop fusion | flops 5241856 | bytes 4222976 | tf_op jit(solution)/shard_map/reduce_sum | solution.py:33
  81.8 2.1 %fusion.19 = f32[256,4,48]{0,2,1:T(8,128)S(1)} fusion(bf16[1024,4,48]{0,2,1:T(8,128)(2,1)S(1)} %bitcast.177, f32[4,256,1024]{2,1,0:T(8,128)S(1)} %get-tuple-element.74, f32[4,256]{1,0:T(4,128)S(1)} %get-tuple-element.73, s32[4,1024]{1,0:T(4,128)S(1)} %bitcast.187, s32[4,256]{1,0:T(4,128)S(1)} %bitcast.200), kind=kOutput, calls=%fused_computation.20 | convolution fusion | flops 105906176 | bytes 4808704 | tf_op jit(solution)/shard_map/hnk,khd->nhd/dot_general | solution.py:34
  86.8 1.5 %copy.256 = f32[1024,4,48]{0,2,1:T(8,128)} copy(f32[1024,4,48]{2,0,1:T(8,128)S(1)} %bitcast.164) | data formatting | bytes 1572864 | tf_op jit(solution)/shard_map/jit(_where)/broadcast_in_dim | solution.py:57
  90.8 10.1 %fusion.56 = (f32[1024]{0:T(1024)}, f32[1024]{0:T(1024)}, f32[1024,4,48]{0,2,1:T(8,128)S(1)}) fusion(f32[1024,4]{0,1:T(4,128)S(1)} %get-tuple-element.54, f32[1024,4]{0,1:T(4,128)S(1)} %get-tuple-element.57, f32[1024,4,48]{0,2,1:T(8,128)} %broadcast_in_dim.455, pred[1024,4]{0,1:T(4,128)(4,1)} %broadcast_in_dim.433, f32[1024,4]{0,1:T(4,128)S(1)} %get-tuple-element.59, ...), kind=kOutput, calls=%fused_computation.120 | convolution fusion | flops 426768384 | bytes 20484096 | tf_op jit(solution)/shard_map/while/body/eval_jaxpr/hnk,khd->nhd/dot_general | solution.py:34
  101.0 5.9 %all-reduce = (f32[1024]{0:T(1024)S(1)}, f32[1024]{0:T(1024)S(1)}) all-reduce(f32[1024]{0:T(1024)} %get-tuple-element.49, f32[1024]{0:T(1024)} %get-tuple-element.48), channel_id=1, replica_groups=mesh['seq'=8,'head'=4] {'head'}, use_global_device_ids=true, to_apply=%region_25.26 | all-reduce | flops 2048 | bytes 16384 | tf_op jit(solution)/shard_map/psum | solution.py:152
  106.9 2.2 %fusion.31 = bf16[1024,192]{0,1:T(8,128)(2,1)} fusion(f32[1024,192]{0,1:T(8,128)S(1)} %copy-done.2, f32[1024,192]{0,1:T(8,128)S(1)} %copy-done.1, f32[1024,192]{0,1:T(8,128)S(1)} %copy.239, f32[1024,4,48]{0,2,1:T(8,128)S(1)} %get-tuple-element.79, f32[192]{0:T(256)} %param.11, f32[192]{0:T(256)} %param.10, f32[1024]{0:T(1024)S(1)} %get-tuple-element.68, ...), kind=kLoop, calls=%fused_computation.46 | loop fusion | flops 3342336 | bytes 3659264 | tf_op jit(solution)/shard_map/convert_element_type | solution.py:158
  (158 shorter events, 33.8 us)
Async XLA Ops:
  0.0 8.0 %copy-start.3 = (bf16[192,1024]{1,0:T(8,128)(2,1)S(1)}, bf16[192,1024]{1,0:T(8,128)(2,1)}, u32[]{:S(2)}) copy-start(bf16[192,1024]{1,0:T(8,128)(2,1)} %param.7) | copy-start | bytes 1179652
  0.0 8.2 %copy-start.5 = (bf16[192,1024]{1,0:T(8,128)(2,1)S(1)}, bf16[192,1024]{1,0:T(8,128)(2,1)}, u32[]{:S(2)}) copy-start(bf16[192,1024]{1,0:T(8,128)(2,1)} %param.8) | copy-start | bytes 1179652
  0.1 31.9 %copy-start.21 = (pred[64,4]{0,1:T(4,128)(4,1)}, pred[64,4]{0,1:T(4,128)(4,1)S(1)}, u32[]{:S(2)}) copy-start(pred[64,4]{0,1:T(4,128)(4,1)S(1)} %iota_compare_fusion.1) | copy-start | bytes 772
  5.1 41.3 %collective-permute-start.5 = (bf16[2,16,192]{2,1,0:T(8,128)(2,1)}, bf16[2,16,192]{2,1,0:T(8,128)(2,1)}, u32[]{:S(2)}, u32[]{:S(2)}) collective-permute-start(bf16[2,16,192]{2,1,0:T(8,128)(2,1)} %copy.249), channel_id=1, source_target_pairs={{0,4},{4,0},{8,12},{12,8},{16,20},{20,16},{24,28},{28,24},{1,5},{5... | collective-permute-start | bytes 36872 | tf_op jit(solution)/shard_map/ppermute | solution.py:16
  8.5 24.0 %copy-start.16 = (pred[16,4]{1,0:T(8,128)(4,1)}, pred[16,4]{1,0:T(8,128)(4,1)S(1)}, u32[]{:S(2)}) copy-start(pred[16,4]{1,0:T(8,128)(4,1)S(1)} %iota_compare_fusion) | copy-start | bytes 196
  12.6 11.3 %copy-start.4 = (bf16[192,1024]{1,0:T(8,128)(2,1)S(1)}, bf16[192,1024]{1,0:T(8,128)(2,1)}, u32[]{:S(2)}) copy-start(bf16[192,1024]{1,0:T(8,128)(2,1)} %param.6) | copy-start | bytes 1179652
  14.3 39.9 %collective-permute-start.2 = (bf16[2,64,192]{1,2,0:T(8,128)(2,1)}, bf16[2,64,192]{1,2,0:T(8,128)(2,1)}, u32[]{:S(2)}, u32[]{:S(2)}) collective-permute-start(bf16[2,64,192]{1,2,0:T(8,128)(2,1)} %bitcast.23), channel_id=1, source_target_pairs={{0,4},{4,0},{8,12},{12,8},{16,20},{20,16},{24,28},{28,24},{1,5},{5... | collective-permute-start | bytes 147464 | tf_op jit(solution)/shard_map/ppermute | solution.py:16
  16.5 6.2 %copy-start.23 = (pred[4,4]{1,0:T(4,128)(4,1)}, pred[4,4]{1,0:T(4,128)(4,1)S(1)}, u32[]{:S(2)}) copy-start(pred[4,4]{1,0:T(4,128)(4,1)S(1)} %iota_compare_fusion.2) | copy-start | bytes 52
  19.0 46.4 %collective-permute-start = (bf16[2,256,192]{1,2,0:T(8,128)(2,1)}, bf16[2,256,192]{1,2,0:T(8,128)(2,1)}, u32[]{:S(2)}, u32[]{:S(2)}) collective-permute-start(bf16[2,256,192]{1,2,0:T(8,128)(2,1)} %bitcast.13), channel_id=1, source_target_pairs={{0,4},{4,0},{8,12},{12,8},{16,20},{20,16},{24,28},{28,24},{1,5},{5... | collective-permute-start | bytes 589832 | tf_op jit(solution)/shard_map/ppermute | solution.py:16
  24.1 4.2 %copy-start.28 = (s32[16]{0:T(128)S(1)}, s32[16]{0:T(128)}, u32[]{:S(2)}) copy-start(s32[16]{0:T(128)} %multiply_add_fusion.4) | copy-start | bytes 196
  24.1 4.9 %copy-start.27 = (s32[64]{0:T(128)S(1)}, s32[64]{0:T(128)}, u32[]{:S(2)}) copy-start(s32[64]{0:T(128)} %multiply_add_fusion.5) | copy-start | bytes 772
  24.1 4.9 %copy-start.26 = (s32[256]{0:T(256)S(1)}, s32[256]{0:T(256)}, u32[]{:S(2)}) copy-start(s32[256]{0:T(256)} %multiply_add_fusion.2) | copy-start | bytes 3076
  24.1 9.2 %copy-start.24 = (pred[4,4]{1,0:T(4,128)(4,1)S(1)}, pred[4,4]{1,0:T(4,128)(4,1)}, u32[]{:S(2)}) copy-start(pred[4,4]{1,0:T(4,128)(4,1)} %copy-done.23) | copy-start | bytes 52
  24.1 10.8 %copy-start.19 = (s32[1024]{0:T(1024)S(1)}, s32[1024]{0:T(1024)}, u32[]{:S(2)}) copy-start(s32[1024]{0:T(1024)} %iota_add_fusion) | copy-start | bytes 12292
  40.5 5.7 %copy-start = (f32[4,1024,1024]{1,2,0:T(8,128)}, f32[4,1024,1024]{1,2,0:T(8,128)S(1)}, u32[]{:S(2)}) copy-start(f32[4,1024,1024]{1,2,0:T(8,128)S(1)} %get-tuple-element.76) | copy-start | bytes 50331652
  40.6 5.7 %copy-start.15 = (f32[4,1024]{1,0:T(4,128)}, f32[4,1024]{1,0:T(4,128)S(1)}, u32[]{:S(2)}) copy-start(f32[4,1024]{1,0:T(4,128)S(1)} %get-tuple-element.75) | copy-start | bytes 49156
  40.6 8.5 %copy-start.17 = (pred[16,4]{1,0:T(8,128)(4,1)S(1)}, pred[16,4]{1,0:T(8,128)(4,1)}, u32[]{:S(2)}) copy-start(pred[16,4]{1,0:T(8,128)(4,1)} %copy-done.16) | copy-start | bytes 196
  40.6 8.5 %copy-start.22 = (pred[64,4]{0,1:T(4,128)(4,1)S(1)}, pred[64,4]{0,1:T(4,128)(4,1)}, u32[]{:S(2)}) copy-start(pred[64,4]{0,1:T(4,128)(4,1)} %copy-done.21) | copy-start | bytes 772
  47.2 4.3 %collective-permute-start.6 = (bf16[2,32,192]{2,1,0:T(8,128)(2,1)S(1)}, bf16[2,32,192]{2,1,0:T(8,128)(2,1)S(1)}, u32[]{:S(2)}, u32[]{:S(2)}) collective-permute-start(bf16[2,32,192]{2,1,0:T(8,128)(2,1)S(1)} %maximum_select_fusion.10), channel_id=1, source_target_pairs={{0,8},{4,12},{8,0},{12,4},{16,24},{20,28},{24,16},{28,20},{1,9},{5... | collective-permute-start | bytes 73736 | tf_op jit(solution)/shard_map/ppermute | solution.py:16
  51.5 5.3 %collective-permute-start.7 = (bf16[2,64,192]{2,1,0:T(8,128)(2,1)S(1)}, bf16[2,64,192]{2,1,0:T(8,128)(2,1)S(1)}, u32[]{:S(2)}, u32[]{:S(2)}) collective-permute-start(bf16[2,64,192]{2,1,0:T(8,128)(2,1)S(1)} %maximum_select_fusion.9), channel_id=1, source_target_pairs={{0,16},{4,20},{8,24},{12,28},{16,0},{20,4},{24,8},{28,12},{1,17},{... | collective-permute-start | bytes 147464 | tf_op jit(solution)/shard_map/ppermute | solution.py:16
  55.4 5.5 %collective-permute-start.3 = (bf16[2,128,192]{1,2,0:T(8,128)(2,1)S(1)}, bf16[2,128,192]{1,2,0:T(8,128)(2,1)S(1)}, u32[]{:S(2)}, u32[]{:S(2)}) collective-permute-start(bf16[2,128,192]{1,2,0:T(8,128)(2,1)S(1)} %maximum_select_fusion.8), channel_id=1, source_target_pairs={{0,8},{4,12},{8,0},{12,4},{16,24},{20,28},{24,16},{28,20},{1,9},{5... | collective-permute-start | bytes 294920 | tf_op jit(solution)/shard_map/ppermute | solution.py:16
  58.2 13.0 %copy-start.20 = (s32[512,4]{0,1:T(4,128)S(1)}, s32[512,4]{0,1:T(4,128)}, u32[]{:S(2)}) copy-start(s32[512,4]{0,1:T(4,128)} %convert_reduce_fusion.2) | copy-start | bytes 24580
  60.9 10.1 %collective-permute-start.4 = (bf16[2,256,192]{1,2,0:T(8,128)(2,1)S(1)}, bf16[2,256,192]{1,2,0:T(8,128)(2,1)S(1)}, u32[]{:S(2)}, u32[]{:S(2)}) collective-permute-start(bf16[2,256,192]{1,2,0:T(8,128)(2,1)S(1)} %maximum_select_fusion.6), channel_id=1, source_target_pairs={{0,16},{4,20},{8,24},{12,28},{16,0},{20,4},{24,8},{28,12},{1,17},{... | collective-permute-start | bytes 589832 | tf_op jit(solution)/shard_map/ppermute | solution.py:16
  66.7 11.2 %collective-permute-start.1 = (bf16[2,512,192]{1,2,0:T(8,128)(2,1)S(1)}, bf16[2,512,192]{1,2,0:T(8,128)(2,1)}, u32[]{:S(2)}, u32[]{:S(2)}) collective-permute-start(bf16[2,512,192]{1,2,0:T(8,128)(2,1)S(1)} %maximum_select_fusion.4), channel_id=1, source_target_pairs={{0,8},{4,12},{8,0},{12,4},{16,24},{20,28},{24,16},{28,20},{1,9},{5... | collective-permute-start | bytes 1179656 | tf_op jit(solution)/shard_map/ppermute | solution.py:16
  90.7 10.2 %copy-start.8 = (f32[1024,4]{0,1:T(4,128)}, f32[1024,4]{0,1:T(4,128)S(1)}, u32[]{:S(2)}) copy-start(f32[1024,4]{0,1:T(4,128)S(1)} %get-tuple-element.54) | copy-start | bytes 49156
  90.7 10.2 %copy-start.9 = (f32[1024,4]{0,1:T(4,128)}, f32[1024,4]{0,1:T(4,128)S(1)}, u32[]{:S(2)}) copy-start(f32[1024,4]{0,1:T(4,128)S(1)} %get-tuple-element.55) | copy-start | bytes 49156
  90.7 10.2 %copy-start.10 = (f32[1024,4]{0,1:T(4,128)}, f32[1024,4]{0,1:T(4,128)S(1)}, u32[]{:S(2)}) copy-start(f32[1024,4]{0,1:T(4,128)S(1)} %get-tuple-element.56) | copy-start | bytes 49156
  90.8 10.2 %copy-start.11 = (f32[1024,4]{0,1:T(4,128)}, f32[1024,4]{0,1:T(4,128)S(1)}, u32[]{:S(2)}) copy-start(f32[1024,4]{0,1:T(4,128)S(1)} %get-tuple-element.57) | copy-start | bytes 49156
  90.8 10.2 %copy-start.12 = (f32[1024,4]{0,1:T(4,128)}, f32[1024,4]{0,1:T(4,128)S(1)}, u32[]{:S(2)}) copy-start(f32[1024,4]{0,1:T(4,128)S(1)} %get-tuple-element.58) | copy-start | bytes 49156
  90.8 10.2 %copy-start.13 = (f32[1024,4]{0,1:T(4,128)}, f32[1024,4]{0,1:T(4,128)S(1)}, u32[]{:S(2)}) copy-start(f32[1024,4]{0,1:T(4,128)S(1)} %get-tuple-element.59) | copy-start | bytes 49156
  90.8 16.1 %copy-start.1 = (f32[1024,192]{0,1:T(8,128)S(1)}, f32[1024,192]{0,1:T(8,128)}, u32[]{:S(2)}) copy-start(f32[1024,192]{0,1:T(8,128)} %copy.248) | copy-start | bytes 2359300
  90.8 16.1 %copy-start.2 = (f32[1024,192]{0,1:T(8,128)S(1)}, f32[1024,192]{0,1:T(8,128)}, u32[]{:S(2)}) copy-start(f32[1024,192]{0,1:T(8,128)} %broadcast_in_dim.444) | copy-start | bytes 2359300
  (6 other events, 15.8 us)
where the time goes:
time: 110 us; the launch traced here: 109 us
  other arithmetic  33.2 us (30%)
  local copies, waits for them, and re-layouts  32.3 us (29%)
  matrix products  19.2 us (17%)
  starting transfers between devices  15.2 us (14%)
  blocking collectives  5.9 us (5%)
  waiting for transfers between devices  2.62 us (2%)
    broadcast_in_dim x31, local copies, waits for them, and re-layouts, spread(): full = jnp.where(widened[None], compact[:, None], filler)  18.2 us
    ppermute x8, starting transfers between devices, partner_2(): return lax.ppermute(value, axis, pairs)  15.2 us
    dot_general x4, matrix products, attend(): jnp.einsum('hnk,khd->nhd', probabilities.astype(jnp.bfloat16), value_rows...  12.7 us
    reduce_sum x6, other arithmetic, pick_rows(): jnp.sum(jnp.where(chosen[:, :, None], split, jnp.zeros((), shaped.dtype))...  7.81 us
    reduce_sum x4, other arithmetic, attend(): totals = jnp.sum(probabilities, axis=-1)  7.27 us
    another operation x8, local copies, waits for them, and re-layouts, per_device(): jnp.stack([keys.reshape(row_count, head_count, HD), values.reshape(row_co...  6.97 us
    dot_general x4, matrix products, attend(): jnp.einsum('nhd,khd->hnk', query_rows, key_rows, preferred_element_type=j...  6.47 us
    psum x1, blocking collectives, per_device(): lax.psum((jnp.sum(attended, axis=1), jnp.sum(attended * attended, axis=1)...  5.9 us
  transfers between devices with their start and end apart: 8, of which 2 were waited for; matrix products, arithmetic and copies ran while one was open for 50% of the time, Pallas kernels for 0%

commit v1 on v0

v1 whole, which is shorter than its diff:
```python
import functools
import math

import jax
import jax.numpy as jnp
import numpy as np
from jax import lax
from jax.experimental import pallas as pl
from jax.experimental.pallas import tpu as pltpu
from jax.sharding import PartitionSpec as P

D = 768
HD = 48
SEG = 1024
HEADS = 4
BLOCKED = -1e30
SCALE = 1.0 / math.sqrt(HD)
LOG2_SCALE = math.log2(math.e) * SCALE
QUERY_CHUNK = 256
F32 = jnp.float32
BF16 = jnp.bfloat16
VMEM = pl.BlockSpec(memory_space=pltpu.VMEM)
SMEM = pl.BlockSpec(memory_space=pltpu.SMEM)
PARAMS = pltpu.CompilerParams(vmem_limit_bytes=40 * 2**20)


def partner(value, axis, mask):
    pairs = [(source, source ^ mask) for source in range(lax.axis_size(axis))]
    return lax.ppermute(value, axis, pairs)


def thirds(value):
    parts = []
    for _ in range(3):
        part = float(np.asarray(value, jnp.bfloat16))
        parts.append(part)
        value -= part
    return parts


def bias_rows(flags, factor):
    return [jnp.where(flags, F32(part), F32(0.0)) for part in thirds(math.log(factor) / SCALE)]


def flag_rows(flags):
    return [jnp.where(flags, F32(1.0), F32(0.0))] * 3


def slide_of(positions, lengths_ref):
    slide = jnp.zeros(positions.shape, jnp.int32)
    end = jnp.int32(0)
    for k in range(lengths_ref.shape[0]):
        end = end + lengths_ref[k]
        slide = slide + jnp.where(positions >= end, 1, 0)
    return slide


def stack_rows(rows, count):
    width = rows[0].shape[1]
    index = lax.broadcasted_iota(jnp.int32, (count, width), 0)
    block = jnp.zeros((count, width), F32)
    for k, row in enumerate(rows):
        block = jnp.where(index == k, row, block)
    return block


def lanes(width):
    return lax.broadcasted_iota(jnp.int32, (1, width), 1)


def compact_index(place, head_place):
    quarter = place >> 6
    return 16 * (place & 15) + 4 * ((place >> 4) & 3) + ((quarter + head_place) & 3)


def pack_kernel(k_ref, v_ref, quarter_ref, sixteenth_ref):
    rows = k_ref.shape[1]
    packed = rows // 4
    head_place = lax.axis_index("head")
    place = lax.broadcasted_iota(jnp.int32, (packed, rows), 0)
    group = lax.broadcasted_iota(jnp.int32, (packed, rows), 1) >> 2
    pick = jnp.where(compact_index(place, head_place) == group, F32(1.0), F32(0.0)).astype(BF16)
    own = lanes(rows) & 3
    results = []
    for ref in (k_ref, v_ref):
        masked = jnp.concatenate(
            [
                ref[i * HD : (i + 1) * HD, :]
                * jnp.broadcast_to(jnp.where(own == i, F32(1.0), F32(0.0)), (HD, rows)).astype(BF16)
                for i in range(HEADS)
            ],
            axis=0,
        )
        results.append(
            lax.dot_general(masked, pick, (((1,), (1,)), ((), ())), preferred_element_type=F32)
        )
    features = HEADS * HD
    quarter_ref[:features, :] = results[0].astype(BF16)
    quarter_ref[features:, :] = results[1].astype(BF16)
    few = packed // 4
    sixteenth_ref[...] = jnp.concatenate([results[0][:, :few], results[1][:, :few]], axis=1).astype(BF16)


def weigh(keys_t, queries, values):
    scores = jnp.dot(keys_t, queries, preferred_element_type=F32)
    peak = jnp.max(scores, axis=0, keepdims=True)
    probs = jnp.exp2((scores - peak) * LOG2_SCALE).astype(BF16)
    return peak, jnp.dot(values, probs, preferred_element_type=F32)


def local_kernel(first, lengths_ref, q_ref, k_ref, v_ref, out_ref):
    rows = q_ref.shape[1]
    slides = lengths_ref.shape[0]
    tile = lanes(rows)
    position = lax.axis_index("seq") * rows + tile
    head_place = lax.axis_index("head")
    slide = slide_of(position, lengths_ref)
    row = lax.broadcasted_iota(jnp.int32, (slides, rows), 0)
    same = slide == row
    query_slides = jnp.where(same, F32(1.0), F32(0.0))
    key_slides = jnp.where(same, F32(0.0), F32(BLOCKED))
    extra = -(-(slides + 9) // 16) * 16 - slides
    ones = jnp.ones((16, rows), BF16)
    for head in range(out_ref.shape[0]):
        i = first + head
        mine = slice(i * HD, (i + 1) * HD)
        second = (tile & 3) == i
        third = (tile & 15) == 4 * head_place + i
        fourth = (tile & 63) == 4 * head_place + i
        query_extra = stack_rows(flag_rows(second) + flag_rows(third) + flag_rows(fourth), extra)
        key_extra = stack_rows(
            bias_rows(second, 2.0) + bias_rows(third, 1.5) + bias_rows(fourth, 4.0 / 3.0), extra
        )
        queries = jnp.concatenate(
            [q_ref[mine, :], jnp.concatenate([query_slides, query_extra], axis=0).astype(BF16)], axis=0
        )
        keys = jnp.concatenate(
            [k_ref[mine, :], jnp.concatenate([key_slides, key_extra], axis=0).astype(BF16)], axis=0
        )
        keys_t = keys.T
        values = jnp.concatenate([v_ref[mine, :], ones], axis=0)
        for start in range(0, rows, QUERY_CHUNK):
            chunk = slice(start, start + QUERY_CHUNK)
            peak, mixed = weigh(keys_t, queries[:, chunk], values)
            out_ref[head, : HD + 8, chunk] = mixed[: HD + 8]
            out_ref[head, HD + 8 :, chunk] = jnp.broadcast_to(peak, (8, peak.shape[1]))


def distant_kernel(kinds, distances, lengths_ref, q_ref, local_a_ref, local_b_ref, *refs):
    pieces, (att_ref, sums_ref, k_ref, v_ref) = refs[: len(kinds)], refs[len(kinds) :]
    rows = q_ref.shape[1]
    features = HEADS * HD
    slides = lengths_ref.shape[0]
    tile = lanes(rows)
    seq_place = lax.axis_index("seq")
    head_place = lax.axis_index("head")
    extra = -(-(HEADS * slides + 8) // 16) * 16 - HEADS * slides

    at = 0
    spans = []
    for kind, distance, piece in zip(kinds, distances, pieces):
        count = rows // 4**kind
        place = lanes(count)
        group = compact_index(place, head_place)
        base = (seq_place ^ distance) * rows + 4 * group
        row = lax.broadcasted_iota(jnp.int32, (slides, count), 0)
        masks = [
            jnp.where(slide_of(base + i, lengths_ref) == row, F32(0.0), F32(BLOCKED))
            for i in range(HEADS)
        ]
        none = jnp.zeros((1, count), F32)
        always = none == 0.0
        in_third = place < rows // 16
        in_fourth = place < rows // 64
        if kind == 1:
            added = bias_rows(in_third, 2.0) + bias_rows(in_fourth, 1.5) + [none, none]
        elif kind == 2:
            added = [none] * 3 + bias_rows(in_fourth, 2.0) + [none + BLOCKED, none]
        else:
            added = [none] * 6 + [none, none + BLOCKED]
        masks.append(stack_rows(added, extra))
        mask_rows = jnp.concatenate(masks, axis=0).astype(BF16)
        if kind == 1:
            key_rows = piece[:features, :]
        else:
            key_rows = piece[:, :count]
        k_ref[at : at + count, :] = jnp.concatenate([key_rows, mask_rows], axis=0).T
        spans.append((at, count))
        at += count
    total_keys = at

    at = 0
    pending = []
    for kind, piece in zip(kinds, pieces):
        count = rows // 4**kind
        if kind == 1:
            v_ref[:features, at : at + count] = piece[features:, :]
            at += count
        else:
            half = rows // 16
            pending.append(piece[:, half : half + count])
            if sum(p.shape[1] for p in pending) == 256:
                v_ref[:features, at : at + 256] = jnp.concatenate(pending, axis=1)
                pending = []
                at += 256
    if pending:
        width = sum(p.shape[1] for p in pending)
        v_ref[:features, at : at + width] = jnp.concatenate(pending, axis=1)
    v_ref[features:, :] = jnp.ones((16, total_keys), BF16)

    slide = slide_of(seq_place * rows + tile, lengths_ref)
    row = lax.broadcasted_iota(jnp.int32, (slides, rows), 0)
    same = slide == row
    masks = [jnp.where(same & ((tile & 3) == i), F32(1.0), F32(0.0)) for i in range(HEADS)]
    third = ((tile >> 2) & 3) == head_place
    fourth = ((tile >> 2) & 15) == head_place
    masks.append(
        stack_rows(
            flag_rows(third) + flag_rows(fourth) + flag_rows(~third)[:1] + flag_rows(~fourth)[:1],
            extra,
        )
    )
    mask_rows = jnp.concatenate(masks, axis=0).astype(BF16)
    queries = jnp.concatenate(
        [
            q_ref[i * HD : (i + 1) * HD, :]
            * jnp.broadcast_to(jnp.where((tile & 3) == i, F32(1.0), F32(0.0)), (HD, rows)).astype(BF16)
            for i in range(HEADS)
        ]
        + [mask_rows],
        axis=0,
    )
    for start in range(0, rows, QUERY_CHUNK):
        chunk = slice(start, start + QUERY_CHUNK)
        peak, mixed = weigh(k_ref[...], queries[:, chunk], v_ref[...])
        total = mixed[features : features + 1]
        own = lanes(QUERY_CHUNK) & 3
        sums = squares = None
        for i in range(HEADS):
            ref = (local_a_ref, local_b_ref)[i // 2]
            selected = own == i
            here = ref[i % 2, HD + 8 : HD + 9, chunk]
            there = jnp.where(selected, peak, F32(BLOCKED))
            top = jnp.maximum(here, there)
            keep = jnp.exp2((here - top) * LOG2_SCALE)
            add = jnp.where(selected, jnp.exp2((there - top) * LOG2_SCALE), F32(0.0))
            inverse = 1.0 / (keep * ref[i % 2, HD : HD + 1, chunk] + add * total)
            attended = (
                ref[i % 2, :HD, chunk] * (keep * inverse)
                + mixed[i * HD : (i + 1) * HD] * (add * inverse)
            )
            att_ref[i * HD : (i + 1) * HD, chunk] = attended
            head_sum = jnp.sum(attended, axis=0, keepdims=True)
            head_squares = jnp.sum(attended * attended, axis=0, keepdims=True)
            sums = head_sum if sums is None else sums + head_sum
            squares = head_squares if squares is None else squares + head_squares
        at = start // QUERY_CHUNK
        sums_ref[at : at + 1, :] = sums
        sums_ref[4 + at : 5 + at, :] = squares


def norm_kernel(att_ref, gain_ref, bias_ref, *refs):
    sum_refs, out_ref = refs[:-1], refs[-1]
    features, rows = att_ref.shape
    r = lax.broadcasted_iota(jnp.int32, (features, features), 0)
    c = lax.broadcasted_iota(jnp.int32, (features, features), 1)
    columns = [
        jnp.sum(jnp.where(r == c, ref[...], 0.0), axis=1, keepdims=True)
        for ref in (gain_ref, bias_ref)
    ]
    sums = sum_refs[0][...]
    for ref in sum_refs[1:]:
        sums = sums + ref[...]
    mean = sums[:4] / D
    variance = sums[4:] / D - mean * mean
    inverse = lax.rsqrt(variance + 1e-05)
    for at in range(rows // QUERY_CHUNK):
        chunk = slice(at * QUERY_CHUNK, (at + 1) * QUERY_CHUNK)
        normed = (att_ref[:, chunk] - mean[at : at + 1]) * inverse[at : at + 1]
        out_ref[:, chunk] = (normed * columns[0] + columns[1]).astype(BF16)


def cost(flops, moved, exps=0):
    return pl.CostEstimate(flops=int(flops), bytes_accessed=int(moved), transcendentals=int(exps))


def per_device(queries, keys, values, slide_lengths, norm_gain, norm_bias):
    features, rows = queries.shape
    devices = lax.axis_size("seq")
    total_rows = rows * devices
    spans = [min(SEG * 4**b, total_rows) // rows for b in range(4)]

    quarter, sixteenth = pl.pallas_call(
        pack_kernel,
        out_shape=(
            jax.ShapeDtypeStruct((2 * features, rows // 4), BF16),
            jax.ShapeDtypeStruct((features, rows // 8), BF16),
        ),
        in_specs=[VMEM, VMEM],
        out_specs=(VMEM, VMEM),
        compiler_params=PARAMS,
        cost_estimate=cost(2 * 384 * 256 * 1024, 10**6),
        name="pack",
    )(keys, values)

    def local(first, *operands):
        return pl.pallas_call(
            functools.partial(local_kernel, first),
            out_shape=jax.ShapeDtypeStruct((2, HD + 16, rows), F32),
            in_specs=[SMEM, VMEM, VMEM, VMEM],
            out_specs=VMEM,
            compiler_params=PARAMS,
            cost_estimate=cost(2 * 2 * rows * rows * 512, 10**6, 2 * rows * rows),
            name="local",
        )(*operands)

    near = [(partner(quarter, "seq", m), m) for m in range(1, spans[1])]
    beyond = [
        (partner(sixteenth, "seq", m), m) for m in range(spans[2], spans[3], spans[2])
    ]
    beyond = beyond + [
        (partner(piece, "seq", m), m ^ d)
        for m in range(spans[1], spans[2], spans[1])
        for piece, d in [(sixteenth, 0)] + beyond
    ]
    local_a = local(0, slide_lengths, queries, keys, values)
    held, beyond_pieces = lax.optimization_barrier((queries, [piece for piece, _ in beyond]))
    beyond = [(piece, d) for piece, (_, d) in zip(beyond_pieces, beyond)]
    beyond = beyond + [
        (partner(piece, "seq", m), m ^ d) for m in range(1, spans[1]) for piece, d in beyond
    ]
    local_b = local(2, slide_lengths, held, keys, values)
    pieces = [(piece, d, 1) for piece, d in near]
    pieces += [(piece, d, 2 if d < spans[2] else 3) for piece, d in beyond]
    kinds = [kind for _, _, kind in pieces]
    distances = [d for _, d, _ in pieces]
    key_count = sum(rows // 4**kind for kind in kinds)
    depth = features + -(-(HEADS * slide_lengths.shape[0] + 8) // 16) * 16

    attended, sums = pl.pallas_call(
        functools.partial(distant_kernel, kinds, distances),
        out_shape=(
            jax.ShapeDtypeStruct((features, rows), F32),
            jax.ShapeDtypeStruct((8, rows // 4), F32),
        ),
        in_specs=[SMEM] + [VMEM] * (3 + len(pieces)),
        out_specs=(VMEM, VMEM),
        scratch_shapes=[
            pltpu.VMEM((key_count, depth), BF16),
            pltpu.VMEM((features + 16, key_count), BF16),
        ],
        compiler_params=PARAMS,
        cost_estimate=cost(2 * rows * key_count * 512, 10**6, rows * key_count),
        name="distant",
    )(slide_lengths, queries, local_a, local_b, *[piece for piece, _, _ in pieces])

    all_sums = [sums] + [partner(sums, "head", m) for m in range(1, lax.axis_size("head"))]
    return pl.pallas_call(
        norm_kernel,
        out_shape=jax.ShapeDtypeStruct((features, rows), BF16),
        in_specs=[VMEM] * (3 + len(all_sums)),
        out_specs=VMEM,
        compiler_params=PARAMS,
        name="norm",
    )(attended, norm_gain[None, :], norm_bias[None, :], *all_sums)


def solution(mesh):
    placed = (P("head", "seq"), P("head", "seq"), P("head", "seq"), P(), P("head"), P("head"))
    return jax.shard_map(
        per_device, mesh=mesh, in_specs=placed, out_specs=P("head", "seq"), check_vma=False
    )
```

time: 110 us -> 37 us (0.34)
  other arithmetic: 33.2 us -> 0 us
  local copies, waits for them, and re-layouts: 32.3 us -> 3.68 us
  matrix products: 19.2 us -> 0 us
  Pallas kernels: 0 us -> 18 us
  blocking collectives: 5.9 us -> 0 us
  starting transfers between devices: 15.2 us -> 13.1 us
    dot_general x8 -> x0, matrix products: 19.2 us -> none  [the longest x4 12.7 us: attend(): jnp.einsum('hnk,khd->nhd', probabilities.astype(jnp.bfloat16), value_rows...]
    broadcast_in_dim x31 -> x0, local copies, waits for them, and re-layouts: 18.2 us -> none  [spread(): full = jnp.where(widened[None], compact[:, None], filler)]
    pallas_call x0 -> x5, Pallas kernels: none -> 18 us  [the longest x2 12.6 us: local(): pl.pallas_call(functools.partial(local_kernel, first), out_shape=jax.Shap...]
    reduce_sum x16 -> x0, other arithmetic: 17.4 us -> none  [the longest x6 7.81 us: pick_rows(): jnp.sum(jnp.where(chosen[:, :, None], split, jnp.zeros((), shaped.dtype))...]
    another operation x11 -> x0, local copies, waits for them, and re-layouts: 9.64 us -> none  [the longest x8 6.97 us: per_device(): jnp.stack([keys.reshape(row_count, head_count, HD), values.reshape(row_co...]
    add x14 -> x0, other arithmetic: 6.61 us -> none  [the longest x7 3.68 us: per_device(): row_start + dilation * jnp.arange(local_rows, dtype=jnp.int32)[:, None]]
    psum x1 -> x0, blocking collectives: 5.9 us -> none  [per_device(): lax.psum((jnp.sum(attended, axis=1), jnp.sum(attended * attended, axis=1)...]
    select_n x10 -> x0, other arithmetic: 5.39 us -> none  [the longest x8 4.82 us: collect(): jnp.where(is_upper, jnp.concatenate([partner, flat_pairs], axis=1), jnp.c...]
  transfers between devices with their start and end apart: 8 -> 10, of which waited for: 2 -> 2; matrix products, arithmetic and copies ran while one was open for 50% -> 0% of each run, Pallas kernels for 0% -> 34%
where the time goes in v1:
time: 37 us; the launch traced here: 36.7 us
  Pallas kernels  18 us (49%)
  starting transfers between devices  13.1 us (35%)
  local copies, waits for them, and re-layouts  3.68 us (10%)
  waiting for transfers between devices  1.89 us (5%)
    ppermute x10, starting transfers between devices, partner(): return lax.ppermute(value, axis, pairs)  13.1 us
    pallas_call x2, Pallas kernels, local(): pl.pallas_call(functools.partial(local_kernel, first), out_shape=jax.Shap...  12.6 us
    pallas_call x1, Pallas kernels, per_device(): pl.pallas_call(functools.partial(distant_kernel, kinds, distances), out_s...  3.9 us
    unnamed x16, local copies, waits for them, and re-layouts  3.68 us
    ppermute x10, waiting for transfers between devices, partner(): return lax.ppermute(value, axis, pairs)  1.89 us
    pallas_call x1, Pallas kernels, per_device(): pl.pallas_call(norm_kernel, out_shape=jax.ShapeDtypeStruct((features, row...  0.93 us
  transfers between devices with their start and end apart: 10, of which 2 were waited for; matrix products, arithmetic and copies ran while one was open for 0% of the time, Pallas kernels for 34%

profile of v1, /device:TPU:0, one launch (start us, length us, event | category | flops | bytes accessed | tf_op | source)
XLA Modules:
  0.0 36.7 jit_solution(14401897845213068778)
XLA Ops:
  0.0 1.0 %copy-done = bf16[192,1024]{1,0:T(8,128)(2,1)S(1)} copy-done((bf16[192,1024]{1,0:T(8,128)(2,1)S(1)}, bf16[192,1024]{1,0:T(8,128)(2,1)}, u32[]{:S(2)}) %copy-start) | copy-done | bytes 393240
  1.0 1.0 %copy-done.2 = bf16[192,1024]{1,0:T(8,128)(2,1)S(1)} copy-done((bf16[192,1024]{1,0:T(8,128)(2,1)S(1)}, bf16[192,1024]{1,0:T(8,128)(2,1)}, u32[]{:S(2)}) %copy-start.2) | copy-done | bytes 393240
  2.0 0.6 %pack.1 = (bf16[384,256]{1,0:T(8,128)(2,1)S(1)}, bf16[192,128]{1,0:T(8,128)(2,1)S(1)}) custom-call(bf16[192,1024]{1,0:T(8,128)(2,1)S(1)} %copy-done, bf16[192,1024]{1,0:T(8,128)(2,1)S(1)} %copy-done.2), custom_call_target="tpu_custom_call" | custom-call | flops 201326592 | bytes 1000000 | tf_op jit(solution)/shard_map/pack/pallas_call | solution.py:293
  2.6 0.0 copy-start.7
  2.6 4.1 %collective-permute-start = (bf16[192,128]{1,0:T(8,128)(2,1)S(1)}, bf16[192,128]{1,0:T(8,128)(2,1)S(1)}, u32[]{:S(2)}, u32[]{:S(2)}) collective-permute-start(bf16[192,128]{1,0:T(8,128)(2,1)S(1)} %get-tuple-element.11), channel_id=1, source_target_pairs={{0,16},{4,20},{8,24},{12,28},{16,0},{20,4},{24,8},{28,12},{1,17},{... | collective-permute-start | bytes 147464 | tf_op jit(solution)/shard_map/ppermute | solution.py:29
  6.7 2.5 %collective-permute-start.3 = (bf16[384,256]{1,0:T(8,128)(2,1)S(1)}, bf16[384,256]{1,0:T(8,128)(2,1)S(1)}, u32[]{:S(2)}, u32[]{:S(2)}) collective-permute-start(bf16[384,256]{1,0:T(8,128)(2,1)S(1)} %get-tuple-element.13), channel_id=1, source_target_pairs={{0,12},{4,8},{8,4},{12,0},{16,28},{20,24},{24,20},{28,16},{1,13},{... | collective-permute-start | bytes 589832 | tf_op jit(solution)/shard_map/ppermute | solution.py:29
  9.2 0.4 %collective-permute-start.2 = (bf16[384,256]{1,0:T(8,128)(2,1)S(1)}, bf16[384,256]{1,0:T(8,128)(2,1)S(1)}, u32[]{:S(2)}, u32[]{:S(2)}) collective-permute-start(bf16[384,256]{1,0:T(8,128)(2,1)S(1)} %get-tuple-element.13), channel_id=1, source_target_pairs={{0,8},{4,12},{8,0},{12,4},{16,24},{20,28},{24,16},{28,20},{1,9},{5... | collective-permute-start | bytes 589832 | tf_op jit(solution)/shard_map/ppermute | solution.py:29
  9.6 0.5 %collective-permute-start.1 = (bf16[384,256]{1,0:T(8,128)(2,1)S(1)}, bf16[384,256]{1,0:T(8,128)(2,1)S(1)}, u32[]{:S(2)}, u32[]{:S(2)}) collective-permute-start(bf16[384,256]{1,0:T(8,128)(2,1)S(1)} %get-tuple-element.13), channel_id=1, source_target_pairs={{0,4},{4,0},{8,12},{12,8},{16,20},{20,16},{24,28},{28,24},{1,5},{5... | collective-permute-start | bytes 589832 | tf_op jit(solution)/shard_map/ppermute | solution.py:29
  10.2 0.0 collective-permute-done.refs_3_
  10.2 2.5 %collective-permute-start.6 = (bf16[192,128]{1,0:T(8,128)(2,1)S(1)}, bf16[192,128]{1,0:T(8,128)(2,1)S(1)}, u32[]{:S(2)}, u32[]{:S(2)}) collective-permute-start(bf16[192,128]{1,0:T(8,128)(2,1)S(1)} %collective-permute-done.refs_3_), channel_id=1, source_target_pairs={{0,12},{4,8},{8,4},{12,0},{16,28},{20,24},{24,20},{28,16},{1,13},{... | collective-permute-start | bytes 147464 | tf_op jit(solution)/shard_map/ppermute | solution.py:29
  12.7 0.0 copy-done.1
  12.7 1.0 %copy-done.6 = bf16[192,1024]{1,0:T(8,128)(2,1)S(1)} copy-done((bf16[192,1024]{1,0:T(8,128)(2,1)S(1)}, bf16[192,1024]{1,0:T(8,128)(2,1)}, u32[]{:S(2)}) %copy-start.6) | copy-done | bytes 393240
  13.7 6.3 %local.2.local_a_ref = f32[2,64,1024]{2,1,0:T(8,128)S(1)} custom-call(s32[8]{0:T(128)S(1)} %copy-done.7, bf16[192,1024]{1,0:T(8,128)(2,1)S(1)} %copy-done.6, bf16[192,1024]{1,0:T(8,128)(2,1)S(1)} %copy-done.1, bf16[192,1024]{1,0:T(8,128)(2,1)S(1)} %copy-done.3), custom_call_target="tpu_custom_call" | custom-call | flops 2147483648 | bytes 1000000 | tf_op jit(solution)/shard_map/local/pallas_call | solution.py:307
  20.0 0.5 %collective-permute-start.5 = (bf16[192,128]{1,0:T(8,128)(2,1)S(1)}, bf16[192,128]{1,0:T(8,128)(2,1)S(1)}, u32[]{:S(2)}, u32[]{:S(2)}) collective-permute-start(bf16[192,128]{1,0:T(8,128)(2,1)S(1)} %collective-permute-done.refs_3_), channel_id=1, source_target_pairs={{0,8},{4,12},{8,0},{12,4},{16,24},{20,28},{24,16},{28,20},{1,9},{5... | collective-permute-start | bytes 147464 | tf_op jit(solution)/shard_map/ppermute | solution.py:29
  20.5 0.0 collective-permute-done.6.refs_6_
  20.5 0.5 %collective-permute-start.4 = (bf16[192,128]{1,0:T(8,128)(2,1)S(1)}, bf16[192,128]{1,0:T(8,128)(2,1)S(1)}, u32[]{:S(2)}, u32[]{:S(2)}) collective-permute-start(bf16[192,128]{1,0:T(8,128)(2,1)S(1)} %collective-permute-done.refs_3_), channel_id=1, source_target_pairs={{0,4},{4,0},{8,12},{12,8},{16,20},{20,16},{24,28},{28,24},{1,5},{5... | collective-permute-start | bytes 147464 | tf_op jit(solution)/shard_map/ppermute | solution.py:29
  21.0 6.3 %local.3.local_b_ref = f32[2,64,1024]{2,1,0:T(8,128)S(1)} custom-call(s32[8]{0:T(128)S(1)} %copy-done.7, bf16[192,1024]{1,0:T(8,128)(2,1)S(1)} %copy-done.6, bf16[192,1024]{1,0:T(8,128)(2,1)S(1)} %copy-done.1, bf16[192,1024]{1,0:T(8,128)(2,1)S(1)} %copy-done.3), custom_call_target="tpu_custom_call" | custom-call | flops 2147483648 | bytes 1000000 | tf_op jit(solution)/shard_map/local/pallas_call | solution.py:307
  27.3 0.0 collective-permute-done.5.refs_5_
  27.3 0.0 collective-permute-done.4.refs_4_
  27.4 0.0 collective-permute-done.3.refs_2_
  27.4 0.0 collective-permute-done.2.refs_1_
  27.4 0.0 collective-permute-done.1.refs_0_
  27.4 0.0 copy-start.5
  27.4 3.9 %distant.1 = (f32[192,1024]{1,0:T(8,128)S(1)}, f32[8,256]{1,0:T(8,128)S(1)}) custom-call(s32[8]{0:T(128)S(1)} %copy-done.7, bf16[192,1024]{1,0:T(8,128)(2,1)S(1)} %copy-done.6, f32[2,64,1024]{2,1,0:T(8,128)S(1)} %local.2.local_a_ref, f32[2,64,1024]{2,1,0:T(8,128)S(1)} %local.3.local_b_ref, bf16[384,256]{1,0:T(8,128)(2,1)S(1)} %collective-permute-done.1.refs_0_, ...), custom_call_target="tpu_custom_call" | custom-call | flops 1073741824 | bytes 1000000 | tf_op jit(solution)/shard_map/distant/pallas_call | solution.py:340
  31.3 0.1 collective-permute-start.9
  31.4 1.6 %collective-permute-start.8 = (f32[8,256]{1,0:T(8,128)S(1)}, f32[8,256]{1,0:T(8,128)S(1)}, u32[]{:S(2)}, u32[]{:S(2)}) collective-permute-start(f32[8,256]{1,0:T(8,128)S(1)} %get-tuple-element.16.refs_0_), channel_id=1, source_target_pairs={{0,2},{1,3},{2,0},{3,1},{4,6},{5,7},{6,4},{7,5},{8,10},{9,11},{10,... | collective-permute-start | bytes 24584 | tf_op jit(solution)/shard_map/ppermute | solution.py:29
  33.0 0.3 collective-permute-start.7
  33.2 1.2 %collective-permute-done.9.refs_3_ = f32[8,256]{1,0:T(8,128)S(1)} collective-permute-done((f32[8,256]{1,0:T(8,128)S(1)}, f32[8,256]{1,0:T(8,128)S(1)}, u32[]{:S(2)}, u32[]{:S(2)}) %collective-permute-start.9) | collective-permute-done | bytes 8224 | tf_op jit(solution)/shard_map/ppermute | solution.py:29
  34.5 0.6 %collective-permute-done.8.refs_2_ = f32[8,256]{1,0:T(8,128)S(1)} collective-permute-done((f32[8,256]{1,0:T(8,128)S(1)}, f32[8,256]{1,0:T(8,128)S(1)}, u32[]{:S(2)}, u32[]{:S(2)}) %collective-permute-start.8) | collective-permute-done | bytes 8224 | tf_op jit(solution)/shard_map/ppermute | solution.py:29
  35.1 0.0 collective-permute-done.7.refs_1_
  35.1 0.7 %copy-done.4 = f32[192]{0:T(256)S(1)} copy-done((f32[192]{0:T(256)S(1)}, f32[192]{0:T(256)}, u32[]{:S(2)}) %copy-start.4) | copy-done | bytes 792
  35.8 0.9 %norm.1 = bf16[192,1024]{1,0:T(8,128)(2,1)} custom-call(f32[192,1024]{1,0:T(8,128)S(1)} %get-tuple-element.15.att_ref, f32[1,192]{1,0:T(1,128)S(1)} %bitcast.2, f32[1,192]{1,0:T(1,128)S(1)} %bitcast.3, f32[8,256]{1,0:T(8,128)S(1)} %get-tuple-element.16.refs_0_, f32[8,256]{1,0:T(8,128)S(1)} %collective-permute-done.7.refs_1_, ...), custom_call_target="tpu_custom_call" | custom-call | tf_op jit(solution)/shard_map/norm/pallas_call | solution.py:358
  (9 shorter events, 0.0 us)
Async XLA Ops:
  0.0 1.0 %copy-start = (bf16[192,1024]{1,0:T(8,128)(2,1)S(1)}, bf16[192,1024]{1,0:T(8,128)(2,1)}, u32[]{:S(2)}) copy-start(bf16[192,1024]{1,0:T(8,128)(2,1)} %k_ref.5) | copy-start | bytes 1179652
  1.0 1.0 %copy-start.2 = (bf16[192,1024]{1,0:T(8,128)(2,1)S(1)}, bf16[192,1024]{1,0:T(8,128)(2,1)}, u32[]{:S(2)}) copy-start(bf16[192,1024]{1,0:T(8,128)(2,1)} %v_ref.5) | copy-start | bytes 1179652
  2.0 10.7 %copy-start.1 = (bf16[192,1024]{1,0:T(8,128)(2,1)S(1)}, bf16[192,1024]{1,0:T(8,128)(2,1)}, u32[]{:S(2)}) copy-start(bf16[192,1024]{1,0:T(8,128)(2,1)} %k_ref.5) | copy-start | bytes 1179652
  2.0 10.7 %copy-start.3 = (bf16[192,1024]{1,0:T(8,128)(2,1)S(1)}, bf16[192,1024]{1,0:T(8,128)(2,1)}, u32[]{:S(2)}) copy-start(bf16[192,1024]{1,0:T(8,128)(2,1)} %v_ref.5) | copy-start | bytes 1179652
  2.6 10.1 %copy-start.7 = (s32[8]{0:T(128)S(1)}, s32[8]{0:T(128)}, u32[]{:S(2)}) copy-start(s32[8]{0:T(128)} %lengths_ref.5) | copy-start | bytes 100
  2.6 7.6 %collective-permute-start = (bf16[192,128]{1,0:T(8,128)(2,1)S(1)}, bf16[192,128]{1,0:T(8,128)(2,1)S(1)}, u32[]{:S(2)}, u32[]{:S(2)}) collective-permute-start(bf16[192,128]{1,0:T(8,128)(2,1)S(1)} %get-tuple-element.11), channel_id=1, source_target_pairs={{0,16},{4,20},{8,24},{12,28},{16,0},{20,4},{24,8},{28,12},{1,17},{... | collective-permute-start | bytes 147464 | tf_op jit(solution)/shard_map/ppermute | solution.py:29
  6.7 20.7 %collective-permute-start.3 = (bf16[384,256]{1,0:T(8,128)(2,1)S(1)}, bf16[384,256]{1,0:T(8,128)(2,1)S(1)}, u32[]{:S(2)}, u32[]{:S(2)}) collective-permute-start(bf16[384,256]{1,0:T(8,128)(2,1)S(1)} %get-tuple-element.13), channel_id=1, source_target_pairs={{0,12},{4,8},{8,4},{12,0},{16,28},{20,24},{24,20},{28,16},{1,13},{... | collective-permute-start | bytes 589832 | tf_op jit(solution)/shard_map/ppermute | solution.py:29
  9.2 18.2 %collective-permute-start.2 = (bf16[384,256]{1,0:T(8,128)(2,1)S(1)}, bf16[384,256]{1,0:T(8,128)(2,1)S(1)}, u32[]{:S(2)}, u32[]{:S(2)}) collective-permute-start(bf16[384,256]{1,0:T(8,128)(2,1)S(1)} %get-tuple-element.13), channel_id=1, source_target_pairs={{0,8},{4,12},{8,0},{12,4},{16,24},{20,28},{24,16},{28,20},{1,9},{5... | collective-permute-start | bytes 589832 | tf_op jit(solution)/shard_map/ppermute | solution.py:29
  9.6 17.7 %collective-permute-start.1 = (bf16[384,256]{1,0:T(8,128)(2,1)S(1)}, bf16[384,256]{1,0:T(8,128)(2,1)S(1)}, u32[]{:S(2)}, u32[]{:S(2)}) collective-permute-start(bf16[384,256]{1,0:T(8,128)(2,1)S(1)} %get-tuple-element.13), channel_id=1, source_target_pairs={{0,4},{4,0},{8,12},{12,8},{16,20},{20,16},{24,28},{28,24},{1,5},{5... | collective-permute-start | bytes 589832 | tf_op jit(solution)/shard_map/ppermute | solution.py:29
  10.2 10.3 %collective-permute-start.6 = (bf16[192,128]{1,0:T(8,128)(2,1)S(1)}, bf16[192,128]{1,0:T(8,128)(2,1)S(1)}, u32[]{:S(2)}, u32[]{:S(2)}) collective-permute-start(bf16[192,128]{1,0:T(8,128)(2,1)S(1)} %collective-permute-done.refs_3_), channel_id=1, source_target_pairs={{0,12},{4,8},{8,4},{12,0},{16,28},{20,24},{24,20},{28,16},{1,13},{... | collective-permute-start | bytes 147464 | tf_op jit(solution)/shard_map/ppermute | solution.py:29
  12.7 1.0 %copy-start.6 = (bf16[192,1024]{1,0:T(8,128)(2,1)S(1)}, bf16[192,1024]{1,0:T(8,128)(2,1)}, u32[]{:S(2)}) copy-start(bf16[192,1024]{1,0:T(8,128)(2,1)} %q_ref.4) | copy-start | bytes 1179652
  20.0 7.4 %collective-permute-start.5 = (bf16[192,128]{1,0:T(8,128)(2,1)S(1)}, bf16[192,128]{1,0:T(8,128)(2,1)S(1)}, u32[]{:S(2)}, u32[]{:S(2)}) collective-permute-start(bf16[192,128]{1,0:T(8,128)(2,1)S(1)} %collective-permute-done.refs_3_), channel_id=1, source_target_pairs={{0,8},{4,12},{8,0},{12,4},{16,24},{20,28},{24,16},{28,20},{1,9},{5... | collective-permute-start | bytes 147464 | tf_op jit(solution)/shard_map/ppermute | solution.py:29
  20.5 6.8 %collective-permute-start.4 = (bf16[192,128]{1,0:T(8,128)(2,1)S(1)}, bf16[192,128]{1,0:T(8,128)(2,1)S(1)}, u32[]{:S(2)}, u32[]{:S(2)}) collective-permute-start(bf16[192,128]{1,0:T(8,128)(2,1)S(1)} %collective-permute-done.refs_3_), channel_id=1, source_target_pairs={{0,4},{4,0},{8,12},{12,8},{16,20},{20,16},{24,28},{28,24},{1,5},{5... | collective-permute-start | bytes 147464 | tf_op jit(solution)/shard_map/ppermute | solution.py:29
  27.4 7.7 %copy-start.5 = (f32[192]{0:T(256)S(1)}, f32[192]{0:T(256)}, u32[]{:S(2)}) copy-start(f32[192]{0:T(256)} %param.11) | copy-start | bytes 2308
  31.3 3.2 %collective-permute-start.9 = (f32[8,256]{1,0:T(8,128)S(1)}, f32[8,256]{1,0:T(8,128)S(1)}, u32[]{:S(2)}, u32[]{:S(2)}) collective-permute-start(f32[8,256]{1,0:T(8,128)S(1)} %get-tuple-element.16.refs_0_), channel_id=1, source_target_pairs={{0,3},{1,2},{2,1},{3,0},{4,7},{5,6},{6,5},{7,4},{8,11},{9,10},{10,... | collective-permute-start | bytes 24584 | tf_op jit(solution)/shard_map/ppermute | solution.py:29
  31.4 3.7 %collective-permute-start.8 = (f32[8,256]{1,0:T(8,128)S(1)}, f32[8,256]{1,0:T(8,128)S(1)}, u32[]{:S(2)}, u32[]{:S(2)}) collective-permute-start(f32[8,256]{1,0:T(8,128)S(1)} %get-tuple-element.16.refs_0_), channel_id=1, source_target_pairs={{0,2},{1,3},{2,0},{3,1},{4,6},{5,7},{6,4},{7,5},{8,10},{9,11},{10,... | collective-permute-start | bytes 24584 | tf_op jit(solution)/shard_map/ppermute | solution.py:29
  33.0 2.1 %collective-permute-start.7 = (f32[8,256]{1,0:T(8,128)S(1)}, f32[8,256]{1,0:T(8,128)S(1)}, u32[]{:S(2)}, u32[]{:S(2)}) collective-permute-start(f32[8,256]{1,0:T(8,128)S(1)} %get-tuple-element.16.refs_0_), channel_id=1, source_target_pairs={{0,1},{1,0},{2,3},{3,2},{4,5},{5,4},{6,7},{7,6},{8,9},{9,8},{10,11... | collective-permute-start | bytes 24584 | tf_op jit(solution)/shard_map/ppermute | solution.py:29
  35.1 0.7 %copy-start.4 = (f32[192]{0:T(256)S(1)}, f32[192]{0:T(256)}, u32[]{:S(2)}) copy-start(f32[192]{0:T(256)} %param.10) | copy-start | bytes 2308

commit v2 on v1

v2 whole, which is shorter than its diff:
```python
import functools
import math

import jax
import jax.numpy as jnp
import numpy as np
from jax import lax
from jax.experimental import pallas as pl
from jax.experimental.pallas import tpu as pltpu
from jax.sharding import PartitionSpec as P

D = 768
HD = 48
SEG = 1024
HEADS = 4
BLOCKED = -1e30
SCALE = 1.0 / math.sqrt(HD)
LOG2_SCALE = math.log2(math.e) * SCALE
QUERY_CHUNK = 1024
SAFE = 60.0
F32 = jnp.float32
BF16 = jnp.bfloat16
HBM = pl.BlockSpec(memory_space=pltpu.HBM)
VMEM = pl.BlockSpec(memory_space=pltpu.VMEM)
SMEM = pl.BlockSpec(memory_space=pltpu.SMEM)
PACK_LIMIT = 60 * 2**20
PARAMS = pltpu.CompilerParams(vmem_limit_bytes=40 * 2**20)


def partner(value, axis, mask):
    pairs = [(source, source ^ mask) for source in range(lax.axis_size(axis))]
    return lax.ppermute(value, axis, pairs)


def thirds(value):
    parts = []
    for _ in range(3):
        part = float(np.asarray(value, jnp.bfloat16))
        parts.append(part)
        value -= part
    return parts


def bias_rows(flags, factor):
    return [jnp.where(flags, F32(part), F32(0.0)) for part in thirds(math.log(factor) / SCALE)]


def flag_rows(flags):
    return [jnp.where(flags, F32(1.0), F32(0.0))] * 3


def slide_of(positions, lengths_ref):
    slide = jnp.zeros(positions.shape, jnp.int32)
    end = jnp.int32(0)
    for k in range(lengths_ref.shape[0]):
        end = end + lengths_ref[k]
        slide = slide + jnp.where(positions >= end, 1, 0)
    return slide


def stack_rows(rows, count):
    width = rows[0].shape[1]
    index = lax.broadcasted_iota(jnp.int32, (count, width), 0)
    block = jnp.zeros((count, width), F32)
    for k, row in enumerate(rows):
        block = jnp.where(index == k, row, block)
    return block


def lanes(width):
    return lax.broadcasted_iota(jnp.int32, (1, width), 1)


def compact_index(place, head_place):
    quarter = place >> 6
    return 16 * (place & 15) + 4 * ((place >> 4) & 3) + ((quarter + head_place) & 3)


def only_head(ref, own):
    width = ref.shape[1]
    return [
        ref[i * HD : (i + 1) * HD, :]
        * jnp.broadcast_to(jnp.where(own == i, F32(1.0), F32(0.0)), (HD, width)).astype(BF16)
        for i in range(HEADS)
    ]


def pack_kernel(k_hbm, v_hbm, pair_ref, sixteenth_ref, *scratch):
    targets, arrived = scratch[:2], scratch[2]
    copies = []
    for at, (source, target) in enumerate(zip((k_hbm, v_hbm), targets)):
        for i in range(HEADS):
            part = pl.ds(i * HD, HD)
            copies.append(
                pltpu.make_async_copy(source.at[part, :], target.at[part, :], arrived.at[at, i])
            )
    for copy in copies:
        copy.start()
    features, rows = targets[0].shape
    packed = rows // 4
    head_place = lax.axis_index("head")
    place = lax.broadcasted_iota(jnp.int32, (packed, rows), 0)
    group = lax.broadcasted_iota(jnp.int32, (packed, rows), 1) >> 2
    pick = jnp.where(compact_index(place, head_place) == group, F32(1.0), F32(0.0)).astype(BF16)
    own = lanes(rows) & 3
    results = []
    for at, ref in enumerate(targets):
        for copy in copies[at * HEADS : (at + 1) * HEADS]:
            copy.wait()
        masked = jnp.concatenate(only_head(ref, own), axis=0)
        compact = lax.dot_general(masked, pick, (((1,), (1,)), ((), ())), preferred_element_type=F32)
        pair_ref[at * features : (at + 1) * features, :] = compact.astype(BF16)
        results.append(compact[:, : packed // 4])
    sixteenth_ref[...] = jnp.concatenate(results, axis=1).astype(BF16)


def relay_kernel(one_ref, two_ref, *refs):
    beyond, (to_one, to_two) = refs[:-2], refs[-2:]
    features, width = to_one.shape[0], one_ref.shape[1]
    to_one[:, :width] = two_ref[features:, :]
    to_two[:, :width] = one_ref[:features, :]
    for piece in beyond:
        for out in (to_one, to_two):
            out[:, width : width + piece.shape[1]] = piece[...]
        width += piece.shape[1]


def mask_kernel(kinds, distances, lengths_ref, gain_ref, bias_ref, q_ref, q_out, k_mask_out, affine_out, q_norm_out, slide_out):
    rows = q_ref.shape[1]
    features = HEADS * HD
    slides = lengths_ref.shape[0]
    tile = lanes(rows)
    seq_place = lax.axis_index("seq")
    head_place = lax.axis_index("head")
    extra = k_mask_out.shape[0] - HEADS * slides

    at = 0
    for kind, distance in zip(kinds, distances):
        count = rows // 4**kind
        place = lanes(count)
        base = (seq_place ^ distance) * rows + 4 * compact_index(place, head_place)
        row = lax.broadcasted_iota(jnp.int32, (slides, count), 0)
        masks = [
            jnp.where(slide_of(base + i, lengths_ref) == row, F32(0.0), F32(BLOCKED))
            for i in range(HEADS)
        ]
        none = jnp.zeros((1, count), F32)
        in_third = place < rows // 16
        in_fourth = place < rows // 64
        if kind == 1:
            added = bias_rows(in_third, 2.0) + bias_rows(in_fourth, 1.5) + [none, none]
        elif kind == 2:
            added = [none] * 3 + bias_rows(in_fourth, 2.0) + [none + BLOCKED, none]
        else:
            added = [none] * 6 + [none, none + BLOCKED]
        masks.append(stack_rows(added, extra))
        k_mask_out[:, at : at + count] = jnp.concatenate(masks, axis=0).astype(BF16)
        at += count

    slide = slide_of(seq_place * rows + tile, lengths_ref)
    same = slide == lax.broadcasted_iota(jnp.int32, (slides, rows), 0)
    slide_out[...] = jnp.where(same, F32(1.0), F32(0.0))
    masks = [jnp.where(same & ((tile & 3) == i), F32(1.0), F32(0.0)) for i in range(HEADS)]
    third = ((tile >> 2) & 3) == head_place
    fourth = ((tile >> 2) & 15) == head_place
    masks.append(
        stack_rows(
            flag_rows(third) + flag_rows(fourth) + flag_rows(~third)[:1] + flag_rows(~fourth)[:1],
            extra,
        )
    )
    q_out[:features, :] = jnp.concatenate(only_head(q_ref, tile & 3), axis=0)
    q_out[features:, :] = jnp.concatenate(masks, axis=0).astype(BF16)

    q_norm_out[...] = jnp.full(q_norm_out.shape, largest_norm(q_ref[...]))

    r = lax.broadcasted_iota(jnp.int32, (features, features), 0)
    c = lax.broadcasted_iota(jnp.int32, (features, features), 1)
    for at, ref in enumerate((gain_ref, bias_ref)):
        column = jnp.sum(jnp.where(r == c, ref[...], 0.0), axis=1, keepdims=True)
        affine_out[at] = jnp.broadcast_to(column, (features, 128))


def largest_norm(rows):
    rows = rows.astype(F32)
    squares = rows * rows
    return functools.reduce(
        jnp.maximum,
        [jnp.max(jnp.sum(squares[i : i + HD], axis=0)) for i in range(0, rows.shape[0], HD)],
    )


def small(query_norm, key_norm):
    return query_norm * key_norm <= (SAFE / SCALE) ** 2


def weigh(keys_t, queries, values, find_peak):
    scores = jnp.dot(keys_t, queries, preferred_element_type=F32)
    if find_peak:
        peak = jnp.max(scores, axis=0, keepdims=True)
        scores = scores - peak
    else:
        peak = jnp.zeros((1, scores.shape[1]), F32)
    probs = jnp.exp2(scores * LOG2_SCALE).astype(BF16)
    return peak, jnp.dot(values, probs, preferred_element_type=F32)


def both_ways(safe, branch):
    pl.when(safe)(functools.partial(branch, False))
    pl.when(jnp.logical_not(safe))(functools.partial(branch, True))


def local_kernel(first, slide_ref, q_ref, k_ref, v_ref, out_ref):
    rows = q_ref.shape[1]
    slides = slide_ref.shape[0]
    heads = out_ref.shape[0]
    tile = lanes(rows)
    head_place = lax.axis_index("head")
    query_slides = slide_ref[...]
    key_slides = (1.0 - query_slides) * F32(BLOCKED)
    extra = -(-(slides + 9) // 16) * 16 - slides
    ones = jnp.ones((16, rows), BF16)
    all_mine = slice(first * HD, (first + heads) * HD)

    def branch(find_peak):
        for head in range(heads):
            i = first + head
            mine = slice(i * HD, (i + 1) * HD)
            second = (tile & 3) == i
            third = (tile & 15) == 4 * head_place + i
            fourth = (tile & 63) == 4 * head_place + i
            query_extra = stack_rows(flag_rows(second) + flag_rows(third) + flag_rows(fourth), extra)
            key_extra = stack_rows(
                bias_rows(second, 2.0) + bias_rows(third, 1.5) + bias_rows(fourth, 4.0 / 3.0), extra
            )
            queries = jnp.concatenate(
                [q_ref[mine, :], jnp.concatenate([query_slides, query_extra], axis=0).astype(BF16)],
                axis=0,
            )
            keys = jnp.concatenate(
                [k_ref[mine, :], jnp.concatenate([key_slides, key_extra], axis=0).astype(BF16)],
                axis=0,
            )
            keys_t = keys.T
            values = jnp.concatenate([v_ref[mine, :], ones], axis=0)
            for start in range(0, rows, QUERY_CHUNK):
                chunk = slice(start, start + QUERY_CHUNK)
                peak, mixed = weigh(keys_t, queries[:, chunk], values, find_peak)
                out_ref[head, : HD + 8, chunk] = mixed[: HD + 8]
                out_ref[head, HD + 8 :, chunk] = jnp.broadcast_to(peak, (8, peak.shape[1]))

    both_ways(small(largest_norm(q_ref[all_mine, :]), largest_norm(k_ref[all_mine, :])), branch)


def distant_parts(pieces, mask_at, q_norm_ref, q_ref, k_mask_ref, k_ref, v_ref, use):
    features = HEADS * HD
    rows = q_ref.shape[1]
    at = 0
    norms = []
    beside = []
    for kind, keys, values in pieces:
        count = rows // 4**kind
        key_rows = keys[:, :count]
        if kind == 1:
            v_ref[:features, at : at + count] = values[...]
        else:
            beside.append(values[:, rows // 16 : rows // 16 + count])
        norms.append(largest_norm(key_rows))
        masks = k_mask_ref[:, mask_at + at : mask_at + at + count]
        k_ref[at : at + count, :] = jnp.concatenate([key_rows, masks], axis=0).T
        at += count
    if beside:
        width = sum(part.shape[1] for part in beside)
        v_ref[:features, at - width : at] = jnp.concatenate(beside, axis=1)
    v_ref[features:, :] = jnp.ones((16, at), BF16)

    def branch(find_peak):
        use(*weigh(k_ref[...], q_ref[...], v_ref[...], find_peak))

    key_norm = functools.reduce(jnp.maximum, norms)
    both_ways(small(jnp.max(q_norm_ref[...]), key_norm), branch)


def halves(ref):
    features = HEADS * HD
    return ref.at[:features, :], ref.at[features:, :]


def near_kernel(q_norm_ref, q_ref, k_mask_ref, one_ref, two_ref, out_ref, k_ref, v_ref):
    features = HEADS * HD

    def use(peak, mixed):
        out_ref[: features + 8, :] = mixed[: features + 8]
        out_ref[features + 8 :, :] = jnp.broadcast_to(peak, (8, peak.shape[1]))

    pieces = [(1, *halves(one_ref)), (1, *halves(two_ref))]
    distant_parts(pieces, 0, q_norm_ref, q_ref, k_mask_ref, k_ref, v_ref, use)


def last_kernel(kinds, mask_at, q_norm_ref, q_ref, k_mask_ref, local_a, local_b, near_ref, *refs):
    att_ref, sums_ref, k_ref, v_ref = refs[-4:]
    features = HEADS * HD
    rows = q_ref.shape[1]
    (from_one, from_two), rest = refs[:2], refs[2:-4]
    width = rows // 4
    pieces = [(1, from_two.at[:, :width], from_one.at[:, :width])]
    beyond = [ref.at[:, at : at + rows // 8] for ref in (from_one, from_two)
              for at in range(width, ref.shape[1], rows // 8)] + list(rest)
    pieces += [(kind, ref, ref) for kind, ref in zip(kinds[1:], beyond)]

    def use(far_peak, far):
        own = lanes(rows) & 3
        near_peak = near_ref[features + 8 : features + 9, :]
        near_total = near_ref[features : features + 1, :]
        far_total = far[features : features + 1]
        sums = squares = None
        for i in range(HEADS):
            ref = (local_a, local_b)[i // 2].at[i % 2]
            mine = slice(i * HD, (i + 1) * HD)
            selected = own == i
            here = ref[HD + 8 : HD + 9, :]
            top = jnp.maximum(
                here, jnp.where(selected, jnp.maximum(near_peak, far_peak), F32(BLOCKED))
            )
            keep = jnp.exp2((here - top) * LOG2_SCALE)
            near_keep = jnp.where(selected, jnp.exp2((near_peak - top) * LOG2_SCALE), F32(0.0))
            far_keep = jnp.where(selected, jnp.exp2((far_peak - top) * LOG2_SCALE), F32(0.0))
            inverse = 1.0 / (
                keep * ref[HD : HD + 1, :] + near_keep * near_total + far_keep * far_total
            )
            attended = (
                ref[:HD, :] * (keep * inverse)
                + near_ref[mine, :] * (near_keep * inverse)
                + far[mine] * (far_keep * inverse)
            )
            att_ref[mine, :] = attended
            head_sum = jnp.sum(attended, axis=0, keepdims=True)
            head_squares = jnp.sum(attended * attended, axis=0, keepdims=True)
            sums = head_sum if sums is None else sums + head_sum
            squares = head_squares if squares is None else squares + head_squares
        quarter = rows // 4
        for at in range(4):
            sums_ref[at : at + 1, :] = sums[:, at * quarter : (at + 1) * quarter]
            sums_ref[4 + at : 5 + at, :] = squares[:, at * quarter : (at + 1) * quarter]

    distant_parts(pieces, mask_at, q_norm_ref, q_ref, k_mask_ref, k_ref, v_ref, use)


def norm_kernel(att_ref, affine_ref, *refs):
    sum_refs, out_ref = refs[:-1], refs[-1]
    sums = sum_refs[0][...]
    for ref in sum_refs[1:]:
        sums = sums + ref[...]
    mean = sums[:4] / D
    variance = sums[4:] / D - mean * mean
    inverse = lax.rsqrt(variance + 1e-05)
    width = affine_ref.shape[2]
    quarter = mean.shape[1]
    for start in range(0, att_ref.shape[1], width):
        at, first = start // quarter, start % quarter
        part = slice(first, first + width)
        normed = (att_ref[:, start : start + width] - mean[at : at + 1, part]) * inverse[at : at + 1, part]
        out_ref[:, start : start + width] = (normed * affine_ref[0] + affine_ref[1]).astype(BF16)


def cost(flops, moved, exps=0):
    return pl.CostEstimate(flops=int(flops), bytes_accessed=int(moved), transcendentals=int(exps))


def per_device(queries, keys, values, slide_lengths, norm_gain, norm_bias):
    features, rows = queries.shape
    total_rows = rows * lax.axis_size("seq")
    spans = [min(SEG * 4**b, total_rows) // rows for b in range(4)]
    assert spans[1] == 4 and features == HEADS * HD
    pair, own = pl.pallas_call(
        pack_kernel,
        out_shape=(
            jax.ShapeDtypeStruct((2 * features, rows // 4), BF16),
            jax.ShapeDtypeStruct((features, rows // 8), BF16),
        ),
        in_specs=[HBM] * 2,
        out_specs=(VMEM,) * 2,
        scratch_shapes=[
            pltpu.VMEM((features, rows), BF16),
            pltpu.VMEM((features, rows), BF16),
            pltpu.SemaphoreType.DMA((2, HEADS)),
        ],
        compiler_params=pltpu.CompilerParams(vmem_limit_bytes=PACK_LIMIT),
        cost_estimate=cost(2 * 384 * 256 * 1024, 10**6),
        name="pack",
    )(keys, values)

    beyond = [(partner(own, "seq", m), m) for m in range(spans[2], spans[3], spans[2])]
    beyond = beyond + [
        (partner(piece, "seq", m), m ^ d)
        for m in range(spans[1], spans[2], spans[1])
        for piece, d in [(own, 0)] + beyond
    ]
    one, two = partner(pair, "seq", 1), partner(pair, "seq", 2)
    beyond_pieces = [piece for piece, _ in beyond]
    relayed = jax.ShapeDtypeStruct((features, rows // 4 + rows // 8 * len(beyond)), BF16)
    to_one, to_two = pl.pallas_call(
        relay_kernel,
        out_shape=(relayed, relayed),
        in_specs=[VMEM] * (2 + len(beyond)),
        out_specs=(VMEM, VMEM),
        compiler_params=PARAMS,
        cost_estimate=cost(0, 10**6),
        name="relay",
    )(one, two, *beyond_pieces)
    from_one, from_two = partner(to_one, "seq", 1), partner(to_two, "seq", 2)
    from_three = [partner(piece, "seq", 3) for piece in beyond_pieces]
    beyond_distances = [d ^ m for m in (1, 2, 0, 3) for _, d in beyond]
    distances = [1, 2, 3] + beyond_distances
    kinds = [1, 1, 1] + [2 if d < spans[2] else 3 for d in beyond_distances]
    counts = [rows // 4**kind for kind in kinds]
    near_count, far_count = sum(counts[:2]), sum(counts[2:])

    mask_rows = -(-(HEADS * slide_lengths.shape[0] + 8) // 16) * 16
    depth = features + mask_rows
    own_queries, key_masks, affine, query_norm, slides = pl.pallas_call(
        functools.partial(mask_kernel, kinds, distances),
        out_shape=(
            jax.ShapeDtypeStruct((depth, rows), BF16),
            jax.ShapeDtypeStruct((mask_rows, near_count + far_count), BF16),
            jax.ShapeDtypeStruct((2, features, 128), F32),
            jax.ShapeDtypeStruct((8, 128), F32),
            jax.ShapeDtypeStruct((slide_lengths.shape[0], rows), F32),
        ),
        in_specs=[SMEM, VMEM, VMEM, VMEM],
        out_specs=(VMEM,) * 5,
        compiler_params=PARAMS,
        cost_estimate=cost(10**8, 10**6),
        name="masks",
    )(slide_lengths, norm_gain[None, :], norm_bias[None, :], queries)

    def local(first, *operands):
        return pl.pallas_call(
            functools.partial(local_kernel, first),
            out_shape=jax.ShapeDtypeStruct((2, HD + 16, rows), F32),
            in_specs=[VMEM] * 4,
            out_specs=VMEM,
            compiler_params=PARAMS,
            cost_estimate=cost(2 * 2 * rows * rows * 512, 10**6, 2 * rows * rows),
            name="local",
        )(*operands)

    local_a = local(0, slides, queries, keys, values)
    held, _ = lax.optimization_barrier((queries, (to_one, to_two)))
    local_b = local(2, slides, held, keys, values)

    def scratch(count):
        return [pltpu.VMEM((count, depth), BF16), pltpu.VMEM((features + 16, count), BF16)]

    near_part = pl.pallas_call(
        near_kernel,
        out_shape=jax.ShapeDtypeStruct((features + 16, rows), F32),
        in_specs=[VMEM] * 5,
        out_specs=VMEM,
        scratch_shapes=scratch(near_count),
        compiler_params=PARAMS,
        cost_estimate=cost(2 * rows * near_count * 512, 10**6, rows * near_count),
        name="near",
    )(query_norm, own_queries, key_masks, one, two)

    attended, sums = pl.pallas_call(
        functools.partial(last_kernel, kinds[2:], near_count),
        out_shape=(
            jax.ShapeDtypeStruct((features, rows), F32),
            jax.ShapeDtypeStruct((8, rows // 4), F32),
        ),
        in_specs=[VMEM] * (8 + 2 * len(beyond)),
        out_specs=(VMEM, VMEM),
        scratch_shapes=scratch(far_count),
        compiler_params=PARAMS,
        cost_estimate=cost(2 * rows * far_count * 512, 10**6, rows * far_count),
        name="last",
    )(
        query_norm, own_queries, key_masks, local_a, local_b, near_part,
        from_one, from_two, *beyond_pieces, *from_three,
    )

    all_sums = [sums] + [partner(sums, "head", m) for m in range(1, lax.axis_size("head"))]
    return pl.pallas_call(
        norm_kernel,
        out_shape=jax.ShapeDtypeStruct((features, rows), BF16),
        in_specs=[VMEM] * (2 + len(all_sums)),
        out_specs=VMEM,
        compiler_params=PARAMS,
        name="norm",
    )(attended, affine, *all_sums)


def solution(mesh):
    placed = (P("head", "seq"), P("head", "seq"), P("head", "seq"), P(), P("head"), P("head"))
    return jax.shard_map(
        per_device, mesh=mesh, in_specs=placed, out_specs=P("head", "seq"), check_vma=False
    )
```

time: 37 us -> 29.3 us (0.79)
  local copies, waits for them, and re-layouts: 3.68 us -> 0.02 us
  Pallas kernels: 18 us -> 14.5 us
  starting transfers between devices: 13.1 us -> 12.7 us
    pallas_call x2, Pallas kernels: 12.6 us -> 6.54 us  [local(): pl.pallas_call(functools.partial(local_kernel, first), out_shape=jax.Shap...]
    unnamed x16 -> x12, local copies, waits for them, and re-layouts: 3.68 us -> 0.02 us
    pallas_call x1, Pallas kernels: 0.57 us -> 2.75 us  [per_device(): pl.pallas_call(pack_kernel, out_shape=(jax.ShapeDtypeStruct((2 * features...]
    ppermute x10 -> x9, starting transfers between devices: 13.1 us -> 12.7 us  [partner(): return lax.ppermute(value, axis, pairs)]
    pallas_call x1 -> x4, Pallas kernels: 3.9 us -> 4.23 us  [the longest x1 1.82 us: per_device(): pl.pallas_call(functools.partial(last_kernel, kinds[2:], near_count), out...]
    ppermute x10 -> x9, waiting for transfers between devices: 1.89 us -> 1.89 us  [partner(): return lax.ppermute(value, axis, pairs)]
  transfers between devices with their start and end apart: 10 -> 9, of which waited for: 2 -> 2; matrix products, arithmetic and copies ran while one was open for 0% -> 0% of each run, Pallas kernels for 34% -> 31%
where the time goes in v2:
time: 29.3 us; the launch traced here: 29.2 us
  Pallas kernels  14.5 us (49%)
  starting transfers between devices  12.7 us (43%)
  waiting for transfers between devices  1.89 us (6%)
    ppermute x9, starting transfers between devices, partner(): return lax.ppermute(value, axis, pairs)  12.7 us
    pallas_call x2, Pallas kernels, local(): pl.pallas_call(functools.partial(local_kernel, first), out_shape=jax.Shap...  6.54 us
    pallas_call x1, Pallas kernels, per_device(): pl.pallas_call(pack_kernel, out_shape=(jax.ShapeDtypeStruct((2 * features...  2.75 us
    ppermute x9, waiting for transfers between devices, partner(): return lax.ppermute(value, axis, pairs)  1.89 us
    pallas_call x1, Pallas kernels, per_device(): pl.pallas_call(functools.partial(last_kernel, kinds[2:], near_count), out...  1.82 us
    pallas_call x1, Pallas kernels, per_device(): pl.pallas_call(near_kernel, out_shape=jax.ShapeDtypeStruct((features + 16...  1.39 us
    pallas_call x1, Pallas kernels, per_device(): pl.pallas_call(functools.partial(mask_kernel, kinds, distances), out_shap...  0.99 us
    pallas_call x1, Pallas kernels, per_device(): pl.pallas_call(norm_kernel, out_shape=jax.ShapeDtypeStruct((features, row...  0.94 us
  transfers between devices with their start and end apart: 9, of which 2 were waited for; matrix products, arithmetic and copies ran while one was open for 0% of the time, Pallas kernels for 31%

profile of v2, /device:TPU:0, one launch (start us, length us, event | category | flops | bytes accessed | tf_op | source)
XLA Modules:
  0.0 29.2 jit_solution(54811408432984561)
XLA Ops:
  0.0 2.8 %pack.1 = (bf16[384,256]{1,0:T(8,128)(2,1)}, bf16[192,128]{1,0:T(8,128)(2,1)}) custom-call(bf16[192,1024]{1,0:T(8,128)(2,1)} %k_ref.3, bf16[192,1024]{1,0:T(8,128)(2,1)} %v_ref.3), custom_call_target="tpu_custom_call" | custom-call | flops 201326592 | bytes 1000000 | tf_op jit(solution)/shard_map/pack/pallas_call | solution.py:375
  2.8 0.0 copy-start.1
  2.8 3.1 %collective-permute-start.1 = (bf16[384,256]{1,0:T(8,128)(2,1)}, bf16[384,256]{1,0:T(8,128)(2,1)S(1)}, u32[]{:S(2)}, u32[]{:S(2)}) collective-permute-start(bf16[384,256]{1,0:T(8,128)(2,1)} %get-tuple-element.21), channel_id=1, source_target_pairs={{0,8},{4,12},{8,0},{12,4},{16,24},{20,28},{24,16},{28,20},{1,9},{5... | collective-permute-start | bytes 589832 | tf_op jit(solution)/shard_map/ppermute | solution.py:32
  5.9 1.5 %collective-permute-start = (bf16[384,256]{1,0:T(8,128)(2,1)}, bf16[384,256]{1,0:T(8,128)(2,1)S(1)}, u32[]{:S(2)}, u32[]{:S(2)}) collective-permute-start(bf16[384,256]{1,0:T(8,128)(2,1)} %get-tuple-element.21), channel_id=1, source_target_pairs={{0,4},{4,0},{8,12},{12,8},{16,20},{20,16},{24,28},{28,24},{1,5},{5... | collective-permute-start | bytes 589832 | tf_op jit(solution)/shard_map/ppermute | solution.py:32
  7.4 2.6 %collective-permute-start.2 = (bf16[192,128]{1,0:T(8,128)(2,1)}, bf16[192,128]{1,0:T(8,128)(2,1)S(1)}, u32[]{:S(2)}, u32[]{:S(2)}) collective-permute-start(bf16[192,128]{1,0:T(8,128)(2,1)} %get-tuple-element.22), channel_id=1, source_target_pairs={{0,16},{4,20},{8,24},{12,28},{16,0},{20,4},{24,8},{28,12},{1,17},{... | collective-permute-start | bytes 147464 | tf_op jit(solution)/shard_map/ppermute | solution.py:32
  10.0 0.0 copy-done
  10.0 0.0 copy-done.3
  10.0 0.0 copy-done.4
  10.0 0.0 copy-done.5
  10.0 1.0 %masks.1 = (bf16[240,1024]{1,0:T(8,128)(2,1)S(1)}, bf16[48,1024]{1,0:T(8,128)(2,1)S(1)}, f32[2,192,128]{2,1,0:T(8,128)S(1)}, f32[8,128]{1,0:T(8,128)S(1)}, f32[8,1024]{1,0:T(8,128)S(1)}) custom-call(s32[8]{0:T(128)S(1)} %copy-done.5, f32[1,192]{1,0:T(1,128)S(1)} %bitcast.2, f32[1,192]{1,0:T(1,128)S(1)} %bitcast.3, bf16[192,1024]{1,0:T(8,128)(2,1)S(1)} %copy-done), custom_call_target="tpu_custom_call" | custom-call | flops 100000000 | bytes 1000000 | tf_op jit(solution)/shard_map/masks/pallas_call | solution.py:421
  11.0 0.0 copy-done.2
  11.0 0.0 copy-done.1
  11.0 3.3 %local.2.local_a = f32[2,64,1024]{2,1,0:T(8,128)S(1)} custom-call(f32[8,1024]{1,0:T(8,128)S(1)} %get-tuple-element.20.slide_ref, bf16[192,1024]{1,0:T(8,128)(2,1)S(1)} %copy-done, bf16[192,1024]{1,0:T(8,128)(2,1)S(1)} %copy-done.1, bf16[192,1024]{1,0:T(8,128)(2,1)S(1)} %copy-done.2), custom_call_target="tpu_custom_call" | custom-call | flops 2147483648 | bytes 1000000 | tf_op jit(solution)/shard_map/local/pallas_call | solution.py:438
  14.3 0.0 collective-permute-done.2.refs_0_.refs_2_
  14.3 1.5 %collective-permute-start.5 = (bf16[192,128]{1,0:T(8,128)(2,1)S(1)}, bf16[192,128]{1,0:T(8,128)(2,1)S(1)}, u32[]{:S(2)}, u32[]{:S(2)}) collective-permute-start(bf16[192,128]{1,0:T(8,128)(2,1)S(1)} %collective-permute-done.2.refs_0_.refs_2_), channel_id=1, source_target_pairs={{0,12},{4,8},{8,4},{12,0},{16,28},{20,24},{24,20},{28,16},{1,13},{... | collective-permute-start | bytes 147464 | tf_op jit(solution)/shard_map/ppermute | solution.py:32
  15.7 0.0 collective-permute-done.1.two_ref
  15.7 0.0 collective-permute-done.one_ref
  15.8 0.6 %collective-permute-start.3 = (bf16[192,384]{1,0:T(8,128)(2,1)S(1)}, bf16[192,384]{1,0:T(8,128)(2,1)S(1)}, u32[]{:S(2)}, u32[]{:S(2)}) collective-permute-start(bf16[192,384]{1,0:T(8,128)(2,1)S(1)} %get-tuple-element.23), channel_id=1, source_target_pairs={{0,4},{4,0},{8,12},{12,8},{16,20},{20,16},{24,28},{28,24},{1,5},{5... | collective-permute-start | bytes 442376 | tf_op jit(solution)/shard_map/ppermute | solution.py:32
  16.4 1.6 %collective-permute-start.4 = (bf16[192,384]{1,0:T(8,128)(2,1)S(1)}, bf16[192,384]{1,0:T(8,128)(2,1)S(1)}, u32[]{:S(2)}, u32[]{:S(2)}) collective-permute-start(bf16[192,384]{1,0:T(8,128)(2,1)S(1)} %get-tuple-element.24), channel_id=1, source_target_pairs={{0,8},{4,12},{8,0},{12,4},{16,24},{20,28},{24,16},{28,20},{1,9},{5... | collective-permute-start | bytes 442376 | tf_op jit(solution)/shard_map/ppermute | solution.py:32
  17.9 3.3 %local.3.local_b = f32[2,64,1024]{2,1,0:T(8,128)S(1)} custom-call(f32[8,1024]{1,0:T(8,128)S(1)} %get-tuple-element.20.slide_ref, bf16[192,1024]{1,0:T(8,128)(2,1)S(1)} %copy-done, bf16[192,1024]{1,0:T(8,128)(2,1)S(1)} %copy-done.1, bf16[192,1024]{1,0:T(8,128)(2,1)S(1)} %copy-done.2), custom_call_target="tpu_custom_call" | custom-call | flops 2147483648 | bytes 1000000 | tf_op jit(solution)/shard_map/local/pallas_call | solution.py:438
  21.2 1.4 %near.1.near_ref = f32[208,1024]{1,0:T(8,128)S(1)} custom-call(f32[8,128]{1,0:T(8,128)S(1)} %get-tuple-element.17.q_norm_ref, bf16[240,1024]{1,0:T(8,128)(2,1)S(1)} %get-tuple-element.18.q_ref, bf16[48,1024]{1,0:T(8,128)(2,1)S(1)} %get-tuple-element.19.k_mask_ref, bf16[384,256]{1,0:T(8,128)(2,1)S(1)} %collective-permute-done.one_ref, ...), custom_call_target="tpu_custom_call" | custom-call | flops 536870912 | bytes 1000000 | tf_op jit(solution)/shard_map/near/pallas_call | solution.py:455
  22.6 0.0 collective-permute-done.5.refs_3_
  22.6 0.0 collective-permute-done.3.refs_0_
  22.6 0.0 collective-permute-done.4.refs_1_
  22.6 1.8 %last.1 = (f32[192,1024]{1,0:T(8,128)S(1)}, f32[8,256]{1,0:T(8,128)S(1)}) custom-call(f32[8,128]{1,0:T(8,128)S(1)} %get-tuple-element.17.q_norm_ref, bf16[240,1024]{1,0:T(8,128)(2,1)S(1)} %get-tuple-element.18.q_ref, bf16[48,1024]{1,0:T(8,128)(2,1)S(1)} %get-tuple-element.19.k_mask_ref, f32[2,64,1024]{2,1,0:T(8,128)S(1)} %local.2.local_a, ...), custom_call_target="tpu_custom_call" | custom-call | flops 536870912 | bytes 1000000 | tf_op jit(solution)/shard_map/last/pallas_call | solution.py:466
  24.5 0.1 collective-permute-start.8
  24.5 1.6 %collective-permute-start.7 = (f32[8,256]{1,0:T(8,128)S(1)}, f32[8,256]{1,0:T(8,128)S(1)}, u32[]{:S(2)}, u32[]{:S(2)}) collective-permute-start(f32[8,256]{1,0:T(8,128)S(1)} %get-tuple-element.28.refs_0_), channel_id=1, source_target_pairs={{0,2},{1,3},{2,0},{3,1},{4,6},{5,7},{6,4},{7,5},{8,10},{9,11},{10,... | collective-permute-start | bytes 24584 | tf_op jit(solution)/shard_map/ppermute | solution.py:32
  26.1 0.3 collective-permute-start.6
  26.4 1.2 %collective-permute-done.8.refs_3_ = f32[8,256]{1,0:T(8,128)S(1)} collective-permute-done((f32[8,256]{1,0:T(8,128)S(1)}, f32[8,256]{1,0:T(8,128)S(1)}, u32[]{:S(2)}, u32[]{:S(2)}) %collective-permute-start.8) | collective-permute-done | bytes 8224 | tf_op jit(solution)/shard_map/ppermute | solution.py:32
  27.6 0.6 %collective-permute-done.7.refs_2_ = f32[8,256]{1,0:T(8,128)S(1)} collective-permute-done((f32[8,256]{1,0:T(8,128)S(1)}, f32[8,256]{1,0:T(8,128)S(1)}, u32[]{:S(2)}, u32[]{:S(2)}) %collective-permute-start.7) | collective-permute-done | bytes 8224 | tf_op jit(solution)/shard_map/ppermute | solution.py:32
  28.3 0.0 collective-permute-done.6.refs_1_
  28.3 0.9 %norm.1 = bf16[192,1024]{1,0:T(8,128)(2,1)} custom-call(f32[192,1024]{1,0:T(8,128)S(1)} %get-tuple-element.26.att_ref, f32[2,192,128]{2,1,0:T(8,128)S(1)} %get-tuple-element.27.affine_ref, f32[8,256]{1,0:T(8,128)S(1)} %get-tuple-element.28.refs_0_, f32[8,256]{1,0:T(8,128)S(1)} %collective-permute-done.6.refs_1_, ...), custom_call_target="tpu_custom_call" | custom-call | tf_op jit(solution)/shard_map/norm/pallas_call | solution.py:484
  (6 shorter events, 0.0 us)
Async XLA Ops:
  0.0 10.0 %copy-start = (bf16[192,1024]{1,0:T(8,128)(2,1)S(1)}, bf16[192,1024]{1,0:T(8,128)(2,1)}, u32[]{:S(2)}) copy-start(bf16[192,1024]{1,0:T(8,128)(2,1)} %q_ref.4) | copy-start | bytes 1179652
  0.0 10.0 %copy-start.3 = (f32[192]{0:T(256)S(1)}, f32[192]{0:T(256)}, u32[]{:S(2)}) copy-start(f32[192]{0:T(256)} %param.10) | copy-start | bytes 2308
  0.0 10.0 %copy-start.4 = (f32[192]{0:T(256)S(1)}, f32[192]{0:T(256)}, u32[]{:S(2)}) copy-start(f32[192]{0:T(256)} %param.11) | copy-start | bytes 2308
  0.0 10.0 %copy-start.5 = (s32[8]{0:T(128)S(1)}, s32[8]{0:T(128)}, u32[]{:S(2)}) copy-start(s32[8]{0:T(128)} %lengths_ref.1) | copy-start | bytes 100
  0.0 11.0 %copy-start.2 = (bf16[192,1024]{1,0:T(8,128)(2,1)S(1)}, bf16[192,1024]{1,0:T(8,128)(2,1)}, u32[]{:S(2)}) copy-start(bf16[192,1024]{1,0:T(8,128)(2,1)} %v_ref.3) | copy-start | bytes 1179652
  2.8 8.2 %copy-start.1 = (bf16[192,1024]{1,0:T(8,128)(2,1)S(1)}, bf16[192,1024]{1,0:T(8,128)(2,1)}, u32[]{:S(2)}) copy-start(bf16[192,1024]{1,0:T(8,128)(2,1)} %k_ref.3) | copy-start | bytes 1179652
  2.8 12.9 %collective-permute-start.1 = (bf16[384,256]{1,0:T(8,128)(2,1)}, bf16[384,256]{1,0:T(8,128)(2,1)S(1)}, u32[]{:S(2)}, u32[]{:S(2)}) collective-permute-start(bf16[384,256]{1,0:T(8,128)(2,1)} %get-tuple-element.21), channel_id=1, source_target_pairs={{0,8},{4,12},{8,0},{12,4},{16,24},{20,28},{24,16},{28,20},{1,9},{5... | collective-permute-start | bytes 589832 | tf_op jit(solution)/shard_map/ppermute | solution.py:32
  5.9 9.9 %collective-permute-start = (bf16[384,256]{1,0:T(8,128)(2,1)}, bf16[384,256]{1,0:T(8,128)(2,1)S(1)}, u32[]{:S(2)}, u32[]{:S(2)}) collective-permute-start(bf16[384,256]{1,0:T(8,128)(2,1)} %get-tuple-element.21), channel_id=1, source_target_pairs={{0,4},{4,0},{8,12},{12,8},{16,20},{20,16},{24,28},{28,24},{1,5},{5... | collective-permute-start | bytes 589832 | tf_op jit(solution)/shard_map/ppermute | solution.py:32
  7.4 6.9 %collective-permute-start.2 = (bf16[192,128]{1,0:T(8,128)(2,1)}, bf16[192,128]{1,0:T(8,128)(2,1)S(1)}, u32[]{:S(2)}, u32[]{:S(2)}) collective-permute-start(bf16[192,128]{1,0:T(8,128)(2,1)} %get-tuple-element.22), channel_id=1, source_target_pairs={{0,16},{4,20},{8,24},{12,28},{16,0},{20,4},{24,8},{28,12},{1,17},{... | collective-permute-start | bytes 147464 | tf_op jit(solution)/shard_map/ppermute | solution.py:32
  14.3 8.3 %collective-permute-start.5 = (bf16[192,128]{1,0:T(8,128)(2,1)S(1)}, bf16[192,128]{1,0:T(8,128)(2,1)S(1)}, u32[]{:S(2)}, u32[]{:S(2)}) collective-permute-start(bf16[192,128]{1,0:T(8,128)(2,1)S(1)} %collective-permute-done.2.refs_0_.refs_2_), channel_id=1, source_target_pairs={{0,12},{4,8},{8,4},{12,0},{16,28},{20,24},{24,20},{28,16},{1,13},{... | collective-permute-start | bytes 147464 | tf_op jit(solution)/shard_map/ppermute | solution.py:32
  15.8 6.8 %collective-permute-start.3 = (bf16[192,384]{1,0:T(8,128)(2,1)S(1)}, bf16[192,384]{1,0:T(8,128)(2,1)S(1)}, u32[]{:S(2)}, u32[]{:S(2)}) collective-permute-start(bf16[192,384]{1,0:T(8,128)(2,1)S(1)} %get-tuple-element.23), channel_id=1, source_target_pairs={{0,4},{4,0},{8,12},{12,8},{16,20},{20,16},{24,28},{28,24},{1,5},{5... | collective-permute-start | bytes 442376 | tf_op jit(solution)/shard_map/ppermute | solution.py:32
  16.4 6.3 %collective-permute-start.4 = (bf16[192,384]{1,0:T(8,128)(2,1)S(1)}, bf16[192,384]{1,0:T(8,128)(2,1)S(1)}, u32[]{:S(2)}, u32[]{:S(2)}) collective-permute-start(bf16[192,384]{1,0:T(8,128)(2,1)S(1)} %get-tuple-element.24), channel_id=1, source_target_pairs={{0,8},{4,12},{8,0},{12,4},{16,24},{20,28},{24,16},{28,20},{1,9},{5... | collective-permute-start | bytes 442376 | tf_op jit(solution)/shard_map/ppermute | solution.py:32
  24.5 3.2 %collective-permute-start.8 = (f32[8,256]{1,0:T(8,128)S(1)}, f32[8,256]{1,0:T(8,128)S(1)}, u32[]{:S(2)}, u32[]{:S(2)}) collective-permute-start(f32[8,256]{1,0:T(8,128)S(1)} %get-tuple-element.28.refs_0_), channel_id=1, source_target_pairs={{0,3},{1,2},{2,1},{3,0},{4,7},{5,6},{6,5},{7,4},{8,11},{9,10},{10,... | collective-permute-start | bytes 24584 | tf_op jit(solution)/shard_map/ppermute | solution.py:32
  24.5 3.7 %collective-permute-start.7 = (f32[8,256]{1,0:T(8,128)S(1)}, f32[8,256]{1,0:T(8,128)S(1)}, u32[]{:S(2)}, u32[]{:S(2)}) collective-permute-start(f32[8,256]{1,0:T(8,128)S(1)} %get-tuple-element.28.refs_0_), channel_id=1, source_target_pairs={{0,2},{1,3},{2,0},{3,1},{4,6},{5,7},{6,4},{7,5},{8,10},{9,11},{10,... | collective-permute-start | bytes 24584 | tf_op jit(solution)/shard_map/ppermute | solution.py:32
  26.1 2.1 %collective-permute-start.6 = (f32[8,256]{1,0:T(8,128)S(1)}, f32[8,256]{1,0:T(8,128)S(1)}, u32[]{:S(2)}, u32[]{:S(2)}) collective-permute-start(f32[8,256]{1,0:T(8,128)S(1)} %get-tuple-element.28.refs_0_), channel_id=1, source_target_pairs={{0,1},{1,0},{2,3},{3,2},{4,5},{5,4},{6,7},{7,6},{8,9},{9,8},{10,11... | collective-permute-start | bytes 24584 | tf_op jit(solution)/shard_map/ppermute | solution.py:32

commit v3 on v2

v3 whole, which is shorter than its diff:
```python
import functools
import math

import jax
import jax.numpy as jnp
import numpy as np
from jax import lax
from jax.experimental import pallas as pl
from jax.experimental.pallas import tpu as pltpu
from jax.sharding import PartitionSpec as P

D = 768
HD = 48
SEG = 1024
HEADS = 4
BLOCKED = -1e30
SCALE = 1.0 / math.sqrt(HD)
LOG2_SCALE = math.log2(math.e) * SCALE
LEAST, MOST = 1e-20, 1e30
F32 = jnp.float32
BF16 = jnp.bfloat16
HBM = pl.BlockSpec(memory_space=pltpu.HBM)
VMEM = pl.BlockSpec(memory_space=pltpu.VMEM)
SMEM = pl.BlockSpec(memory_space=pltpu.SMEM)
PACK_LIMIT = 107 * 2**19
PARAMS = pltpu.CompilerParams(vmem_limit_bytes=40 * 2**20)


def partner(value, axis, mask):
    pairs = [(source, source ^ mask) for source in range(lax.axis_size(axis))]
    return lax.ppermute(value, axis, pairs)


def thirds(value):
    parts = []
    for _ in range(3):
        part = float(np.asarray(value, jnp.bfloat16))
        parts.append(part)
        value -= part
    return parts


def bias_rows(flags, factor):
    return [jnp.where(flags, F32(part), F32(0.0)) for part in thirds(math.log(factor) / SCALE)]


def flag_rows(flags):
    return [jnp.where(flags, F32(1.0), F32(0.0))] * 3


def slide_of(positions, lengths_ref):
    slide = jnp.zeros(positions.shape, jnp.int32)
    end = jnp.int32(0)
    for k in range(lengths_ref.shape[0]):
        end = end + lengths_ref[k]
        slide = slide + jnp.where(positions >= end, 1, 0)
    return slide


def stack_rows(rows, count):
    width = rows[0].shape[1]
    index = lax.broadcasted_iota(jnp.int32, (count, width), 0)
    block = jnp.zeros((count, width), F32)
    for k, row in enumerate(rows):
        block = jnp.where(index == k, row, block)
    return block


def lanes(width):
    return lax.broadcasted_iota(jnp.int32, (1, width), 1)


def compact_index(place, head_place):
    quarter = place >> 6
    return 16 * (place & 15) + 4 * ((place >> 4) & 3) + ((quarter + head_place) & 3)


def only_head(ref, own):
    width = ref.shape[1]
    return [
        ref[i * HD : (i + 1) * HD, :]
        * jnp.broadcast_to(jnp.where(own == i, F32(1.0), F32(0.0)), (HD, width)).astype(BF16)
        for i in range(HEADS)
    ]


def pack_kernel(k_hbm, v_hbm, pair_ref, sixteenth_ref, *scratch):
    targets, arrived = scratch[:2], scratch[2]
    copies = []
    for at, (source, target) in enumerate(zip((k_hbm, v_hbm), targets)):
        for i in range(HEADS):
            part = pl.ds(i * HD, HD)
            copies.append(
                pltpu.make_async_copy(source.at[part, :], target.at[part, :], arrived.at[at, i])
            )
    for copy in copies:
        copy.start()
    features, rows = targets[0].shape
    packed = rows // 4
    head_place = lax.axis_index("head")
    group = lax.broadcasted_iota(jnp.int32, (rows, packed), 0) >> 2
    place = lax.broadcasted_iota(jnp.int32, (rows, packed), 1)
    pick = jnp.where(compact_index(place, head_place) == group, F32(1.0), F32(0.0)).astype(BF16)
    own = lanes(rows) & 3
    results = []
    for at, ref in enumerate(targets):
        for copy in copies[at * HEADS : (at + 1) * HEADS]:
            copy.wait()
        masked = jnp.concatenate(only_head(ref, own), axis=0)
        compact = jnp.dot(masked, pick, preferred_element_type=F32)
        pair_ref[at * features : (at + 1) * features, :] = compact.astype(BF16)
        results.append(compact[:, : packed // 4])
    sixteenth_ref[...] = jnp.concatenate(results, axis=1).astype(BF16)


def relay_kernel(one_ref, two_ref, *refs):
    beyond, (to_one, to_two) = refs[:-2], refs[-2:]
    features, width = to_one.shape[0], one_ref.shape[1]
    to_one[:, :width] = two_ref[features:, :]
    to_two[:, :width] = one_ref[:features, :]
    for at, piece in enumerate(beyond):
        count = piece.shape[1]
        for out, start in ((to_one, width), (to_two, width)):
            out[:, start + at * count : start + (at + 1) * count] = piece[...]


def pass_kernel(*refs):
    out = refs[-1]
    at = 0
    for piece in refs[:-1]:
        out[:, at : at + piece.shape[1]] = piece[...]
        at += piece.shape[1]


def mask_kernel(kinds, distances, lengths_ref, gain_ref, bias_ref, q_ref, q_out, k_mask_out, affine_out, slide_out):
    rows = q_ref.shape[1]
    features = HEADS * HD
    slides = lengths_ref.shape[0]
    tile = lanes(rows)
    seq_place = lax.axis_index("seq")
    head_place = lax.axis_index("head")
    extra = k_mask_out.shape[0] - HEADS * slides

    counts = [rows // 4**kind for kind in kinds]
    total = sum(counts)
    first = jnp.concatenate(
        [
            (seq_place ^ distance) * rows + 4 * compact_index(lanes(count), head_place)
            for count, distance in zip(counts, distances)
        ],
        axis=1,
    )
    slide = slide_of(first + lax.broadcasted_iota(jnp.int32, (HEADS, total), 0), lengths_ref)
    row = lax.broadcasted_iota(jnp.int32, (slides, total), 0)
    masks = [jnp.where(slide[i : i + 1] == row, F32(0.0), F32(BLOCKED)) for i in range(HEADS)]
    added = []
    for kind, count in zip(kinds, counts):
        place = lanes(count)
        none = jnp.zeros((1, count), F32)
        in_third = place < rows // 16
        in_fourth = place < rows // 64
        if kind == 1:
            extras = bias_rows(in_third, 2.0) + bias_rows(in_fourth, 1.5) + [none, none]
        elif kind == 2:
            extras = [none] * 3 + bias_rows(in_fourth, 2.0) + [none + BLOCKED, none]
        else:
            extras = [none] * 6 + [none, none + BLOCKED]
        added.append(stack_rows(extras, extra))
    masks.append(jnp.concatenate(added, axis=1))
    k_mask_out[...] = jnp.concatenate(masks, axis=0).astype(BF16)

    slide = slide_of(seq_place * rows + tile, lengths_ref)
    same = slide == lax.broadcasted_iota(jnp.int32, (slides, rows), 0)
    slide_out[...] = jnp.where(same, F32(1.0), F32(0.0))
    masks = [jnp.where(same & ((tile & 3) == i), F32(1.0), F32(0.0)) for i in range(HEADS)]
    third = ((tile >> 2) & 3) == head_place
    fourth = ((tile >> 2) & 15) == head_place
    masks.append(
        stack_rows(
            flag_rows(third) + flag_rows(fourth) + flag_rows(~third)[:1] + flag_rows(~fourth)[:1],
            extra,
        )
    )
    q_out[:features, :] = jnp.concatenate(only_head(q_ref, tile & 3), axis=0)
    q_out[features:, :] = jnp.concatenate(masks, axis=0).astype(BF16)

    r = lax.broadcasted_iota(jnp.int32, (features, features), 0)
    c = lax.broadcasted_iota(jnp.int32, (features, features), 1)
    for at, ref in enumerate((gain_ref, bias_ref)):
        column = jnp.sum(jnp.where(r == c, ref[...], 0.0), axis=1, keepdims=True)
        affine_out[at] = jnp.broadcast_to(column, (features, 128))


def weigh(keys_t, queries, values):
    scores = jnp.dot(keys_t, queries, preferred_element_type=F32)
    probs = jnp.exp2(scores * LOG2_SCALE).astype(BF16)
    return jnp.dot(values, probs, preferred_element_type=F32)


def weigh_with_peak(keys_t, queries, values):
    scores = jnp.dot(keys_t, queries, preferred_element_type=F32)
    peak = jnp.max(scores, axis=0, keepdims=True)
    probs = jnp.exp2((scores - peak) * LOG2_SCALE).astype(BF16)
    return peak, jnp.dot(values, probs, preferred_element_type=F32)


def local_operands(i, slide_ref, q_ref, k_ref, v_ref):
    rows = q_ref.shape[1]
    slides = slide_ref.shape[0]
    tile = lanes(rows)
    head_place = lax.axis_index("head")
    query_slides = slide_ref[...]
    key_slides = (1.0 - query_slides) * F32(BLOCKED)
    extra = -(-(slides + 9) // 16) * 16 - slides
    mine = slice(i * HD, (i + 1) * HD)
    second = (tile & 3) == i
    third = (tile & 15) == 4 * head_place + i
    fourth = (tile & 63) == 4 * head_place + i
    query_extra = stack_rows(flag_rows(second) + flag_rows(third) + flag_rows(fourth), extra)
    key_extra = stack_rows(
        bias_rows(second, 2.0) + bias_rows(third, 1.5) + bias_rows(fourth, 4.0 / 3.0), extra
    )
    queries = jnp.concatenate(
        [q_ref[mine, :], jnp.concatenate([query_slides, query_extra], axis=0).astype(BF16)], axis=0
    )
    keys = jnp.concatenate(
        [k_ref[mine, :], jnp.concatenate([key_slides, key_extra], axis=0).astype(BF16)], axis=0
    )
    values = jnp.concatenate([v_ref[mine, :], jnp.ones((16, rows), BF16)], axis=0)
    return keys.T, queries, values


def local_kernel(first, slide_ref, q_ref, k_ref, v_ref, out_ref):
    for head in range(out_ref.shape[0]):
        mixed = weigh(*local_operands(first + head, slide_ref, q_ref, k_ref, v_ref))
        out_ref[head] = mixed[: HD + 8]


def lay_out(pieces, mask_at, k_mask_ref, k_ref, v_ref):
    features = HEADS * HD
    at = 0
    beside = []
    for kind, keys, values in pieces:
        count = keys.shape[1] if kind == 1 else keys.shape[1] // 2 // 4 ** (kind - 2)
        if kind == 1:
            v_ref[:features, at : at + count] = values[...]
        else:
            half = values.shape[1] // 2
            beside.append(values[:, half : half + count])
        masks = k_mask_ref[:, mask_at + at : mask_at + at + count]
        k_ref[at : at + count, :] = jnp.concatenate([keys[:, :count], masks], axis=0).T
        at += count
    if beside:
        width = sum(part.shape[1] for part in beside)
        v_ref[:features, at - width : at] = jnp.concatenate(beside, axis=1)
    v_ref[features:, :at] = jnp.ones((16, at), BF16)


def halves(ref):
    features = HEADS * HD
    return ref.at[:features, :], ref.at[features:, :]


def with_more(i, part, total, mixed):
    features = HEADS * HD
    selected = (lanes(mixed.shape[1]) & 3) == i
    return (
        part + jnp.where(selected, mixed[i * HD : (i + 1) * HD], 0.0),
        total + jnp.where(selected, mixed[features : features + 1], 0.0),
    )


def parts_of(ref, i):
    features = HEADS * HD
    return ref[i * HD : (i + 1) * HD, :], ref[features + i : features + i + 1, :]


def store_parts(ref, i, part, total):
    features = HEADS * HD
    ref[i * HD : (i + 1) * HD, :] = part
    ref[features + i : features + i + 1, :] = total


def near_kernel(q_ref, k_mask_ref, local_a, local_b, one_ref, two_ref, out_ref, k_ref, v_ref):
    lay_out([(1, *halves(one_ref)), (1, *halves(two_ref))], 0, k_mask_ref, k_ref, v_ref)
    mixed = weigh(k_ref[...], q_ref[...], v_ref[...])
    for i in range(HEADS):
        ref = (local_a, local_b)[i // 2].at[i % 2]
        store_parts(out_ref, i, *with_more(i, ref[:HD, :], ref[HD : HD + 1, :], mixed))


def far_kernel(kinds, mask_at, q_ref, k_mask_ref, near_ref, *refs):
    out_ref, k_ref, v_ref = refs[-3:]
    pieces = far_pieces(kinds, q_ref.shape[1], *refs[:2], refs[2:-3])
    lay_out(pieces, mask_at, k_mask_ref, k_ref, v_ref)
    mixed = weigh(k_ref[...], q_ref[...], v_ref[...])
    for i in range(HEADS):
        store_parts(out_ref, i, *with_more(i, *parts_of(near_ref, i), mixed))


def far_pieces(kinds, rows, from_one, from_two, rest):
    width = rows // 4
    beyond = [
        ref.at[:, at : at + rows // 8]
        for ref in (from_one, from_two)
        for at in range(width, ref.shape[1], rows // 8)
    ] + list(rest)
    diagonal = (1, from_two.at[:, :width], from_one.at[:, :width])
    return [diagonal] + [(kind, ref, ref) for kind, ref in zip(kinds[1:], beyond)]


def three_pieces(kinds, rows, from_three):
    return [
        (kind, *[from_three.at[:, at * rows // 8 : (at + 1) * rows // 8]] * 2)
        for at, kind in enumerate(kinds)
    ]


def add_up(head_parts, att_ref, sums_ref):
    sums = squares = None
    for i, attended in enumerate(head_parts):
        att_ref[i * HD : (i + 1) * HD, :] = attended
        head_sum = jnp.sum(attended, axis=0, keepdims=True)
        head_squares = jnp.sum(attended * attended, axis=0, keepdims=True)
        sums = head_sum if sums is None else sums + head_sum
        squares = head_squares if squares is None else squares + head_squares
    quarter = sums_ref.shape[1]
    for at in range(4):
        sums_ref[at : at + 1, :] = sums[:, at * quarter : (at + 1) * quarter]
        sums_ref[4 + at : 5 + at, :] = squares[:, at * quarter : (at + 1) * quarter]


def last_kernel(kinds, mask_at, raw_refs, q_ref, k_mask_ref, far_ref, from_three, *refs):
    raw, (att_ref, sums_ref, k_three, v_three, k_ref, v_ref) = refs[:raw_refs], refs[raw_refs:]
    rows = q_ref.shape[1]
    features = HEADS * HD
    own = lanes(rows) & 3
    three = three_pieces(kinds[-(from_three.shape[1] * 8 // rows) :], rows, from_three)
    lay_out(three, mask_at, k_mask_ref, k_three, v_three)
    mixed = weigh(k_three[...], q_ref[...], v_three[...])
    parts = []
    least = most = None
    for i in range(HEADS):
        part, total = with_more(i, *parts_of(far_ref, i), mixed)
        parts.append(part * (1.0 / total))
        least = total if least is None else jnp.minimum(least, total)
        most = total if most is None else jnp.maximum(most, total)
    add_up(parts, att_ref, sums_ref)
    fine = (least >= LEAST) & (most <= MOST)
    worst = jnp.max(jnp.where(fine, 0.0, 1.0))

    @pl.when(worst > 0.0)
    def _():
        slide_ref, queries, keys, values, one_ref, two_ref, from_one, from_two = raw[:8]
        pieces = [(1, *halves(one_ref)), (1, *halves(two_ref))]
        pieces += far_pieces(kinds[2:], rows, from_one, from_two, raw[8:]) + three
        lay_out(pieces, 0, k_mask_ref, k_ref, v_ref)
        far_peak, mixed = weigh_with_peak(k_ref[...], q_ref[...], v_ref[...])
        parts = []
        for i in range(HEADS):
            mine = slice(i * HD, (i + 1) * HD)
            here, local = weigh_with_peak(*local_operands(i, slide_ref, queries, keys, values))
            there = jnp.where(own == i, far_peak, F32(BLOCKED))
            top = jnp.maximum(here, there)
            keep = jnp.exp2((here - top) * LOG2_SCALE)
            add = jnp.where(own == i, jnp.exp2((there - top) * LOG2_SCALE), F32(0.0))
            total = keep * local[HD : HD + 1] + add * mixed[features : features + 1]
            parts.append((local[:HD] * keep + mixed[mine] * add) / total)
        add_up(parts, att_ref, sums_ref)


def norm_kernel(att_ref, affine_ref, *refs):
    sum_refs, out_ref = refs[:-1], refs[-1]
    sums = sum_refs[0][...]
    for ref in sum_refs[1:]:
        sums = sums + ref[...]
    mean = sums[:4] / D
    variance = sums[4:] / D - mean * mean
    inverse = lax.rsqrt(variance + 1e-05)
    width = affine_ref.shape[2]
    quarter = mean.shape[1]
    for start in range(0, att_ref.shape[1], width):
        at, first = start // quarter, start % quarter
        part = slice(first, first + width)
        normed = (att_ref[:, start : start + width] - mean[at : at + 1, part]) * inverse[at : at + 1, part]
        out_ref[:, start : start + width] = (normed * affine_ref[0] + affine_ref[1]).astype(BF16)


def cost(flops, moved, exps=0):
    return pl.CostEstimate(flops=int(flops), bytes_accessed=int(moved), transcendentals=int(exps))


def per_device(queries, keys, values, slide_lengths, norm_gain, norm_bias):
    features, rows = queries.shape
    total_rows = rows * lax.axis_size("seq")
    spans = [min(SEG * 4**b, total_rows) // rows for b in range(4)]
    assert spans[1] == 4 and features == HEADS * HD
    pair, own = pl.pallas_call(
        pack_kernel,
        out_shape=(
            jax.ShapeDtypeStruct((2 * features, rows // 4), BF16),
            jax.ShapeDtypeStruct((features, rows // 8), BF16),
        ),
        in_specs=[HBM] * 2,
        out_specs=(VMEM,) * 2,
        scratch_shapes=[
            pltpu.VMEM((features, rows), BF16),
            pltpu.VMEM((features, rows), BF16),
            pltpu.SemaphoreType.DMA((2, HEADS)),
        ],
        compiler_params=pltpu.CompilerParams(vmem_limit_bytes=PACK_LIMIT),
        cost_estimate=cost(2 * 384 * 256 * 1024, 10**6),
        name="pack",
    )(keys, values)

    beyond = [(partner(own, "seq", m), m) for m in range(spans[2], spans[3], spans[2])]
    beyond = beyond + [
        (partner(piece, "seq", m), m ^ d)
        for m in range(spans[1], spans[2], spans[1])
        for piece, d in [(own, 0)] + beyond
    ]
    one, two = partner(pair, "seq", 1), partner(pair, "seq", 2)
    beyond_distances = [d ^ m for m in (1, 2, 0, 3) for _, d in beyond]
    distances = [1, 2, 3] + beyond_distances
    kinds = [1, 1, 1] + [2 if d < spans[2] else 3 for d in beyond_distances]
    counts = [rows // 4**kind for kind in kinds]
    three = len(kinds) - len(beyond)
    near_count, far_count, three_count = sum(counts[:2]), sum(counts[2:three]), sum(counts[three:])
    key_count = sum(counts)

    mask_rows = -(-(HEADS * slide_lengths.shape[0] + 8) // 16) * 16
    depth = features + mask_rows
    own_queries, key_masks, affine, slides = pl.pallas_call(
        functools.partial(mask_kernel, kinds, distances),
        out_shape=(
            jax.ShapeDtypeStruct((depth, rows), BF16),
            jax.ShapeDtypeStruct((mask_rows, key_count), BF16),
            jax.ShapeDtypeStruct((2, features, 128), F32),
            jax.ShapeDtypeStruct((slide_lengths.shape[0], rows), F32),
        ),
        in_specs=[SMEM, VMEM, VMEM, VMEM],
        out_specs=(VMEM,) * 4,
        compiler_params=PARAMS,
        cost_estimate=cost(10**8, 10**6),
        name="masks",
    )(slide_lengths, norm_gain[None, :], norm_bias[None, :], queries)

    def local(first, work, *operands):
        return pl.pallas_call(
            functools.partial(local_kernel, first),
            out_shape=jax.ShapeDtypeStruct((2, HD + 8, rows), F32),
            in_specs=[VMEM] * 4,
            out_specs=VMEM,
            compiler_params=PARAMS,
            cost_estimate=cost(work, 10**5),
            name="local",
        )(*operands)

    local_a = local(0, 10**9, slides, queries, keys, values)
    beyond_pieces = [piece for piece, _ in beyond]
    local_a, one, two, beyond_pieces = lax.optimization_barrier((local_a, one, two, beyond_pieces))
    relayed = jax.ShapeDtypeStruct((features, rows // 4 + rows // 8 * len(beyond)), BF16)
    passed_on = jax.ShapeDtypeStruct((features, rows // 8 * len(beyond)), BF16)
    to_one, to_two = pl.pallas_call(
        relay_kernel,
        out_shape=(relayed, relayed),
        in_specs=[VMEM] * (2 + len(beyond)),
        out_specs=(VMEM,) * 2,
        compiler_params=PARAMS,
        cost_estimate=cost(0, 10**6),
        name="relay",
    )(one, two, *beyond_pieces)
    from_one, from_two = partner(to_one, "seq", 1), partner(to_two, "seq", 2)
    to_three = pl.pallas_call(
        pass_kernel,
        out_shape=passed_on,
        in_specs=[VMEM] * len(beyond),
        out_specs=VMEM,
        compiler_params=PARAMS,
        cost_estimate=cost(0, 10**5),
        name="pass_on",
    )(*lax.optimization_barrier((beyond_pieces, to_one, to_two))[0])
    from_three = partner(to_three, "seq", 3)
    held, _ = lax.optimization_barrier((queries, (to_one, to_two, to_three)))
    local_b = local(2, 3 * 10**8, slides, held, keys, values)

    def scratch(count):
        return [pltpu.VMEM((count, depth), BF16), pltpu.VMEM((features + 16, count), BF16)]

    near_part = pl.pallas_call(
        near_kernel,
        out_shape=jax.ShapeDtypeStruct((features + 8, rows), F32),
        in_specs=[VMEM] * 6,
        out_specs=VMEM,
        scratch_shapes=scratch(near_count),
        compiler_params=PARAMS,
        cost_estimate=cost(2 * rows * near_count * 512, 10**5),
        name="near",
    )(own_queries, key_masks, local_a, local_b, one, two)

    far_part = pl.pallas_call(
        functools.partial(far_kernel, kinds[2:three], near_count),
        out_shape=jax.ShapeDtypeStruct((features + 8, rows), F32),
        in_specs=[VMEM] * (5 + len(beyond)),
        out_specs=VMEM,
        scratch_shapes=scratch(far_count),
        compiler_params=PARAMS,
        cost_estimate=cost(2 * rows * far_count * 512, 10**5),
        name="far",
    )(own_queries, key_masks, near_part, from_one, from_two, *beyond_pieces)

    raw = (slides, queries, keys, values, one, two, from_one, from_two, *beyond_pieces)
    attended, sums = pl.pallas_call(
        functools.partial(last_kernel, kinds, key_count - three_count, len(raw)),
        out_shape=(
            jax.ShapeDtypeStruct((features, rows), F32),
            jax.ShapeDtypeStruct((8, rows // 4), F32),
        ),
        in_specs=[VMEM] * (4 + len(raw)),
        out_specs=(VMEM, VMEM),
        scratch_shapes=scratch(three_count) + scratch(key_count),
        compiler_params=PARAMS,
        cost_estimate=cost(2 * rows * three_count * 512, 10**5),
        name="last",
    )(own_queries, key_masks, far_part, from_three, *raw)

    all_sums = [sums] + [partner(sums, "head", m) for m in range(1, lax.axis_size("head"))]
    return pl.pallas_call(
        norm_kernel,
        out_shape=jax.ShapeDtypeStruct((features, rows), BF16),
        in_specs=[VMEM] * (2 + len(all_sums)),
        out_specs=VMEM,
        compiler_params=PARAMS,
        name="norm",
    )(attended, affine, *all_sums)


def solution(mesh):
    placed = (P("head", "seq"), P("head", "seq"), P("head", "seq"), P(), P("head"), P("head"))
    return jax.shard_map(
        per_device, mesh=mesh, in_specs=placed, out_specs=P("head", "seq"), check_vma=False
    )
```

time: 29.3 us -> 34 us (1.16)
  Pallas kernels: 14.5 us -> 17.9 us
  waiting for transfers between devices: 1.89 us -> 3.19 us
    pallas_call x2 -> x4, Pallas kernels: 3.21 us -> 10.3 us  [the longest x1 8.77 us: per_device(): pl.pallas_call(functools.partial(last_kernel, kinds, key_count - three_co...]
    pallas_call x2, Pallas kernels: 6.54 us -> 3.95 us  [local(): pl.pallas_call(functools.partial(local_kernel, first), out_shape=jax.Shap...]
    ppermute x9, waiting for transfers between devices: 1.89 us -> 3.19 us  [partner(): return lax.ppermute(value, axis, pairs)]
    pallas_call x1, Pallas kernels: 2.75 us -> 1.94 us  [per_device(): pl.pallas_call(pack_kernel, out_shape=(jax.ShapeDtypeStruct((2 * features...]
  transfers between devices with their start and end apart: 9 -> 9, of which waited for: 2 -> 5; matrix products, arithmetic and copies ran while one was open for 0% -> 0% of each run, Pallas kernels for 31% -> 18%
where the time goes in v3:
time: 34 us; the launch traced here: 33.9 us
  Pallas kernels  17.9 us (53%)
  starting transfers between devices  12.7 us (37%)
  waiting for transfers between devices  3.19 us (9%)
    ppermute x9, starting transfers between devices, partner(): return lax.ppermute(value, axis, pairs)  12.7 us
    pallas_call x1, Pallas kernels, per_device(): pl.pallas_call(functools.partial(last_kernel, kinds, key_count - three_co...  8.77 us
    pallas_call x2, Pallas kernels, local(): pl.pallas_call(functools.partial(local_kernel, first), out_shape=jax.Shap...  3.95 us
    ppermute x9, waiting for transfers between devices, partner(): return lax.ppermute(value, axis, pairs)  3.19 us
    pallas_call x1, Pallas kernels, per_device(): pl.pallas_call(pack_kernel, out_shape=(jax.ShapeDtypeStruct((2 * features...  1.94 us
    pallas_call x1, Pallas kernels, per_device(): pl.pallas_call(norm_kernel, out_shape=jax.ShapeDtypeStruct((features, row...  0.92 us
    pallas_call x1, Pallas kernels, per_device(): pl.pallas_call(functools.partial(mask_kernel, kinds, distances), out_shap...  0.81 us
    pallas_call x1, Pallas kernels, per_device(): pl.pallas_call(functools.partial(far_kernel, kinds[2:three], near_count),...  0.75 us
  transfers between devices with their start and end apart: 9, of which 5 were waited for; matrix products, arithmetic and copies ran while one was open for 0% of the time, Pallas kernels for 18%

profile of v3, /device:TPU:0, one launch (start us, length us, event | category | flops | bytes accessed | tf_op | source)
XLA Modules:
  0.0 33.9 jit_solution(16643663497070122943)
XLA Ops:
  0.0 1.9 %pack.1 = (bf16[384,256]{1,0:T(8,128)(2,1)S(1)}, bf16[192,128]{1,0:T(8,128)(2,1)S(1)}) custom-call(bf16[192,1024]{1,0:T(8,128)(2,1)} %refs_2_.1, bf16[192,1024]{1,0:T(8,128)(2,1)} %refs_3_.1), custom_call_target="tpu_custom_call" | custom-call | flops 201326592 | bytes 1000000 | tf_op jit(solution)/shard_map/pack/pallas_call | solution.py:398
  2.0 0.0 copy-start.1
  2.0 3.1 %collective-permute-start.1 = (bf16[384,256]{1,0:T(8,128)(2,1)S(1)}, bf16[384,256]{1,0:T(8,128)(2,1)S(1)}, u32[]{:S(2)}, u32[]{:S(2)}) collective-permute-start(bf16[384,256]{1,0:T(8,128)(2,1)S(1)} %get-tuple-element.24), channel_id=1, source_target_pairs={{0,8},{4,12},{8,0},{12,4},{16,24},{20,28},{24,16},{28,20},{1,9},{5... | collective-permute-start | bytes 589832 | tf_op jit(solution)/shard_map/ppermute | solution.py:31
  5.1 1.5 %collective-permute-start = (bf16[384,256]{1,0:T(8,128)(2,1)S(1)}, bf16[384,256]{1,0:T(8,128)(2,1)S(1)}, u32[]{:S(2)}, u32[]{:S(2)}) collective-permute-start(bf16[384,256]{1,0:T(8,128)(2,1)S(1)} %get-tuple-element.24), channel_id=1, source_target_pairs={{0,4},{4,0},{8,12},{12,8},{16,20},{20,16},{24,28},{28,24},{1,5},{5... | collective-permute-start | bytes 589832 | tf_op jit(solution)/shard_map/ppermute | solution.py:31
  6.6 2.6 %collective-permute-start.2 = (bf16[192,128]{1,0:T(8,128)(2,1)S(1)}, bf16[192,128]{1,0:T(8,128)(2,1)S(1)}, u32[]{:S(2)}, u32[]{:S(2)}) collective-permute-start(bf16[192,128]{1,0:T(8,128)(2,1)S(1)} %get-tuple-element.25), channel_id=1, source_target_pairs={{0,16},{4,20},{8,24},{12,28},{16,0},{20,4},{24,8},{28,12},{1,17},{... | collective-permute-start | bytes 147464 | tf_op jit(solution)/shard_map/ppermute | solution.py:31
  9.2 0.0 copy-done
  9.2 0.0 copy-done.3
  9.2 0.0 copy-done.4
  9.2 0.0 copy-done.5
  9.2 0.8 %masks.1 = (bf16[240,1024]{1,0:T(8,128)(2,1)S(1)}, bf16[48,1024]{1,0:T(8,128)(2,1)S(1)}, f32[2,192,128]{2,1,0:T(8,128)S(1)}, f32[8,1024]{1,0:T(8,128)S(1)}) custom-call(s32[8]{0:T(128)S(1)} %copy-done.5, f32[1,192]{1,0:T(1,128)S(1)} %bitcast.2, f32[1,192]{1,0:T(1,128)S(1)} %bitcast.3, bf16[192,1024]{1,0:T(8,128)(2,1)S(1)} %copy-done), custom_call_target="tpu_custom_call" | custom-call | flops 100000000 | bytes 1000000 | tf_op jit(solution)/shard_map/masks/pallas_call | solution.py:433
  10.0 0.0 copy-done.2
  10.0 2.0 %local.2.local_a = f32[2,56,1024]{2,1,0:T(8,128)S(1)} custom-call(f32[8,1024]{1,0:T(8,128)S(1)} %get-tuple-element.23.slide_ref.refs_0_, bf16[192,1024]{1,0:T(8,128)(2,1)S(1)} %copy-done, bf16[192,1024]{1,0:T(8,128)(2,1)S(1)} %copy-done.1, bf16[192,1024]{1,0:T(8,128)(2,1)S(1)} %copy-done.2), custom_call_target="tpu_custom_call" | custom-call | flops 1000000000 | bytes 100000 | tf_op jit(solution)/shard_map/local/pallas_call | solution.py:449
  12.0 0.1 collective-permute-done.2.refs_0_.refs_2_.refs_8_
  12.1 0.0 collective-permute-done.1.two_ref.refs_5_
  12.1 0.0 collective-permute-done.one_ref.refs_4_
  12.1 0.9 %collective-permute-start.3 = (bf16[192,384]{1,0:T(8,128)(2,1)S(1)}, bf16[192,384]{1,0:T(8,128)(2,1)S(1)}, u32[]{:S(2)}, u32[]{:S(2)}) collective-permute-start(bf16[192,384]{1,0:T(8,128)(2,1)S(1)} %get-tuple-element.30), channel_id=1, source_target_pairs={{0,4},{4,0},{8,12},{12,8},{16,20},{20,16},{24,28},{28,24},{1,5},{5... | collective-permute-start | bytes 442376 | tf_op jit(solution)/shard_map/ppermute | solution.py:31
  13.0 2.4 %collective-permute-start.4 = (bf16[192,384]{1,0:T(8,128)(2,1)S(1)}, bf16[192,384]{1,0:T(8,128)(2,1)S(1)}, u32[]{:S(2)}, u32[]{:S(2)}) collective-permute-start(bf16[192,384]{1,0:T(8,128)(2,1)S(1)} %get-tuple-element.31), channel_id=1, source_target_pairs={{0,8},{4,12},{8,0},{12,4},{16,24},{20,28},{24,16},{28,20},{1,9},{5... | collective-permute-start | bytes 442376 | tf_op jit(solution)/shard_map/ppermute | solution.py:31
  15.4 0.3 collective-permute-start.5
  15.7 2.0 %local.3.local_b = f32[2,56,1024]{2,1,0:T(8,128)S(1)} custom-call(f32[8,1024]{1,0:T(8,128)S(1)} %get-tuple-element.23.slide_ref.refs_0_, bf16[192,1024]{1,0:T(8,128)(2,1)S(1)} %copy-done, bf16[192,1024]{1,0:T(8,128)(2,1)S(1)} %copy-done.1, bf16[192,1024]{1,0:T(8,128)(2,1)S(1)} %copy-done.2), custom_call_target="tpu_custom_call" | custom-call | flops 300000000 | bytes 100000 | tf_op jit(solution)/shard_map/local/pallas_call | solution.py:449
  17.7 0.7 %near.1.near_ref = f32[200,1024]{1,0:T(8,128)S(1)} custom-call(bf16[240,1024]{1,0:T(8,128)(2,1)S(1)} %get-tuple-element.21.q_ref, bf16[48,1024]{1,0:T(8,128)(2,1)S(1)} %get-tuple-element.22.k_mask_ref, f32[2,56,1024]{2,1,0:T(8,128)S(1)} %local.2.local_a, f32[2,56,1024]{2,1,0:T(8,128)S(1)} %local.3.local_b, ...), custom_call_target="tpu_custom_call" | custom-call | flops 536870912 | bytes 100000 | tf_op jit(solution)/shard_map/near/pallas_call | solution.py:490
  18.4 0.0 collective-permute-done.3.refs_0_.refs_6_
  18.4 0.1 collective-permute-done.4.refs_1_.refs_7_
  18.5 0.8 %far.1.far_ref = f32[200,1024]{1,0:T(8,128)S(1)} custom-call(bf16[240,1024]{1,0:T(8,128)(2,1)S(1)} %get-tuple-element.21.q_ref, bf16[48,1024]{1,0:T(8,128)(2,1)S(1)} %get-tuple-element.22.k_mask_ref, f32[200,1024]{1,0:T(8,128)S(1)} %near.1.near_ref, bf16[192,384]{1,0:T(8,128)(2,1)S(1)} %collective-permute-done.3.refs_0_.refs_6_, ...), custom_call_target="tpu_custom_call" | custom-call | flops 469762048 | bytes 100000 | tf_op jit(solution)/shard_map/far/pallas_call | solution.py:501
  19.3 1.1 %collective-permute-done.5.from_three = bf16[192,128]{1,0:T(8,128)(2,1)S(1)} collective-permute-done((bf16[192,128]{1,0:T(8,128)(2,1)S(1)}, bf16[192,128]{1,0:T(8,128)(2,1)S(1)}, u32[]{:S(2)}, u32[]{:S(2)}) %collective-permute-start.5) | collective-permute-done | bytes 49184 | tf_op jit(solution)/shard_map/ppermute | solution.py:31
  20.4 8.8 %last.1 = (f32[192,1024]{1,0:T(8,128)S(1)}, f32[8,256]{1,0:T(8,128)S(1)}) custom-call(bf16[240,1024]{1,0:T(8,128)(2,1)S(1)} %get-tuple-element.21.q_ref, bf16[48,1024]{1,0:T(8,128)(2,1)S(1)} %get-tuple-element.22.k_mask_ref, f32[200,1024]{1,0:T(8,128)S(1)} %far.1.far_ref, bf16[192,128]{1,0:T(8,128)(2,1)S(1)} %collective-permute-done.5.from_three, ...), custom_call_target="tpu_custom_call" | custom-call | flops 67108864 | bytes 100000 | tf_op jit(solution)/shard_map/last/pallas_call | solution.py:513
  29.2 0.1 collective-permute-start.8
  29.2 1.6 %collective-permute-start.7 = (f32[8,256]{1,0:T(8,128)S(1)}, f32[8,256]{1,0:T(8,128)S(1)}, u32[]{:S(2)}, u32[]{:S(2)}) collective-permute-start(f32[8,256]{1,0:T(8,128)S(1)} %get-tuple-element.36.refs_0_), channel_id=1, source_target_pairs={{0,2},{1,3},{2,0},{3,1},{4,6},{5,7},{6,4},{7,5},{8,10},{9,11},{10,... | collective-permute-start | bytes 24584 | tf_op jit(solution)/shard_map/ppermute | solution.py:31
  30.8 0.3 collective-permute-start.6
  31.1 1.2 %collective-permute-done.8.refs_3_ = f32[8,256]{1,0:T(8,128)S(1)} collective-permute-done((f32[8,256]{1,0:T(8,128)S(1)}, f32[8,256]{1,0:T(8,128)S(1)}, u32[]{:S(2)}, u32[]{:S(2)}) %collective-permute-start.8) | collective-permute-done | bytes 8224 | tf_op jit(solution)/shard_map/ppermute | solution.py:31
  32.3 0.6 %collective-permute-done.7.refs_2_ = f32[8,256]{1,0:T(8,128)S(1)} collective-permute-done((f32[8,256]{1,0:T(8,128)S(1)}, f32[8,256]{1,0:T(8,128)S(1)}, u32[]{:S(2)}, u32[]{:S(2)}) %collective-permute-start.7) | collective-permute-done | bytes 8224 | tf_op jit(solution)/shard_map/ppermute | solution.py:31
  33.0 0.0 collective-permute-done.6.refs_1_
  33.0 0.9 %norm.1 = bf16[192,1024]{1,0:T(8,128)(2,1)} custom-call(f32[192,1024]{1,0:T(8,128)S(1)} %get-tuple-element.34.att_ref, f32[2,192,128]{2,1,0:T(8,128)S(1)} %get-tuple-element.35.affine_ref, f32[8,256]{1,0:T(8,128)S(1)} %get-tuple-element.36.refs_0_, f32[8,256]{1,0:T(8,128)S(1)} %collective-permute-done.6.refs_1_, ...), custom_call_target="tpu_custom_call" | custom-call | tf_op jit(solution)/shard_map/norm/pallas_call | solution.py:528
  (8 shorter events, 0.0 us)
Async XLA Ops:
  0.0 9.2 %copy-start = (bf16[192,1024]{1,0:T(8,128)(2,1)S(1)}, bf16[192,1024]{1,0:T(8,128)(2,1)}, u32[]{:S(2)}) copy-start(bf16[192,1024]{1,0:T(8,128)(2,1)} %refs_1_.1) | copy-start | bytes 1179652
  0.0 9.2 %copy-start.3 = (f32[192]{0:T(256)S(1)}, f32[192]{0:T(256)}, u32[]{:S(2)}) copy-start(f32[192]{0:T(256)} %param.10) | copy-start | bytes 2308
  0.0 9.2 %copy-start.4 = (f32[192]{0:T(256)S(1)}, f32[192]{0:T(256)}, u32[]{:S(2)}) copy-start(f32[192]{0:T(256)} %param.11) | copy-start | bytes 2308
  0.0 9.2 %copy-start.5 = (s32[8]{0:T(128)S(1)}, s32[8]{0:T(128)}, u32[]{:S(2)}) copy-start(s32[8]{0:T(128)} %lengths_ref.1) | copy-start | bytes 100
  0.0 10.0 %copy-start.2 = (bf16[192,1024]{1,0:T(8,128)(2,1)S(1)}, bf16[192,1024]{1,0:T(8,128)(2,1)}, u32[]{:S(2)}) copy-start(bf16[192,1024]{1,0:T(8,128)(2,1)} %refs_3_.1) | copy-start | bytes 1179652
  2.0 8.0 %copy-start.1 = (bf16[192,1024]{1,0:T(8,128)(2,1)S(1)}, bf16[192,1024]{1,0:T(8,128)(2,1)}, u32[]{:S(2)}) copy-start(bf16[192,1024]{1,0:T(8,128)(2,1)} %refs_2_.1) | copy-start | bytes 1179652
  2.0 10.1 %collective-permute-start.1 = (bf16[384,256]{1,0:T(8,128)(2,1)S(1)}, bf16[384,256]{1,0:T(8,128)(2,1)S(1)}, u32[]{:S(2)}, u32[]{:S(2)}) collective-permute-start(bf16[384,256]{1,0:T(8,128)(2,1)S(1)} %get-tuple-element.24), channel_id=1, source_target_pairs={{0,8},{4,12},{8,0},{12,4},{16,24},{20,28},{24,16},{28,20},{1,9},{5... | collective-permute-start | bytes 589832 | tf_op jit(solution)/shard_map/ppermute | solution.py:31
  5.1 7.0 %collective-permute-start = (bf16[384,256]{1,0:T(8,128)(2,1)S(1)}, bf16[384,256]{1,0:T(8,128)(2,1)S(1)}, u32[]{:S(2)}, u32[]{:S(2)}) collective-permute-start(bf16[384,256]{1,0:T(8,128)(2,1)S(1)} %get-tuple-element.24), channel_id=1, source_target_pairs={{0,4},{4,0},{8,12},{12,8},{16,20},{20,16},{24,28},{28,24},{1,5},{5... | collective-permute-start | bytes 589832 | tf_op jit(solution)/shard_map/ppermute | solution.py:31
  6.6 5.5 %collective-permute-start.2 = (bf16[192,128]{1,0:T(8,128)(2,1)S(1)}, bf16[192,128]{1,0:T(8,128)(2,1)S(1)}, u32[]{:S(2)}, u32[]{:S(2)}) collective-permute-start(bf16[192,128]{1,0:T(8,128)(2,1)S(1)} %get-tuple-element.25), channel_id=1, source_target_pairs={{0,16},{4,20},{8,24},{12,28},{16,0},{20,4},{24,8},{28,12},{1,17},{... | collective-permute-start | bytes 147464 | tf_op jit(solution)/shard_map/ppermute | solution.py:31
  12.1 6.3 %collective-permute-start.3 = (bf16[192,384]{1,0:T(8,128)(2,1)S(1)}, bf16[192,384]{1,0:T(8,128)(2,1)S(1)}, u32[]{:S(2)}, u32[]{:S(2)}) collective-permute-start(bf16[192,384]{1,0:T(8,128)(2,1)S(1)} %get-tuple-element.30), channel_id=1, source_target_pairs={{0,4},{4,0},{8,12},{12,8},{16,20},{20,16},{24,28},{28,24},{1,5},{5... | collective-permute-start | bytes 442376 | tf_op jit(solution)/shard_map/ppermute | solution.py:31
  13.0 5.5 %collective-permute-start.4 = (bf16[192,384]{1,0:T(8,128)(2,1)S(1)}, bf16[192,384]{1,0:T(8,128)(2,1)S(1)}, u32[]{:S(2)}, u32[]{:S(2)}) collective-permute-start(bf16[192,384]{1,0:T(8,128)(2,1)S(1)} %get-tuple-element.31), channel_id=1, source_target_pairs={{0,8},{4,12},{8,0},{12,4},{16,24},{20,28},{24,16},{28,20},{1,9},{5... | collective-permute-start | bytes 442376 | tf_op jit(solution)/shard_map/ppermute | solution.py:31
  15.4 5.0 %collective-permute-start.5 = (bf16[192,128]{1,0:T(8,128)(2,1)S(1)}, bf16[192,128]{1,0:T(8,128)(2,1)S(1)}, u32[]{:S(2)}, u32[]{:S(2)}) collective-permute-start(bf16[192,128]{1,0:T(8,128)(2,1)S(1)} %pass_on.1), channel_id=1, source_target_pairs={{0,12},{4,8},{8,4},{12,0},{16,28},{20,24},{24,20},{28,16},{1,13},{... | collective-permute-start | bytes 147464 | tf_op jit(solution)/shard_map/ppermute | solution.py:31
  29.2 3.2 %collective-permute-start.8 = (f32[8,256]{1,0:T(8,128)S(1)}, f32[8,256]{1,0:T(8,128)S(1)}, u32[]{:S(2)}, u32[]{:S(2)}) collective-permute-start(f32[8,256]{1,0:T(8,128)S(1)} %get-tuple-element.36.refs_0_), channel_id=1, source_target_pairs={{0,3},{1,2},{2,1},{3,0},{4,7},{5,6},{6,5},{7,4},{8,11},{9,10},{10,... | collective-permute-start | bytes 24584 | tf_op jit(solution)/shard_map/ppermute | solution.py:31
  29.2 3.7 %collective-permute-start.7 = (f32[8,256]{1,0:T(8,128)S(1)}, f32[8,256]{1,0:T(8,128)S(1)}, u32[]{:S(2)}, u32[]{:S(2)}) collective-permute-start(f32[8,256]{1,0:T(8,128)S(1)} %get-tuple-element.36.refs_0_), channel_id=1, source_target_pairs={{0,2},{1,3},{2,0},{3,1},{4,6},{5,7},{6,4},{7,5},{8,10},{9,11},{10,... | collective-permute-start | bytes 24584 | tf_op jit(solution)/shard_map/ppermute | solution.py:31
  30.8 2.1 %collective-permute-start.6 = (f32[8,256]{1,0:T(8,128)S(1)}, f32[8,256]{1,0:T(8,128)S(1)}, u32[]{:S(2)}, u32[]{:S(2)}) collective-permute-start(f32[8,256]{1,0:T(8,128)S(1)} %get-tuple-element.36.refs_0_), channel_id=1, source_target_pairs={{0,1},{1,0},{2,3},{3,2},{4,5},{5,4},{6,7},{7,6},{8,9},{9,8},{10,11... | collective-permute-start | bytes 24584 | tf_op jit(solution)/shard_map/ppermute | solution.py:31

commit v4 on v3

--- a/solution.py
+++ b/solution.py
@@ -113,15 +113,10 @@
     sixteenth_ref[...] = jnp.concatenate(results, axis=1).astype(BF16)
 
 
-def relay_kernel(one_ref, two_ref, *refs):
-    beyond, (to_one, to_two) = refs[:-2], refs[-2:]
-    features, width = to_one.shape[0], one_ref.shape[1]
-    to_one[:, :width] = two_ref[features:, :]
-    to_two[:, :width] = one_ref[:features, :]
-    for at, piece in enumerate(beyond):
-        count = piece.shape[1]
-        for out, start in ((to_one, width), (to_two, width)):
-            out[:, start + at * count : start + (at + 1) * count] = piece[...]
+def relay_kernel(two_ref, to_one, to_two):
+    half = to_two.shape[0]
+    to_one[...] = two_ref[half:, :]
+    to_two[...] = two_ref[:half, :]
 
 
 def pass_kernel(*refs):
@@ -130,6 +125,10 @@
     for piece in refs[:-1]:
         out[:, at : at + piece.shape[1]] = piece[...]
         at += piece.shape[1]
+
+
+def diagonal_pair(from_one, from_two):
+    return from_two, from_one
 
 
 def mask_kernel(kinds, distances, lengths_ref, gain_ref, bias_ref, q_ref, q_out, k_mask_out, affine_out, slide_out):
@@ -236,18 +235,30 @@
         out_ref[head] = mixed[: HD + 8]
 
 
-def lay_out(pieces, mask_at, k_mask_ref, k_ref, v_ref):
+def count_of(kind, keys):
+    return keys.shape[1] if kind == 1 else keys.shape[1] // 2 // 4 ** (kind - 2)
+
+
+def with_masks(pieces, mask_at):
+    placed = []
+    for kind, keys, values in pieces:
+        placed.append((kind, keys, values, mask_at))
+        mask_at += count_of(kind, keys)
+    return placed
+
+
+def lay_out(pieces, k_mask_ref, k_ref, v_ref):
     features = HEADS * HD
     at = 0
     beside = []
-    for kind, keys, values in pieces:
-        count = keys.shape[1] if kind == 1 else keys.shape[1] // 2 // 4 ** (kind - 2)
+    for kind, keys, values, mask_at in pieces:
+        count = count_of(kind, keys)
         if kind == 1:
             v_ref[:features, at : at + count] = values[...]
         else:
             half = values.shape[1] // 2
             beside.append(values[:, half : half + count])
-        masks = k_mask_ref[:, mask_at + at : mask_at + at + count]
+        masks = k_mask_ref[:, mask_at : mask_at + count]
         k_ref[at : at + count, :] = jnp.concatenate([keys[:, :count], masks], axis=0).T
         at += count
     if beside:
@@ -281,39 +292,26 @@
     ref[features + i : features + i + 1, :] = total
 
 
-def near_kernel(q_ref, k_mask_ref, local_a, local_b, one_ref, two_ref, out_ref, k_ref, v_ref):
-    lay_out([(1, *halves(one_ref)), (1, *halves(two_ref))], 0, k_mask_ref, k_ref, v_ref)
+def near_pieces(kinds, one_ref, two_ref, direct):
+    pieces = [(1, *halves(one_ref)), (1, *halves(two_ref))]
+    return pieces + [(kind, ref, ref) for kind, ref in zip(kinds, direct)]
+
+
+def last_pieces(kinds, from_one, from_two, from_beyond):
+    width = from_one.shape[1] // 2
+    passed_on = [from_beyond.at[:, at * width : (at + 1) * width] for at in range(len(kinds))]
+    pieces = [(1, *diagonal_pair(from_one, from_two))]
+    return pieces + [(kind, ref, ref) for kind, ref in zip(kinds, passed_on)]
+
+
+def near_kernel(kinds, q_ref, k_mask_ref, local_a, local_c, local_d, one_ref, two_ref, *refs):
+    direct, (out_ref, k_ref, v_ref) = refs[:-3], refs[-3:]
+    pieces = with_masks(near_pieces(kinds, one_ref, two_ref, direct), 0)
+    lay_out(pieces, k_mask_ref, k_ref, v_ref)
     mixed = weigh(k_ref[...], q_ref[...], v_ref[...])
     for i in range(HEADS):
-        ref = (local_a, local_b)[i // 2].at[i % 2]
+        ref = [ref.at[j] for ref in (local_a, local_c, local_d) for j in range(ref.shape[0])][i]
         store_parts(out_ref, i, *with_more(i, ref[:HD, :], ref[HD : HD + 1, :], mixed))
-
-
-def far_kernel(kinds, mask_at, q_ref, k_mask_ref, near_ref, *refs):
-    out_ref, k_ref, v_ref = refs[-3:]
-    pieces = far_pieces(kinds, q_ref.shape[1], *refs[:2], refs[2:-3])
-    lay_out(pieces, mask_at, k_mask_ref, k_ref, v_ref)
-    mixed = weigh(k_ref[...], q_ref[...], v_ref[...])
-    for i in range(HEADS):
-        store_parts(out_ref, i, *with_more(i, *parts_of(near_ref, i), mixed))
-
-
-def far_pieces(kinds, rows, from_one, from_two, rest):
-    width = rows // 4
-    beyond = [
-        ref.at[:, at : at + rows // 8]
-        for ref in (from_one, from_two)
-        for at in range(width, ref.shape[1], rows // 8)
-    ] + list(rest)
-    diagonal = (1, from_two.at[:, :width], from_one.at[:, :width])
-    return [diagonal] + [(kind, ref, ref) for kind, ref in zip(kinds[1:], beyond)]
-
-
-def three_pieces(kinds, rows, from_three):
-    return [
-        (kind, *[from_three.at[:, at * rows // 8 : (at + 1) * rows // 8]] * 2)
-        for at, kind in enumerate(kinds)
-    ]
 
 
 def add_up(head_parts, att_ref, sums_ref):
@@ -330,18 +328,18 @@
         sums_ref[4 + at : 5 + at, :] = squares[:, at * quarter : (at + 1) * quarter]
 
 
-def last_kernel(kinds, mask_at, raw_refs, q_ref, k_mask_ref, far_ref, from_three, *refs):
-    raw, (att_ref, sums_ref, k_three, v_three, k_ref, v_ref) = refs[:raw_refs], refs[raw_refs:]
-    rows = q_ref.shape[1]
-    features = HEADS * HD
-    own = lanes(rows) & 3
-    three = three_pieces(kinds[-(from_three.shape[1] * 8 // rows) :], rows, from_three)
-    lay_out(three, mask_at, k_mask_ref, k_three, v_three)
-    mixed = weigh(k_three[...], q_ref[...], v_three[...])
+def last_kernel(kinds, raw_refs, q_ref, k_mask_ref, near_ref, from_one, from_two, from_beyond, *refs):
+    raw, (att_ref, sums_ref, k_last, v_last, k_ref, v_ref) = refs[:raw_refs], refs[raw_refs:]
+    features = HEADS * HD
+    own = lanes(q_ref.shape[1]) & 3
+    last = last_pieces(kinds, from_one, from_two, from_beyond)
+    last = with_masks(last, k_ref.shape[0] - k_last.shape[0])
+    lay_out(last, k_mask_ref, k_last, v_last)
+    mixed = weigh(k_last[...], q_ref[...], v_last[...])
     parts = []
     least = most = None
     for i in range(HEADS):
-        part, total = with_more(i, *parts_of(far_ref, i), mixed)
+        part, total = with_more(i, *parts_of(near_ref, i), mixed)
         parts.append(part * (1.0 / total))
         least = total if least is None else jnp.minimum(least, total)
         most = total if most is None else jnp.maximum(most, total)
@@ -351,10 +349,10 @@
 
     @pl.when(worst > 0.0)
     def _():
-        slide_ref, queries, keys, values, one_ref, two_ref, from_one, from_two = raw[:8]
-        pieces = [(1, *halves(one_ref)), (1, *halves(two_ref))]
-        pieces += far_pieces(kinds[2:], rows, from_one, from_two, raw[8:]) + three
-        lay_out(pieces, 0, k_mask_ref, k_ref, v_ref)
+        slide_ref, queries, keys, values, one_ref, two_ref = raw[:6]
+        pieces = with_masks(near_pieces(kinds, one_ref, two_ref, raw[6:]), 0) + last
+        pieces.sort(key=lambda piece: piece[0] > 1)
+        lay_out(pieces, k_mask_ref, k_ref, v_ref)
         far_peak, mixed = weigh_with_peak(k_ref[...], q_ref[...], v_ref[...])
         parts = []
         for i in range(HEADS):
@@ -413,20 +411,22 @@
         name="pack",
     )(keys, values)
 
-    beyond = [(partner(own, "seq", m), m) for m in range(spans[2], spans[3], spans[2])]
-    beyond = beyond + [
-        (partner(piece, "seq", m), m ^ d)
-        for m in range(spans[1], spans[2], spans[1])
-        for piece, d in [(own, 0)] + beyond
+    one, two = partner(pair, "seq", 1), partner(pair, "seq", 2)
+    held = [(own, 0)]
+    held += [(partner(own, "seq", m), m) for m in range(spans[2], spans[3], spans[2])]
+    beyond = held[1:] + [
+        (partner(piece, "seq", m ^ side), m ^ side ^ d)
+        for m in range(0, spans[2], spans[1])
+        for side in (0, 1)
+        for piece, d in (held if m else held[1:] * side)
     ]
-    one, two = partner(pair, "seq", 1), partner(pair, "seq", 2)
-    beyond_distances = [d ^ m for m in (1, 2, 0, 3) for _, d in beyond]
-    distances = [1, 2, 3] + beyond_distances
-    kinds = [1, 1, 1] + [2 if d < spans[2] else 3 for d in beyond_distances]
+    beyond_kinds = [2 if d < spans[2] else 3 for _, d in beyond]
+    kinds = [1, 1] + beyond_kinds + [1] + beyond_kinds
+    distances = [1, 2] + [d for _, d in beyond] + [3] + [2 ^ d for _, d in beyond]
     counts = [rows // 4**kind for kind in kinds]
-    three = len(kinds) - len(beyond)
-    near_count, far_count, three_count = sum(counts[:2]), sum(counts[2:three]), sum(counts[three:])
     key_count = sum(counts)
+    near_count = (key_count + counts[0]) // 2
+    last_count = key_count - near_count
 
     mask_rows = -(-(HEADS * slide_lengths.shape[0] + 8) // 16) * 16
     depth = features + mask_rows
@@ -445,84 +445,77 @@
         name="masks",
     )(slide_lengths, norm_gain[None, :], norm_bias[None, :], queries)
 
-    def local(first, work, *operands):
+    def local(first, count, work, *operands):
         return pl.pallas_call(
             functools.partial(local_kernel, first),
-            out_shape=jax.ShapeDtypeStruct((2, HD + 8, rows), F32),
+            out_shape=jax.ShapeDtypeStruct((count, HD + 8, rows), F32),
             in_specs=[VMEM] * 4,
             out_specs=VMEM,
             compiler_params=PARAMS,
-            cost_estimate=cost(work, 10**5),
+            cost_estimate=cost(work, 10**3),
             name="local",
         )(*operands)
 
-    local_a = local(0, 10**9, slides, queries, keys, values)
+    local_a = local(0, 1, 10**9, slides, queries, keys, values)
     beyond_pieces = [piece for piece, _ in beyond]
-    local_a, one, two, beyond_pieces = lax.optimization_barrier((local_a, one, two, beyond_pieces))
-    relayed = jax.ShapeDtypeStruct((features, rows // 4 + rows // 8 * len(beyond)), BF16)
-    passed_on = jax.ShapeDtypeStruct((features, rows // 8 * len(beyond)), BF16)
+    local_a, two = lax.optimization_barrier((local_a, two))
     to_one, to_two = pl.pallas_call(
         relay_kernel,
-        out_shape=(relayed, relayed),
-        in_specs=[VMEM] * (2 + len(beyond)),
+        out_shape=(
+            jax.ShapeDtypeStruct((features, rows // 4), BF16),
+            jax.ShapeDtypeStruct((features, rows // 4), BF16),
+        ),
+        in_specs=[VMEM],
         out_specs=(VMEM,) * 2,
         compiler_params=PARAMS,
         cost_estimate=cost(0, 10**6),
         name="relay",
-    )(one, two, *beyond_pieces)
-    from_one, from_two = partner(to_one, "seq", 1), partner(to_two, "seq", 2)
-    to_three = pl.pallas_call(
+    )(two)
+    from_one, from_two = partner(to_one, "seq", 1), partner(to_two, "seq", 1)
+    held, _ = lax.optimization_barrier((queries, (to_one, to_two)))
+    local_c = local(1, 1, 10**6, slides, held, keys, values)
+    beyond_pieces, local_c = lax.optimization_barrier((beyond_pieces, local_c))
+    to_beyond = pl.pallas_call(
         pass_kernel,
-        out_shape=passed_on,
+        out_shape=jax.ShapeDtypeStruct((features, rows // 8 * len(beyond)), BF16),
         in_specs=[VMEM] * len(beyond),
         out_specs=VMEM,
         compiler_params=PARAMS,
         cost_estimate=cost(0, 10**5),
         name="pass_on",
-    )(*lax.optimization_barrier((beyond_pieces, to_one, to_two))[0])
-    from_three = partner(to_three, "seq", 3)
-    held, _ = lax.optimization_barrier((queries, (to_one, to_two, to_three)))
-    local_b = local(2, 3 * 10**8, slides, held, keys, values)
+    )(*beyond_pieces)
+    from_beyond = partner(to_beyond, "seq", 2)
+    held, _ = lax.optimization_barrier((queries, to_beyond))
+    local_d = local(2, 2, 10**6, slides, held, keys, values)
 
     def scratch(count):
         return [pltpu.VMEM((count, depth), BF16), pltpu.VMEM((features + 16, count), BF16)]
 
     near_part = pl.pallas_call(
-        near_kernel,
+        functools.partial(near_kernel, beyond_kinds),
         out_shape=jax.ShapeDtypeStruct((features + 8, rows), F32),
-        in_specs=[VMEM] * 6,
+        in_specs=[VMEM] * (7 + len(beyond)),
         out_specs=VMEM,
         scratch_shapes=scratch(near_count),
         compiler_params=PARAMS,
-        cost_estimate=cost(2 * rows * near_count * 512, 10**5),
+        cost_estimate=cost(10**6, 10**4),
         name="near",
-    )(own_queries, key_masks, local_a, local_b, one, two)
-
-    far_part = pl.pallas_call(
-        functools.partial(far_kernel, kinds[2:three], near_count),
-        out_shape=jax.ShapeDtypeStruct((features + 8, rows), F32),
-        in_specs=[VMEM] * (5 + len(beyond)),
-        out_specs=VMEM,
-        scratch_shapes=scratch(far_count),
-        compiler_params=PARAMS,
-        cost_estimate=cost(2 * rows * far_count * 512, 10**5),
-        name="far",
-    )(own_queries, key_masks, near_part, from_one, from_two, *beyond_pieces)
-
-    raw = (slides, queries, keys, values, one, two, from_one, from_two, *beyond_pieces)
+    )(own_queries, key_masks, local_a, local_c, local_d, one, two, *beyond_pieces)
+
+    raw = (slides, queries, keys, values, one, two, *beyond_pieces)
     attended, sums = pl.pallas_call(
-        functools.partial(last_kernel, kinds, key_count - three_count, len(raw)),
+        functools.partial(last_kernel, beyond_kinds, len(raw)),
         out_shape=(
             jax.ShapeDtypeStruct((features, rows), F32),
             jax.ShapeDtypeStruct((8, rows // 4), F32),
         ),
-        in_specs=[VMEM] * (4 + len(raw)),
+        in_specs=[VMEM] * (6 + len(raw)),
         out_specs=(VMEM, VMEM),
-        scratch_shapes=scratch(three_count) + scratch(key_count),
+        scratch_shapes=scratch(last_count) + scratch(key_count),
         compiler_params=PARAMS,
-        cost_estimate=cost(2 * rows * three_count * 512, 10**5),
+        cost_estimate=cost(2 * rows * last_count * 512, 10**5),
         name="last",
-    )(own_queries, key_masks, far_part, from_three, *raw)
+    )(own_queries, key_masks, near_part, from_one, from_two, from_beyond, *raw)
 
     all_sums = [sums] + [partner(sums, "head", m) for m in range(1, lax.axis_size("head"))]
     return pl.pallas_call(

time: 34 us -> 33.2 us (0.976)
  waiting for transfers between devices: 3.19 us -> 2.61 us
    ppermute x9 -> x10, waiting for transfers between devices: 3.19 us -> 2.61 us  [partner(): return lax.ppermute(value, axis, pairs)]
    pallas_call x5 -> x4, Pallas kernels: 10.3 us -> 9.82 us  [the longest x1 8.88 us: per_device(): pl.pallas_call(functools.partial(last_kernel, beyond_kinds, len(raw)), ou...]
    pallas_call x2 -> x3, Pallas kernels: 3.95 us -> 4.11 us  [local(): pl.pallas_call(functools.partial(local_kernel, first), out_shape=jax.Shap...]
    ppermute x9 -> x10, starting transfers between devices: 12.7 us -> 12.7 us  [partner(): return lax.ppermute(value, axis, pairs)]
  transfers between devices with their start and end apart: 9 -> 10, of which waited for: 5 -> 4; matrix products, arithmetic and copies ran while one was open for 0% -> 0% of each run, Pallas kernels for 18% -> 18%
where the time goes in v4:
time: 33.2 us; the launch traced here: 33.1 us
  Pallas kernels  17.6 us (53%)
  starting transfers between devices  12.7 us (38%)
  waiting for transfers between devices  2.61 us (8%)
    ppermute x10, starting transfers between devices, partner(): return lax.ppermute(value, axis, pairs)  12.7 us
    pallas_call x1, Pallas kernels, per_device(): pl.pallas_call(functools.partial(last_kernel, beyond_kinds, len(raw)), ou...  8.88 us
    pallas_call x3, Pallas kernels, local(): pl.pallas_call(functools.partial(local_kernel, first), out_shape=jax.Shap...  4.11 us
    ppermute x10, waiting for transfers between devices, partner(): return lax.ppermute(value, axis, pairs)  2.61 us
    pallas_call x1, Pallas kernels, per_device(): pl.pallas_call(pack_kernel, out_shape=(jax.ShapeDtypeStruct((2 * features...  1.94 us
    pallas_call x1, Pallas kernels, per_device(): pl.pallas_call(norm_kernel, out_shape=jax.ShapeDtypeStruct((features, row...  0.92 us
    pallas_call x1, Pallas kernels, per_device(): pl.pallas_call(functools.partial(near_kernel, beyond_kinds), out_shape=ja...  0.9 us
    pallas_call x1, Pallas kernels, per_device(): pl.pallas_call(functools.partial(mask_kernel, kinds, distances), out_shap...  0.8 us
  transfers between devices with their start and end apart: 10, of which 4 were waited for; matrix products, arithmetic and copies ran while one was open for 0% of the time, Pallas kernels for 18%

profile of v4, /device:TPU:0, one launch (start us, length us, event | category | flops | bytes accessed | tf_op | source)
XLA Modules:
  0.0 33.1 jit_solution(10445414316324365368)
XLA Ops:
  0.0 1.9 %pack.1 = (bf16[384,256]{1,0:T(8,128)(2,1)S(1)}, bf16[192,128]{1,0:T(8,128)(2,1)S(1)}) custom-call(bf16[192,1024]{1,0:T(8,128)(2,1)} %refs_2_.1, bf16[192,1024]{1,0:T(8,128)(2,1)} %refs_3_.1), custom_call_target="tpu_custom_call" | custom-call | flops 201326592 | bytes 1000000 | tf_op jit(solution)/shard_map/pack/pallas_call | solution.py:396
  2.0 0.0 copy-start.1
  2.0 3.1 %collective-permute-start = (bf16[384,256]{1,0:T(8,128)(2,1)S(1)}, bf16[384,256]{1,0:T(8,128)(2,1)S(1)}, u32[]{:S(2)}, u32[]{:S(2)}) collective-permute-start(bf16[384,256]{1,0:T(8,128)(2,1)S(1)} %get-tuple-element.25), channel_id=1, source_target_pairs={{0,8},{4,12},{8,0},{12,4},{16,24},{20,28},{24,16},{28,20},{1,9},{5... | collective-permute-start | bytes 589832 | tf_op jit(solution)/shard_map/ppermute | solution.py:31
  5.1 3.5 %collective-permute-start.2 = (bf16[192,128]{1,0:T(8,128)(2,1)S(1)}, bf16[192,128]{1,0:T(8,128)(2,1)S(1)}, u32[]{:S(2)}, u32[]{:S(2)}) collective-permute-start(bf16[192,128]{1,0:T(8,128)(2,1)S(1)} %get-tuple-element.27), channel_id=1, source_target_pairs={{0,20},{4,16},{8,28},{12,24},{16,4},{20,0},{24,12},{28,8},{1,21},{... | collective-permute-start | bytes 147464 | tf_op jit(solution)/shard_map/ppermute | solution.py:31
  8.6 0.3 %collective-permute-start.1 = (bf16[192,128]{1,0:T(8,128)(2,1)S(1)}, bf16[192,128]{1,0:T(8,128)(2,1)S(1)}, u32[]{:S(2)}, u32[]{:S(2)}) collective-permute-start(bf16[192,128]{1,0:T(8,128)(2,1)S(1)} %get-tuple-element.27), channel_id=1, source_target_pairs={{0,16},{4,20},{8,24},{12,28},{16,0},{20,4},{24,8},{28,12},{1,17},{... | collective-permute-start | bytes 147464 | tf_op jit(solution)/shard_map/ppermute | solution.py:31
  8.9 0.5 %collective-permute-start.3 = (bf16[384,256]{1,0:T(8,128)(2,1)S(1)}, bf16[384,256]{1,0:T(8,128)(2,1)S(1)}, u32[]{:S(2)}, u32[]{:S(2)}) collective-permute-start(bf16[384,256]{1,0:T(8,128)(2,1)S(1)} %get-tuple-element.25), channel_id=1, source_target_pairs={{0,4},{4,0},{8,12},{12,8},{16,20},{20,16},{24,28},{28,24},{1,5},{5... | collective-permute-start | bytes 589832 | tf_op jit(solution)/shard_map/ppermute | solution.py:31
  9.5 0.0 copy-done
  9.5 0.0 copy-done.3
  9.5 0.8 %masks.1 = (bf16[240,1024]{1,0:T(8,128)(2,1)S(1)}, bf16[48,1024]{1,0:T(8,128)(2,1)S(1)}, f32[2,192,128]{2,1,0:T(8,128)S(1)}, f32[8,1024]{1,0:T(8,128)S(1)}) custom-call(s32[8]{0:T(128)S(1)} %copy-done.5, f32[1,192]{1,0:T(1,128)S(1)} %bitcast.2, f32[1,192]{1,0:T(1,128)S(1)} %bitcast.3, bf16[192,1024]{1,0:T(8,128)(2,1)S(1)} %copy-done), custom_call_target="tpu_custom_call" | custom-call | flops 100000000 | bytes 1000000 | tf_op jit(solution)/shard_map/masks/pallas_call | solution.py:433
  10.3 0.0 copy-done.2
  10.3 1.1 %local.3.local_a = f32[1,56,1024]{2,1,0:T(8,128)S(1)} custom-call(f32[8,1024]{1,0:T(8,128)S(1)} %get-tuple-element.24.slide_ref.refs_0_, bf16[192,1024]{1,0:T(8,128)(2,1)S(1)} %copy-done, bf16[192,1024]{1,0:T(8,128)(2,1)S(1)} %copy-done.1, bf16[192,1024]{1,0:T(8,128)(2,1)S(1)} %copy-done.2), custom_call_target="tpu_custom_call" | custom-call | flops 1000000000 | bytes 1000 | tf_op jit(solution)/shard_map/local/pallas_call | solution.py:449
  11.4 0.0 collective-permute-done.two_ref.refs_5_
  11.4 1.9 %collective-permute-start.4 = (bf16[192,256]{1,0:T(8,128)(2,1)S(1)}, bf16[192,256]{1,0:T(8,128)(2,1)S(1)}, u32[]{:S(2)}, u32[]{:S(2)}) collective-permute-start(bf16[192,256]{1,0:T(8,128)(2,1)S(1)} %get-tuple-element.29), channel_id=1, source_target_pairs={{0,4},{4,0},{8,12},{12,8},{16,20},{20,16},{24,28},{28,24},{1,5},{5... | collective-permute-start | bytes 294920 | tf_op jit(solution)/shard_map/ppermute | solution.py:31
  13.3 0.2 collective-permute-start.5
  13.5 1.1 %local.4.local_c = f32[1,56,1024]{2,1,0:T(8,128)S(1)} custom-call(f32[8,1024]{1,0:T(8,128)S(1)} %get-tuple-element.24.slide_ref.refs_0_, bf16[192,1024]{1,0:T(8,128)(2,1)S(1)} %copy-done, bf16[192,1024]{1,0:T(8,128)(2,1)S(1)} %copy-done.1, bf16[192,1024]{1,0:T(8,128)(2,1)S(1)} %copy-done.2), custom_call_target="tpu_custom_call" | custom-call | flops 1000000 | bytes 1000 | tf_op jit(solution)/shard_map/local/pallas_call | solution.py:449
  14.6 0.0 collective-permute-done.2.refs_1_.refs_7_
  14.6 0.1 collective-permute-done.1.refs_0_.refs_6_
  14.7 1.2 %collective-permute-start.6 = (bf16[192,256]{1,0:T(8,128)(2,1)S(1)}, bf16[192,256]{1,0:T(8,128)(2,1)S(1)}, u32[]{:S(2)}, u32[]{:S(2)}) collective-permute-start(bf16[192,256]{1,0:T(8,128)(2,1)S(1)} %pass_on.1), channel_id=1, source_target_pairs={{0,8},{4,12},{8,0},{12,4},{16,24},{20,28},{24,16},{28,20},{1,9},{5... | collective-permute-start | bytes 294920 | tf_op jit(solution)/shard_map/ppermute | solution.py:31
  15.9 2.0 %local.5.local_d = f32[2,56,1024]{2,1,0:T(8,128)S(1)} custom-call(f32[8,1024]{1,0:T(8,128)S(1)} %get-tuple-element.24.slide_ref.refs_0_, bf16[192,1024]{1,0:T(8,128)(2,1)S(1)} %copy-done, bf16[192,1024]{1,0:T(8,128)(2,1)S(1)} %copy-done.1, bf16[192,1024]{1,0:T(8,128)(2,1)S(1)} %copy-done.2), custom_call_target="tpu_custom_call" | custom-call | flops 1000000 | bytes 1000 | tf_op jit(solution)/shard_map/local/pallas_call | solution.py:449
  17.9 0.0 collective-permute-done.3.one_ref.refs_4_
  17.9 0.9 %near.1.near_ref = f32[200,1024]{1,0:T(8,128)S(1)} custom-call(bf16[240,1024]{1,0:T(8,128)(2,1)S(1)} %get-tuple-element.22.q_ref, bf16[48,1024]{1,0:T(8,128)(2,1)S(1)} %get-tuple-element.23.k_mask_ref, f32[1,56,1024]{2,1,0:T(8,128)S(1)} %local.3.local_a, f32[1,56,1024]{2,1,0:T(8,128)S(1)} %local.4.local_c, f32[2,56,1024]{2,1,0:T(8,128)S(1)} %local.5.local_d, ...), custom_call_target="tpu_custom_call" | custom-call | flops 1000000 | bytes 10000 | tf_op jit(solution)/shard_map/near/pallas_call | solution.py:494
  18.8 0.0 collective-permute-done.4.from_one
  18.8 0.6 %collective-permute-done.5.from_two = bf16[192,256]{1,0:T(8,128)(2,1)S(1)} collective-permute-done((bf16[192,256]{1,0:T(8,128)(2,1)S(1)}, bf16[192,256]{1,0:T(8,128)(2,1)S(1)}, u32[]{:S(2)}, u32[]{:S(2)}) %collective-permute-start.5) | collective-permute-done | bytes 98336 | tf_op jit(solution)/shard_map/ppermute | solution.py:31
  19.5 0.0 collective-permute-done.6.from_beyond
  19.5 8.9 %last.1 = (f32[192,1024]{1,0:T(8,128)S(1)}, f32[8,256]{1,0:T(8,128)S(1)}) custom-call(bf16[240,1024]{1,0:T(8,128)(2,1)S(1)} %get-tuple-element.22.q_ref, bf16[48,1024]{1,0:T(8,128)(2,1)S(1)} %get-tuple-element.23.k_mask_ref, f32[200,1024]{1,0:T(8,128)S(1)} %near.1.near_ref, bf16[192,256]{1,0:T(8,128)(2,1)S(1)} %collective-permute-done.4.from_one, ...), custom_call_target="tpu_custom_call" | custom-call | flops 402653184 | bytes 100000 | tf_op jit(solution)/shard_map/last/pallas_call | solution.py:506
  28.4 0.1 collective-permute-start.9
  28.4 1.6 %collective-permute-start.8 = (f32[8,256]{1,0:T(8,128)S(1)}, f32[8,256]{1,0:T(8,128)S(1)}, u32[]{:S(2)}, u32[]{:S(2)}) collective-permute-start(f32[8,256]{1,0:T(8,128)S(1)} %get-tuple-element.38.refs_0_), channel_id=1, source_target_pairs={{0,2},{1,3},{2,0},{3,1},{4,6},{5,7},{6,4},{7,5},{8,10},{9,11},{10,... | collective-permute-start | bytes 24584 | tf_op jit(solution)/shard_map/ppermute | solution.py:31
  30.0 0.3 collective-permute-start.7
  30.3 1.2 %collective-permute-done.9.refs_3_ = f32[8,256]{1,0:T(8,128)S(1)} collective-permute-done((f32[8,256]{1,0:T(8,128)S(1)}, f32[8,256]{1,0:T(8,128)S(1)}, u32[]{:S(2)}, u32[]{:S(2)}) %collective-permute-start.9) | collective-permute-done | bytes 8224 | tf_op jit(solution)/shard_map/ppermute | solution.py:31
  31.5 0.6 %collective-permute-done.8.refs_2_ = f32[8,256]{1,0:T(8,128)S(1)} collective-permute-done((f32[8,256]{1,0:T(8,128)S(1)}, f32[8,256]{1,0:T(8,128)S(1)}, u32[]{:S(2)}, u32[]{:S(2)}) %collective-permute-start.8) | collective-permute-done | bytes 8224 | tf_op jit(solution)/shard_map/ppermute | solution.py:31
  32.2 0.0 collective-permute-done.7.refs_1_
  32.2 0.9 %norm.1 = bf16[192,1024]{1,0:T(8,128)(2,1)} custom-call(f32[192,1024]{1,0:T(8,128)S(1)} %get-tuple-element.36.att_ref, f32[2,192,128]{2,1,0:T(8,128)S(1)} %get-tuple-element.37.affine_ref, f32[8,256]{1,0:T(8,128)S(1)} %get-tuple-element.38.refs_0_, f32[8,256]{1,0:T(8,128)S(1)} %collective-permute-done.7.refs_1_, ...), custom_call_target="tpu_custom_call" | custom-call | tf_op jit(solution)/shard_map/norm/pallas_call | solution.py:521
  (10 shorter events, 0.0 us)
Async XLA Ops:
  0.0 9.5 %copy-start = (bf16[192,1024]{1,0:T(8,128)(2,1)S(1)}, bf16[192,1024]{1,0:T(8,128)(2,1)}, u32[]{:S(2)}) copy-start(bf16[192,1024]{1,0:T(8,128)(2,1)} %refs_1_.1) | copy-start | bytes 1179652
  0.0 9.5 %copy-start.3 = (f32[192]{0:T(256)S(1)}, f32[192]{0:T(256)}, u32[]{:S(2)}) copy-start(f32[192]{0:T(256)} %param.10) | copy-start | bytes 2308
  0.0 9.5 %copy-start.4 = (f32[192]{0:T(256)S(1)}, f32[192]{0:T(256)}, u32[]{:S(2)}) copy-start(f32[192]{0:T(256)} %param.11) | copy-start | bytes 2308
  0.0 9.5 %copy-start.5 = (s32[8]{0:T(128)S(1)}, s32[8]{0:T(128)}, u32[]{:S(2)}) copy-start(s32[8]{0:T(128)} %lengths_ref.1) | copy-start | bytes 100
  0.0 10.3 %copy-start.2 = (bf16[192,1024]{1,0:T(8,128)(2,1)S(1)}, bf16[192,1024]{1,0:T(8,128)(2,1)}, u32[]{:S(2)}) copy-start(bf16[192,1024]{1,0:T(8,128)(2,1)} %refs_3_.1) | copy-start | bytes 1179652
  2.0 8.3 %copy-start.1 = (bf16[192,1024]{1,0:T(8,128)(2,1)S(1)}, bf16[192,1024]{1,0:T(8,128)(2,1)}, u32[]{:S(2)}) copy-start(bf16[192,1024]{1,0:T(8,128)(2,1)} %refs_2_.1) | copy-start | bytes 1179652
  2.0 9.4 %collective-permute-start = (bf16[384,256]{1,0:T(8,128)(2,1)S(1)}, bf16[384,256]{1,0:T(8,128)(2,1)S(1)}, u32[]{:S(2)}, u32[]{:S(2)}) collective-permute-start(bf16[384,256]{1,0:T(8,128)(2,1)S(1)} %get-tuple-element.25), channel_id=1, source_target_pairs={{0,8},{4,12},{8,0},{12,4},{16,24},{20,28},{24,16},{28,20},{1,9},{5... | collective-permute-start | bytes 589832 | tf_op jit(solution)/shard_map/ppermute | solution.py:31
  5.1 9.5 %collective-permute-start.2 = (bf16[192,128]{1,0:T(8,128)(2,1)S(1)}, bf16[192,128]{1,0:T(8,128)(2,1)S(1)}, u32[]{:S(2)}, u32[]{:S(2)}) collective-permute-start(bf16[192,128]{1,0:T(8,128)(2,1)S(1)} %get-tuple-element.27), channel_id=1, source_target_pairs={{0,20},{4,16},{8,28},{12,24},{16,4},{20,0},{24,12},{28,8},{1,21},{... | collective-permute-start | bytes 147464 | tf_op jit(solution)/shard_map/ppermute | solution.py:31
  8.6 6.1 %collective-permute-start.1 = (bf16[192,128]{1,0:T(8,128)(2,1)S(1)}, bf16[192,128]{1,0:T(8,128)(2,1)S(1)}, u32[]{:S(2)}, u32[]{:S(2)}) collective-permute-start(bf16[192,128]{1,0:T(8,128)(2,1)S(1)} %get-tuple-element.27), channel_id=1, source_target_pairs={{0,16},{4,20},{8,24},{12,28},{16,0},{20,4},{24,8},{28,12},{1,17},{... | collective-permute-start | bytes 147464 | tf_op jit(solution)/shard_map/ppermute | solution.py:31
  8.9 9.0 %collective-permute-start.3 = (bf16[384,256]{1,0:T(8,128)(2,1)S(1)}, bf16[384,256]{1,0:T(8,128)(2,1)S(1)}, u32[]{:S(2)}, u32[]{:S(2)}) collective-permute-start(bf16[384,256]{1,0:T(8,128)(2,1)S(1)} %get-tuple-element.25), channel_id=1, source_target_pairs={{0,4},{4,0},{8,12},{12,8},{16,20},{20,16},{24,28},{28,24},{1,5},{5... | collective-permute-start | bytes 589832 | tf_op jit(solution)/shard_map/ppermute | solution.py:31
  11.4 7.4 %collective-permute-start.4 = (bf16[192,256]{1,0:T(8,128)(2,1)S(1)}, bf16[192,256]{1,0:T(8,128)(2,1)S(1)}, u32[]{:S(2)}, u32[]{:S(2)}) collective-permute-start(bf16[192,256]{1,0:T(8,128)(2,1)S(1)} %get-tuple-element.29), channel_id=1, source_target_pairs={{0,4},{4,0},{8,12},{12,8},{16,20},{20,16},{24,28},{28,24},{1,5},{5... | collective-permute-start | bytes 294920 | tf_op jit(solution)/shard_map/ppermute | solution.py:31
  13.3 6.2 %collective-permute-start.5 = (bf16[192,256]{1,0:T(8,128)(2,1)S(1)}, bf16[192,256]{1,0:T(8,128)(2,1)S(1)}, u32[]{:S(2)}, u32[]{:S(2)}) collective-permute-start(bf16[192,256]{1,0:T(8,128)(2,1)S(1)} %get-tuple-element.30), channel_id=1, source_target_pairs={{0,4},{4,0},{8,12},{12,8},{16,20},{20,16},{24,28},{28,24},{1,5},{5... | collective-permute-start | bytes 294920 | tf_op jit(solution)/shard_map/ppermute | solution.py:31
  14.7 4.8 %collective-permute-start.6 = (bf16[192,256]{1,0:T(8,128)(2,1)S(1)}, bf16[192,256]{1,0:T(8,128)(2,1)S(1)}, u32[]{:S(2)}, u32[]{:S(2)}) collective-permute-start(bf16[192,256]{1,0:T(8,128)(2,1)S(1)} %pass_on.1), channel_id=1, source_target_pairs={{0,8},{4,12},{8,0},{12,4},{16,24},{20,28},{24,16},{28,20},{1,9},{5... | collective-permute-start | bytes 294920 | tf_op jit(solution)/shard_map/ppermute | solution.py:31
  28.4 3.2 %collective-permute-start.9 = (f32[8,256]{1,0:T(8,128)S(1)}, f32[8,256]{1,0:T(8,128)S(1)}, u32[]{:S(2)}, u32[]{:S(2)}) collective-permute-start(f32[8,256]{1,0:T(8,128)S(1)} %get-tuple-element.38.refs_0_), channel_id=1, source_target_pairs={{0,3},{1,2},{2,1},{3,0},{4,7},{5,6},{6,5},{7,4},{8,11},{9,10},{10,... | collective-permute-start | bytes 24584 | tf_op jit(solution)/shard_map/ppermute | solution.py:31
  28.4 3.7 %collective-permute-start.8 = (f32[8,256]{1,0:T(8,128)S(1)}, f32[8,256]{1,0:T(8,128)S(1)}, u32[]{:S(2)}, u32[]{:S(2)}) collective-permute-start(f32[8,256]{1,0:T(8,128)S(1)} %get-tuple-element.38.refs_0_), channel_id=1, source_target_pairs={{0,2},{1,3},{2,0},{3,1},{4,6},{5,7},{6,4},{7,5},{8,10},{9,11},{10,... | collective-permute-start | bytes 24584 | tf_op jit(solution)/shard_map/ppermute | solution.py:31
  30.0 2.1 %collective-permute-start.7 = (f32[8,256]{1,0:T(8,128)S(1)}, f32[8,256]{1,0:T(8,128)S(1)}, u32[]{:S(2)}, u32[]{:S(2)}) collective-permute-start(f32[8,256]{1,0:T(8,128)S(1)} %get-tuple-element.38.refs_0_), channel_id=1, source_target_pairs={{0,1},{1,0},{2,3},{3,2},{4,5},{5,4},{6,7},{7,6},{8,9},{9,8},{10,11... | collective-permute-start | bytes 24584 | tf_op jit(solution)/shard_map/ppermute | solution.py:31

commit v5 on v4

--- a/solution.py
+++ b/solution.py
@@ -297,11 +297,19 @@
     return pieces + [(kind, ref, ref) for kind, ref in zip(kinds, direct)]
 
 
-def last_pieces(kinds, from_one, from_two, from_beyond):
-    width = from_one.shape[1] // 2
+def last_pieces(kinds, from_beyond):
+    width = from_beyond.shape[1] // len(kinds)
     passed_on = [from_beyond.at[:, at * width : (at + 1) * width] for at in range(len(kinds))]
-    pieces = [(1, *diagonal_pair(from_one, from_two))]
-    return pieces + [(kind, ref, ref) for kind, ref in zip(kinds, passed_on)]
+    return [(kind, ref, ref) for kind, ref in zip(kinds, passed_on)]
+
+
+def far_kernel(mask_at, q_ref, k_mask_ref, near_ref, from_one, from_two, out_ref, k_ref, v_ref):
+    diagonal = [(1, *diagonal_pair(from_one, from_two))]
+    lay_out(with_masks(diagonal, mask_at), k_mask_ref, k_ref, v_ref)
+    mixed = weigh(k_ref[...], q_ref[...], v_ref[...])
+    for i in range(HEADS):
+        part, total = with_more(i, *parts_of(near_ref, i), mixed)
+        store_parts(out_ref, i, part, total)
 
 
 def near_kernel(kinds, q_ref, k_mask_ref, local_a, local_c, local_d, one_ref, two_ref, *refs):
@@ -328,11 +336,11 @@
         sums_ref[4 + at : 5 + at, :] = squares[:, at * quarter : (at + 1) * quarter]
 
 
-def last_kernel(kinds, raw_refs, q_ref, k_mask_ref, near_ref, from_one, from_two, from_beyond, *refs):
+def last_kernel(kinds, raw_refs, q_ref, k_mask_ref, near_ref, from_beyond, *refs):
     raw, (att_ref, sums_ref, k_last, v_last, k_ref, v_ref) = refs[:raw_refs], refs[raw_refs:]
     features = HEADS * HD
     own = lanes(q_ref.shape[1]) & 3
-    last = last_pieces(kinds, from_one, from_two, from_beyond)
+    last = last_pieces(kinds, from_beyond)
     last = with_masks(last, k_ref.shape[0] - k_last.shape[0])
     lay_out(last, k_mask_ref, k_last, v_last)
     mixed = weigh(k_last[...], q_ref[...], v_last[...])
@@ -349,8 +357,9 @@
 
     @pl.when(worst > 0.0)
     def _():
-        slide_ref, queries, keys, values, one_ref, two_ref = raw[:6]
-        pieces = with_masks(near_pieces(kinds, one_ref, two_ref, raw[6:]), 0) + last
+        slide_ref, queries, keys, values, one_ref, two_ref, from_one, from_two = raw[:8]
+        pieces = near_pieces(kinds, one_ref, two_ref, raw[8:])
+        pieces = with_masks(pieces + [(1, *diagonal_pair(from_one, from_two))], 0) + last
         pieces.sort(key=lambda piece: piece[0] > 1)
         lay_out(pieces, k_mask_ref, k_ref, v_ref)
         far_peak, mixed = weigh_with_peak(k_ref[...], q_ref[...], v_ref[...])
@@ -456,7 +465,7 @@
             name="local",
         )(*operands)
 
-    local_a = local(0, 1, 10**9, slides, queries, keys, values)
+    local_a = local(0, 1, 10**8, slides, queries, keys, values)
     beyond_pieces = [piece for piece, _ in beyond]
     local_a, two = lax.optimization_barrier((local_a, two))
     to_one, to_two = pl.pallas_call(
@@ -502,20 +511,31 @@
         name="near",
     )(own_queries, key_masks, local_a, local_c, local_d, one, two, *beyond_pieces)
 
-    raw = (slides, queries, keys, values, one, two, *beyond_pieces)
+    far_part = pl.pallas_call(
+        functools.partial(far_kernel, near_count),
+        out_shape=jax.ShapeDtypeStruct((features + 8, rows), F32),
+        in_specs=[VMEM] * 5,
+        out_specs=VMEM,
+        scratch_shapes=scratch(counts[0]),
+        compiler_params=PARAMS,
+        cost_estimate=cost(10**6, 10**4),
+        name="far",
+    )(own_queries, key_masks, near_part, from_one, from_two)
+
+    raw = (slides, queries, keys, values, one, two, from_one, from_two, *beyond_pieces)
     attended, sums = pl.pallas_call(
         functools.partial(last_kernel, beyond_kinds, len(raw)),
         out_shape=(
             jax.ShapeDtypeStruct((features, rows), F32),
             jax.ShapeDtypeStruct((8, rows // 4), F32),
         ),
-        in_specs=[VMEM] * (6 + len(raw)),
+        in_specs=[VMEM] * (4 + len(raw)),
         out_specs=(VMEM, VMEM),
-        scratch_shapes=scratch(last_count) + scratch(key_count),
+        scratch_shapes=scratch(last_count - counts[0]) + scratch(key_count),
         compiler_params=PARAMS,
         cost_estimate=cost(2 * rows * last_count * 512, 10**5),
         name="last",
-    )(own_queries, key_masks, near_part, from_one, from_two, from_beyond, *raw)
+    )(own_queries, key_masks, far_part, from_beyond, *raw)
 
     all_sums = [sums] + [partner(sums, "head", m) for m in range(1, lax.axis_size("head"))]
     return pl.pallas_call(

time: 33.2 us -> 33.2 us (level)
  Pallas kernels: 17.6 us -> 18.1 us
  starting transfers between devices: 12.7 us -> 12.3 us
    pallas_call x0 -> x1, Pallas kernels: none -> 0.57 us  [per_device(): pl.pallas_call(functools.partial(far_kernel, near_count), out_shape=jax.S...]
    ppermute x10, starting transfers between devices: 12.7 us -> 12.3 us  [partner(): return lax.ppermute(value, axis, pairs)]
  transfers between devices with their start and end apart: 10 -> 10, of which waited for: 4 -> 4; matrix products, arithmetic and copies ran while one was open for 0% -> 0% of each run, Pallas kernels for 18% -> 19%
where the time goes in v5:
time: 33.2 us; the launch traced here: 33 us
  Pallas kernels  18.1 us (55%)
  starting transfers between devices  12.3 us (37%)
  waiting for transfers between devices  2.45 us (7%)
    ppermute x10, starting transfers between devices, partner(): return lax.ppermute(value, axis, pairs)  12.3 us
    pallas_call x1, Pallas kernels, per_device(): pl.pallas_call(functools.partial(last_kernel, beyond_kinds, len(raw)), ou...  8.79 us
    pallas_call x3, Pallas kernels, local(): pl.pallas_call(functools.partial(local_kernel, first), out_shape=jax.Shap...  4.11 us
    ppermute x10, waiting for transfers between devices, partner(): return lax.ppermute(value, axis, pairs)  2.45 us
    pallas_call x1, Pallas kernels, per_device(): pl.pallas_call(pack_kernel, out_shape=(jax.ShapeDtypeStruct((2 * features...  1.94 us
    pallas_call x1, Pallas kernels, per_device(): pl.pallas_call(norm_kernel, out_shape=jax.ShapeDtypeStruct((features, row...  0.92 us
    pallas_call x1, Pallas kernels, per_device(): pl.pallas_call(functools.partial(near_kernel, beyond_kinds), out_shape=ja...  0.9 us
    pallas_call x1, Pallas kernels, per_device(): pl.pallas_call(functools.partial(mask_kernel, kinds, distances), out_shap...  0.8 us
  transfers between devices with their start and end apart: 10, of which 4 were waited for; matrix products, arithmetic and copies ran while one was open for 0% of the time, Pallas kernels for 19%

profile of v5, /device:TPU:0, one launch (start us, length us, event | category | flops | bytes accessed | tf_op | source)
XLA Modules:
  0.0 33.0 jit_solution(5324837363828040732)
XLA Ops:
  0.0 1.9 %pack.1 = (bf16[384,256]{1,0:T(8,128)(2,1)S(1)}, bf16[192,128]{1,0:T(8,128)(2,1)S(1)}) custom-call(bf16[192,1024]{1,0:T(8,128)(2,1)} %refs_2_.1, bf16[192,1024]{1,0:T(8,128)(2,1)} %refs_3_.1), custom_call_target="tpu_custom_call" | custom-call | flops 201326592 | bytes 1000000 | tf_op jit(solution)/shard_map/pack/pallas_call | solution.py:405
  2.0 0.0 copy-start.1
  2.0 3.1 %collective-permute-start = (bf16[384,256]{1,0:T(8,128)(2,1)S(1)}, bf16[384,256]{1,0:T(8,128)(2,1)S(1)}, u32[]{:S(2)}, u32[]{:S(2)}) collective-permute-start(bf16[384,256]{1,0:T(8,128)(2,1)S(1)} %get-tuple-element.25), channel_id=1, source_target_pairs={{0,8},{4,12},{8,0},{12,4},{16,24},{20,28},{24,16},{28,20},{1,9},{5... | collective-permute-start | bytes 589832 | tf_op jit(solution)/shard_map/ppermute | solution.py:31
  5.1 1.5 %collective-permute-start.3 = (bf16[384,256]{1,0:T(8,128)(2,1)S(1)}, bf16[384,256]{1,0:T(8,128)(2,1)S(1)}, u32[]{:S(2)}, u32[]{:S(2)}) collective-permute-start(bf16[384,256]{1,0:T(8,128)(2,1)S(1)} %get-tuple-element.25), channel_id=1, source_target_pairs={{0,4},{4,0},{8,12},{12,8},{16,20},{20,16},{24,28},{28,24},{1,5},{5... | collective-permute-start | bytes 589832 | tf_op jit(solution)/shard_map/ppermute | solution.py:31
  6.6 2.6 %collective-permute-start.2 = (bf16[192,128]{1,0:T(8,128)(2,1)S(1)}, bf16[192,128]{1,0:T(8,128)(2,1)S(1)}, u32[]{:S(2)}, u32[]{:S(2)}) collective-permute-start(bf16[192,128]{1,0:T(8,128)(2,1)S(1)} %get-tuple-element.27), channel_id=1, source_target_pairs={{0,20},{4,16},{8,28},{12,24},{16,4},{20,0},{24,12},{28,8},{1,21},{... | collective-permute-start | bytes 147464 | tf_op jit(solution)/shard_map/ppermute | solution.py:31
  9.1 0.3 %collective-permute-start.1 = (bf16[192,128]{1,0:T(8,128)(2,1)S(1)}, bf16[192,128]{1,0:T(8,128)(2,1)S(1)}, u32[]{:S(2)}, u32[]{:S(2)}) collective-permute-start(bf16[192,128]{1,0:T(8,128)(2,1)S(1)} %get-tuple-element.27), channel_id=1, source_target_pairs={{0,16},{4,20},{8,24},{12,28},{16,0},{20,4},{24,8},{28,12},{1,17},{... | collective-permute-start | bytes 147464 | tf_op jit(solution)/shard_map/ppermute | solution.py:31
  9.5 0.0 copy-done
  9.5 0.8 %masks.1 = (bf16[240,1024]{1,0:T(8,128)(2,1)S(1)}, bf16[48,1024]{1,0:T(8,128)(2,1)S(1)}, f32[2,192,128]{2,1,0:T(8,128)S(1)}, f32[8,1024]{1,0:T(8,128)S(1)}) custom-call(s32[8]{0:T(128)S(1)} %copy-done.5, f32[1,192]{1,0:T(1,128)S(1)} %bitcast.2, f32[1,192]{1,0:T(1,128)S(1)} %bitcast.3, bf16[192,1024]{1,0:T(8,128)(2,1)S(1)} %copy-done), custom_call_target="tpu_custom_call" | custom-call | flops 100000000 | bytes 1000000 | tf_op jit(solution)/shard_map/masks/pallas_call | solution.py:442
  10.3 0.0 copy-done.2
  10.3 1.1 %local.3.local_a = f32[1,56,1024]{2,1,0:T(8,128)S(1)} custom-call(f32[8,1024]{1,0:T(8,128)S(1)} %get-tuple-element.24.slide_ref.refs_0_, bf16[192,1024]{1,0:T(8,128)(2,1)S(1)} %copy-done, bf16[192,1024]{1,0:T(8,128)(2,1)S(1)} %copy-done.1, bf16[192,1024]{1,0:T(8,128)(2,1)S(1)} %copy-done.2), custom_call_target="tpu_custom_call" | custom-call | flops 100000000 | bytes 1000 | tf_op jit(solution)/shard_map/local/pallas_call | solution.py:458
  11.4 0.0 collective-permute-done.two_ref.refs_5_
  11.4 1.6 %collective-permute-start.4 = (bf16[192,256]{1,0:T(8,128)(2,1)S(1)}, bf16[192,256]{1,0:T(8,128)(2,1)S(1)}, u32[]{:S(2)}, u32[]{:S(2)}) collective-permute-start(bf16[192,256]{1,0:T(8,128)(2,1)S(1)} %get-tuple-element.29), channel_id=1, source_target_pairs={{0,4},{4,0},{8,12},{12,8},{16,20},{20,16},{24,28},{28,24},{1,5},{5... | collective-permute-start | bytes 294920 | tf_op jit(solution)/shard_map/ppermute | solution.py:31
  12.9 0.5 %collective-permute-start.5 = (bf16[192,256]{1,0:T(8,128)(2,1)S(1)}, bf16[192,256]{1,0:T(8,128)(2,1)S(1)}, u32[]{:S(2)}, u32[]{:S(2)}) collective-permute-start(bf16[192,256]{1,0:T(8,128)(2,1)S(1)} %get-tuple-element.30), channel_id=1, source_target_pairs={{0,4},{4,0},{8,12},{12,8},{16,20},{20,16},{24,28},{28,24},{1,5},{5... | collective-permute-start | bytes 294920 | tf_op jit(solution)/shard_map/ppermute | solution.py:31
  13.5 1.1 %local.4.local_c = f32[1,56,1024]{2,1,0:T(8,128)S(1)} custom-call(f32[8,1024]{1,0:T(8,128)S(1)} %get-tuple-element.24.slide_ref.refs_0_, bf16[192,1024]{1,0:T(8,128)(2,1)S(1)} %copy-done, bf16[192,1024]{1,0:T(8,128)(2,1)S(1)} %copy-done.1, bf16[192,1024]{1,0:T(8,128)(2,1)S(1)} %copy-done.2), custom_call_target="tpu_custom_call" | custom-call | flops 1000000 | bytes 1000 | tf_op jit(solution)/shard_map/local/pallas_call | solution.py:458
  14.6 0.0 collective-permute-done.2.refs_1_.refs_9_
  14.6 0.2 collective-permute-done.1.refs_0_.refs_8_
  14.8 0.8 %collective-permute-start.6 = (bf16[192,256]{1,0:T(8,128)(2,1)S(1)}, bf16[192,256]{1,0:T(8,128)(2,1)S(1)}, u32[]{:S(2)}, u32[]{:S(2)}) collective-permute-start(bf16[192,256]{1,0:T(8,128)(2,1)S(1)} %pass_on.1), channel_id=1, source_target_pairs={{0,8},{4,12},{8,0},{12,4},{16,24},{20,28},{24,16},{28,20},{1,9},{5... | collective-permute-start | bytes 294920 | tf_op jit(solution)/shard_map/ppermute | solution.py:31
  15.7 2.0 %local.5.local_d = f32[2,56,1024]{2,1,0:T(8,128)S(1)} custom-call(f32[8,1024]{1,0:T(8,128)S(1)} %get-tuple-element.24.slide_ref.refs_0_, bf16[192,1024]{1,0:T(8,128)(2,1)S(1)} %copy-done, bf16[192,1024]{1,0:T(8,128)(2,1)S(1)} %copy-done.1, bf16[192,1024]{1,0:T(8,128)(2,1)S(1)} %copy-done.2), custom_call_target="tpu_custom_call" | custom-call | flops 1000000 | bytes 1000 | tf_op jit(solution)/shard_map/local/pallas_call | solution.py:458
  17.7 0.0 collective-permute-done.3.one_ref.refs_4_
  17.7 0.9 %near.1.near_ref = f32[200,1024]{1,0:T(8,128)S(1)} custom-call(bf16[240,1024]{1,0:T(8,128)(2,1)S(1)} %get-tuple-element.22.q_ref, bf16[48,1024]{1,0:T(8,128)(2,1)S(1)} %get-tuple-element.23.k_mask_ref, f32[1,56,1024]{2,1,0:T(8,128)S(1)} %local.3.local_a, f32[1,56,1024]{2,1,0:T(8,128)S(1)} %local.4.local_c, f32[2,56,1024]{2,1,0:T(8,128)S(1)} %local.5.local_d, ...), custom_call_target="tpu_custom_call" | custom-call | flops 1000000 | bytes 10000 | tf_op jit(solution)/shard_map/near/pallas_call | solution.py:503
  18.6 0.0 collective-permute-done.4.from_one.refs_6_
  18.6 0.0 collective-permute-done.5.from_two.refs_7_
  18.6 0.6 %far.1.near_ref = f32[200,1024]{1,0:T(8,128)S(1)} custom-call(bf16[240,1024]{1,0:T(8,128)(2,1)S(1)} %get-tuple-element.22.q_ref, bf16[48,1024]{1,0:T(8,128)(2,1)S(1)} %get-tuple-element.23.k_mask_ref, f32[200,1024]{1,0:T(8,128)S(1)} %near.1.near_ref, bf16[192,256]{1,0:T(8,128)(2,1)S(1)} %collective-permute-done.4.from_one.refs_6_, ...), custom_call_target="tpu_custom_call" | custom-call | flops 1000000 | bytes 10000 | tf_op jit(solution)/shard_map/far/pallas_call | solution.py:514
  19.2 0.3 %collective-permute-done.6.from_beyond = bf16[192,256]{1,0:T(8,128)(2,1)S(1)} collective-permute-done((bf16[192,256]{1,0:T(8,128)(2,1)S(1)}, bf16[192,256]{1,0:T(8,128)(2,1)S(1)}, u32[]{:S(2)}, u32[]{:S(2)}) %collective-permute-start.6) | collective-permute-done | bytes 98336 | tf_op jit(solution)/shard_map/ppermute | solution.py:31
  19.5 8.8 %last.1 = (f32[192,1024]{1,0:T(8,128)S(1)}, f32[8,256]{1,0:T(8,128)S(1)}) custom-call(bf16[240,1024]{1,0:T(8,128)(2,1)S(1)} %get-tuple-element.22.q_ref, bf16[48,1024]{1,0:T(8,128)(2,1)S(1)} %get-tuple-element.23.k_mask_ref, f32[200,1024]{1,0:T(8,128)S(1)} %far.1.near_ref, bf16[192,256]{1,0:T(8,128)(2,1)S(1)} %collective-permute-done.6.from_beyond, ...), custom_call_target="tpu_custom_call" | custom-call | flops 402653184 | bytes 100000 | tf_op jit(solution)/shard_map/last/pallas_call | solution.py:526
  28.3 0.1 collective-permute-start.9
  28.4 1.6 %collective-permute-start.8 = (f32[8,256]{1,0:T(8,128)S(1)}, f32[8,256]{1,0:T(8,128)S(1)}, u32[]{:S(2)}, u32[]{:S(2)}) collective-permute-start(f32[8,256]{1,0:T(8,128)S(1)} %get-tuple-element.38.refs_0_), channel_id=1, source_target_pairs={{0,2},{1,3},{2,0},{3,1},{4,6},{5,7},{6,4},{7,5},{8,10},{9,11},{10,... | collective-permute-start | bytes 24584 | tf_op jit(solution)/shard_map/ppermute | solution.py:31
  29.9 0.3 collective-permute-start.7
  30.2 1.2 %collective-permute-done.9.refs_3_ = f32[8,256]{1,0:T(8,128)S(1)} collective-permute-done((f32[8,256]{1,0:T(8,128)S(1)}, f32[8,256]{1,0:T(8,128)S(1)}, u32[]{:S(2)}, u32[]{:S(2)}) %collective-permute-start.9) | collective-permute-done | bytes 8224 | tf_op jit(solution)/shard_map/ppermute | solution.py:31
  31.5 0.6 %collective-permute-done.8.refs_2_ = f32[8,256]{1,0:T(8,128)S(1)} collective-permute-done((f32[8,256]{1,0:T(8,128)S(1)}, f32[8,256]{1,0:T(8,128)S(1)}, u32[]{:S(2)}, u32[]{:S(2)}) %collective-permute-start.8) | collective-permute-done | bytes 8224 | tf_op jit(solution)/shard_map/ppermute | solution.py:31
  32.1 0.0 collective-permute-done.7.refs_1_
  32.1 0.9 %norm.1 = bf16[192,1024]{1,0:T(8,128)(2,1)} custom-call(f32[192,1024]{1,0:T(8,128)S(1)} %get-tuple-element.36.att_ref, f32[2,192,128]{2,1,0:T(8,128)S(1)} %get-tuple-element.37.affine_ref, f32[8,256]{1,0:T(8,128)S(1)} %get-tuple-element.38.refs_0_, f32[8,256]{1,0:T(8,128)S(1)} %collective-permute-done.7.refs_1_, ...), custom_call_target="tpu_custom_call" | custom-call | tf_op jit(solution)/shard_map/norm/pallas_call | solution.py:541
  (11 shorter events, 0.0 us)
Async XLA Ops:
  0.0 9.5 %copy-start = (bf16[192,1024]{1,0:T(8,128)(2,1)S(1)}, bf16[192,1024]{1,0:T(8,128)(2,1)}, u32[]{:S(2)}) copy-start(bf16[192,1024]{1,0:T(8,128)(2,1)} %refs_1_.1) | copy-start | bytes 1179652
  0.0 9.5 %copy-start.3 = (f32[192]{0:T(256)S(1)}, f32[192]{0:T(256)}, u32[]{:S(2)}) copy-start(f32[192]{0:T(256)} %param.10) | copy-start | bytes 2308
  0.0 9.5 %copy-start.4 = (f32[192]{0:T(256)S(1)}, f32[192]{0:T(256)}, u32[]{:S(2)}) copy-start(f32[192]{0:T(256)} %param.11) | copy-start | bytes 2308
  0.0 9.5 %copy-start.5 = (s32[8]{0:T(128)S(1)}, s32[8]{0:T(128)}, u32[]{:S(2)}) copy-start(s32[8]{0:T(128)} %lengths_ref.1) | copy-start | bytes 100
  0.0 10.3 %copy-start.2 = (bf16[192,1024]{1,0:T(8,128)(2,1)S(1)}, bf16[192,1024]{1,0:T(8,128)(2,1)}, u32[]{:S(2)}) copy-start(bf16[192,1024]{1,0:T(8,128)(2,1)} %refs_3_.1) | copy-start | bytes 1179652
  2.0 8.3 %copy-start.1 = (bf16[192,1024]{1,0:T(8,128)(2,1)S(1)}, bf16[192,1024]{1,0:T(8,128)(2,1)}, u32[]{:S(2)}) copy-start(bf16[192,1024]{1,0:T(8,128)(2,1)} %refs_2_.1) | copy-start | bytes 1179652
  2.0 9.4 %collective-permute-start = (bf16[384,256]{1,0:T(8,128)(2,1)S(1)}, bf16[384,256]{1,0:T(8,128)(2,1)S(1)}, u32[]{:S(2)}, u32[]{:S(2)}) collective-permute-start(bf16[384,256]{1,0:T(8,128)(2,1)S(1)} %get-tuple-element.25), channel_id=1, source_target_pairs={{0,8},{4,12},{8,0},{12,4},{16,24},{20,28},{24,16},{28,20},{1,9},{5... | collective-permute-start | bytes 589832 | tf_op jit(solution)/shard_map/ppermute | solution.py:31
  5.1 12.6 %collective-permute-start.3 = (bf16[384,256]{1,0:T(8,128)(2,1)S(1)}, bf16[384,256]{1,0:T(8,128)(2,1)S(1)}, u32[]{:S(2)}, u32[]{:S(2)}) collective-permute-start(bf16[384,256]{1,0:T(8,128)(2,1)S(1)} %get-tuple-element.25), channel_id=1, source_target_pairs={{0,4},{4,0},{8,12},{12,8},{16,20},{20,16},{24,28},{28,24},{1,5},{5... | collective-permute-start | bytes 589832 | tf_op jit(solution)/shard_map/ppermute | solution.py:31
  6.6 8.0 %collective-permute-start.2 = (bf16[192,128]{1,0:T(8,128)(2,1)S(1)}, bf16[192,128]{1,0:T(8,128)(2,1)S(1)}, u32[]{:S(2)}, u32[]{:S(2)}) collective-permute-start(bf16[192,128]{1,0:T(8,128)(2,1)S(1)} %get-tuple-element.27), channel_id=1, source_target_pairs={{0,20},{4,16},{8,28},{12,24},{16,4},{20,0},{24,12},{28,8},{1,21},{... | collective-permute-start | bytes 147464 | tf_op jit(solution)/shard_map/ppermute | solution.py:31
  9.1 5.7 %collective-permute-start.1 = (bf16[192,128]{1,0:T(8,128)(2,1)S(1)}, bf16[192,128]{1,0:T(8,128)(2,1)S(1)}, u32[]{:S(2)}, u32[]{:S(2)}) collective-permute-start(bf16[192,128]{1,0:T(8,128)(2,1)S(1)} %get-tuple-element.27), channel_id=1, source_target_pairs={{0,16},{4,20},{8,24},{12,28},{16,0},{20,4},{24,8},{28,12},{1,17},{... | collective-permute-start | bytes 147464 | tf_op jit(solution)/shard_map/ppermute | solution.py:31
  11.4 7.2 %collective-permute-start.4 = (bf16[192,256]{1,0:T(8,128)(2,1)S(1)}, bf16[192,256]{1,0:T(8,128)(2,1)S(1)}, u32[]{:S(2)}, u32[]{:S(2)}) collective-permute-start(bf16[192,256]{1,0:T(8,128)(2,1)S(1)} %get-tuple-element.29), channel_id=1, source_target_pairs={{0,4},{4,0},{8,12},{12,8},{16,20},{20,16},{24,28},{28,24},{1,5},{5... | collective-permute-start | bytes 294920 | tf_op jit(solution)/shard_map/ppermute | solution.py:31
  12.9 5.6 %collective-permute-start.5 = (bf16[192,256]{1,0:T(8,128)(2,1)S(1)}, bf16[192,256]{1,0:T(8,128)(2,1)S(1)}, u32[]{:S(2)}, u32[]{:S(2)}) collective-permute-start(bf16[192,256]{1,0:T(8,128)(2,1)S(1)} %get-tuple-element.30), channel_id=1, source_target_pairs={{0,4},{4,0},{8,12},{12,8},{16,20},{20,16},{24,28},{28,24},{1,5},{5... | collective-permute-start | bytes 294920 | tf_op jit(solution)/shard_map/ppermute | solution.py:31
  14.8 4.7 %collective-permute-start.6 = (bf16[192,256]{1,0:T(8,128)(2,1)S(1)}, bf16[192,256]{1,0:T(8,128)(2,1)S(1)}, u32[]{:S(2)}, u32[]{:S(2)}) collective-permute-start(bf16[192,256]{1,0:T(8,128)(2,1)S(1)} %pass_on.1), channel_id=1, source_target_pairs={{0,8},{4,12},{8,0},{12,4},{16,24},{20,28},{24,16},{28,20},{1,9},{5... | collective-permute-start | bytes 294920 | tf_op jit(solution)/shard_map/ppermute | solution.py:31
  28.3 3.2 %collective-permute-start.9 = (f32[8,256]{1,0:T(8,128)S(1)}, f32[8,256]{1,0:T(8,128)S(1)}, u32[]{:S(2)}, u32[]{:S(2)}) collective-permute-start(f32[8,256]{1,0:T(8,128)S(1)} %get-tuple-element.38.refs_0_), channel_id=1, source_target_pairs={{0,3},{1,2},{2,1},{3,0},{4,7},{5,6},{6,5},{7,4},{8,11},{9,10},{10,... | collective-permute-start | bytes 24584 | tf_op jit(solution)/shard_map/ppermute | solution.py:31
  28.4 3.7 %collective-permute-start.8 = (f32[8,256]{1,0:T(8,128)S(1)}, f32[8,256]{1,0:T(8,128)S(1)}, u32[]{:S(2)}, u32[]{:S(2)}) collective-permute-start(f32[8,256]{1,0:T(8,128)S(1)} %get-tuple-element.38.refs_0_), channel_id=1, source_target_pairs={{0,2},{1,3},{2,0},{3,1},{4,6},{5,7},{6,4},{7,5},{8,10},{9,11},{10,... | collective-permute-start | bytes 24584 | tf_op jit(solution)/shard_map/ppermute | solution.py:31
  29.9 2.2 %collective-permute-start.7 = (f32[8,256]{1,0:T(8,128)S(1)}, f32[8,256]{1,0:T(8,128)S(1)}, u32[]{:S(2)}, u32[]{:S(2)}) collective-permute-start(f32[8,256]{1,0:T(8,128)S(1)} %get-tuple-element.38.refs_0_), channel_id=1, source_target_pairs={{0,1},{1,0},{2,3},{3,2},{4,5},{5,4},{6,7},{7,6},{8,9},{9,8},{10,11... | collective-permute-start | bytes 24584 | tf_op jit(solution)/shard_map/ppermute | solution.py:31

commit v6 on v5

--- a/solution.py
+++ b/solution.py
@@ -344,16 +344,11 @@
     last = with_masks(last, k_ref.shape[0] - k_last.shape[0])
     lay_out(last, k_mask_ref, k_last, v_last)
     mixed = weigh(k_last[...], q_ref[...], v_last[...])
-    parts = []
-    least = most = None
-    for i in range(HEADS):
-        part, total = with_more(i, *parts_of(near_ref, i), mixed)
-        parts.append(part * (1.0 / total))
-        least = total if least is None else jnp.minimum(least, total)
-        most = total if most is None else jnp.maximum(most, total)
-    add_up(parts, att_ref, sums_ref)
-    fine = (least >= LEAST) & (most <= MOST)
-    worst = jnp.max(jnp.where(fine, 0.0, 1.0))
+    sets = [with_more(i, *parts_of(near_ref, i), mixed) for i in range(HEADS)]
+    totals = [total for _, total in sets]
+    least, most = functools.reduce(jnp.minimum, totals), functools.reduce(jnp.maximum, totals)
+    worst = jnp.max(jnp.where((least >= LEAST) & (most <= MOST), 0.0, 1.0))
+    add_up([part * (1.0 / total) for part, total in sets], att_ref, sums_ref)
 
     @pl.when(worst > 0.0)
     def _():

time: 33.2 us -> 33.2 us (level)
  no operation moved by 1% of the time
where the time goes in v6:
time: 33.2 us; the launch traced here: 33 us
  Pallas kernels  18.1 us (55%)
  starting transfers between devices  12.3 us (37%)
  waiting for transfers between devices  2.45 us (7%)
    ppermute x10, starting transfers between devices, partner(): return lax.ppermute(value, axis, pairs)  12.3 us
    pallas_call x1, Pallas kernels, per_device(): pl.pallas_call(functools.partial(last_kernel, beyond_kinds, len(raw)), ou...  8.78 us
    pallas_call x3, Pallas kernels, local(): pl.pallas_call(functools.partial(local_kernel, first), out_shape=jax.Shap...  4.11 us
    ppermute x10, waiting for transfers between devices, partner(): return lax.ppermute(value, axis, pairs)  2.45 us
    pallas_call x1, Pallas kernels, per_device(): pl.pallas_call(pack_kernel, out_shape=(jax.ShapeDtypeStruct((2 * features...  1.94 us
    pallas_call x1, Pallas kernels, per_device(): pl.pallas_call(norm_kernel, out_shape=jax.ShapeDtypeStruct((features, row...  0.92 us
    pallas_call x1, Pallas kernels, per_device(): pl.pallas_call(functools.partial(near_kernel, beyond_kinds), out_shape=ja...  0.9 us
    pallas_call x1, Pallas kernels, per_device(): pl.pallas_call(functools.partial(mask_kernel, kinds, distances), out_shap...  0.8 us
  transfers between devices with their start and end apart: 10, of which 4 were waited for; matrix products, arithmetic and copies ran while one was open for 0% of the time, Pallas kernels for 19%

profile of v6, /device:TPU:0, one launch (start us, length us, event | category | flops | bytes accessed | tf_op | source)
XLA Modules:
  0.0 33.0 jit_solution(7741134684517865678)
XLA Ops:
  0.0 1.9 %pack.1 = (bf16[384,256]{1,0:T(8,128)(2,1)S(1)}, bf16[192,128]{1,0:T(8,128)(2,1)S(1)}) custom-call(bf16[192,1024]{1,0:T(8,128)(2,1)} %refs_2_.1, bf16[192,1024]{1,0:T(8,128)(2,1)} %refs_3_.1), custom_call_target="tpu_custom_call" | custom-call | flops 201326592 | bytes 1000000 | tf_op jit(solution)/shard_map/pack/pallas_call | solution.py:400
  2.0 0.0 copy-start.1
  2.0 3.1 %collective-permute-start = (bf16[384,256]{1,0:T(8,128)(2,1)S(1)}, bf16[384,256]{1,0:T(8,128)(2,1)S(1)}, u32[]{:S(2)}, u32[]{:S(2)}) collective-permute-start(bf16[384,256]{1,0:T(8,128)(2,1)S(1)} %get-tuple-element.25), channel_id=1, source_target_pairs={{0,8},{4,12},{8,0},{12,4},{16,24},{20,28},{24,16},{28,20},{1,9},{5... | collective-permute-start | bytes 589832 | tf_op jit(solution)/shard_map/ppermute | solution.py:31
  5.1 1.5 %collective-permute-start.3 = (bf16[384,256]{1,0:T(8,128)(2,1)S(1)}, bf16[384,256]{1,0:T(8,128)(2,1)S(1)}, u32[]{:S(2)}, u32[]{:S(2)}) collective-permute-start(bf16[384,256]{1,0:T(8,128)(2,1)S(1)} %get-tuple-element.25), channel_id=1, source_target_pairs={{0,4},{4,0},{8,12},{12,8},{16,20},{20,16},{24,28},{28,24},{1,5},{5... | collective-permute-start | bytes 589832 | tf_op jit(solution)/shard_map/ppermute | solution.py:31
  6.6 2.6 %collective-permute-start.2 = (bf16[192,128]{1,0:T(8,128)(2,1)S(1)}, bf16[192,128]{1,0:T(8,128)(2,1)S(1)}, u32[]{:S(2)}, u32[]{:S(2)}) collective-permute-start(bf16[192,128]{1,0:T(8,128)(2,1)S(1)} %get-tuple-element.27), channel_id=1, source_target_pairs={{0,20},{4,16},{8,28},{12,24},{16,4},{20,0},{24,12},{28,8},{1,21},{... | collective-permute-start | bytes 147464 | tf_op jit(solution)/shard_map/ppermute | solution.py:31
  9.1 0.3 %collective-permute-start.1 = (bf16[192,128]{1,0:T(8,128)(2,1)S(1)}, bf16[192,128]{1,0:T(8,128)(2,1)S(1)}, u32[]{:S(2)}, u32[]{:S(2)}) collective-permute-start(bf16[192,128]{1,0:T(8,128)(2,1)S(1)} %get-tuple-element.27), channel_id=1, source_target_pairs={{0,16},{4,20},{8,24},{12,28},{16,0},{20,4},{24,8},{28,12},{1,17},{... | collective-permute-start | bytes 147464 | tf_op jit(solution)/shard_map/ppermute | solution.py:31
  9.5 0.0 copy-done
  9.5 0.0 copy-done.4
  9.5 0.8 %masks.1 = (bf16[240,1024]{1,0:T(8,128)(2,1)S(1)}, bf16[48,1024]{1,0:T(8,128)(2,1)S(1)}, f32[2,192,128]{2,1,0:T(8,128)S(1)}, f32[8,1024]{1,0:T(8,128)S(1)}) custom-call(s32[8]{0:T(128)S(1)} %copy-done.5, f32[1,192]{1,0:T(1,128)S(1)} %bitcast.2, f32[1,192]{1,0:T(1,128)S(1)} %bitcast.3, bf16[192,1024]{1,0:T(8,128)(2,1)S(1)} %copy-done), custom_call_target="tpu_custom_call" | custom-call | flops 100000000 | bytes 1000000 | tf_op jit(solution)/shard_map/masks/pallas_call | solution.py:437
  10.3 1.1 %local.3.local_a = f32[1,56,1024]{2,1,0:T(8,128)S(1)} custom-call(f32[8,1024]{1,0:T(8,128)S(1)} %get-tuple-element.24.slide_ref.refs_0_, bf16[192,1024]{1,0:T(8,128)(2,1)S(1)} %copy-done, bf16[192,1024]{1,0:T(8,128)(2,1)S(1)} %copy-done.1, bf16[192,1024]{1,0:T(8,128)(2,1)S(1)} %copy-done.2), custom_call_target="tpu_custom_call" | custom-call | flops 100000000 | bytes 1000 | tf_op jit(solution)/shard_map/local/pallas_call | solution.py:453
  11.4 0.0 collective-permute-done.two_ref.refs_5_
  11.4 1.6 %collective-permute-start.4 = (bf16[192,256]{1,0:T(8,128)(2,1)S(1)}, bf16[192,256]{1,0:T(8,128)(2,1)S(1)}, u32[]{:S(2)}, u32[]{:S(2)}) collective-permute-start(bf16[192,256]{1,0:T(8,128)(2,1)S(1)} %get-tuple-element.29), channel_id=1, source_target_pairs={{0,4},{4,0},{8,12},{12,8},{16,20},{20,16},{24,28},{28,24},{1,5},{5... | collective-permute-start | bytes 294920 | tf_op jit(solution)/shard_map/ppermute | solution.py:31
  12.9 0.5 %collective-permute-start.5 = (bf16[192,256]{1,0:T(8,128)(2,1)S(1)}, bf16[192,256]{1,0:T(8,128)(2,1)S(1)}, u32[]{:S(2)}, u32[]{:S(2)}) collective-permute-start(bf16[192,256]{1,0:T(8,128)(2,1)S(1)} %get-tuple-element.30), channel_id=1, source_target_pairs={{0,4},{4,0},{8,12},{12,8},{16,20},{20,16},{24,28},{28,24},{1,5},{5... | collective-permute-start | bytes 294920 | tf_op jit(solution)/shard_map/ppermute | solution.py:31
  13.5 1.1 %local.4.local_c = f32[1,56,1024]{2,1,0:T(8,128)S(1)} custom-call(f32[8,1024]{1,0:T(8,128)S(1)} %get-tuple-element.24.slide_ref.refs_0_, bf16[192,1024]{1,0:T(8,128)(2,1)S(1)} %copy-done, bf16[192,1024]{1,0:T(8,128)(2,1)S(1)} %copy-done.1, bf16[192,1024]{1,0:T(8,128)(2,1)S(1)} %copy-done.2), custom_call_target="tpu_custom_call" | custom-call | flops 1000000 | bytes 1000 | tf_op jit(solution)/shard_map/local/pallas_call | solution.py:453
  14.6 0.0 collective-permute-done.2.refs_1_.refs_9_
  14.6 0.2 collective-permute-done.1.refs_0_.refs_8_
  14.8 0.8 %collective-permute-start.6 = (bf16[192,256]{1,0:T(8,128)(2,1)S(1)}, bf16[192,256]{1,0:T(8,128)(2,1)S(1)}, u32[]{:S(2)}, u32[]{:S(2)}) collective-permute-start(bf16[192,256]{1,0:T(8,128)(2,1)S(1)} %pass_on.1), channel_id=1, source_target_pairs={{0,8},{4,12},{8,0},{12,4},{16,24},{20,28},{24,16},{28,20},{1,9},{5... | collective-permute-start | bytes 294920 | tf_op jit(solution)/shard_map/ppermute | solution.py:31
  15.7 2.0 %local.5.local_d = f32[2,56,1024]{2,1,0:T(8,128)S(1)} custom-call(f32[8,1024]{1,0:T(8,128)S(1)} %get-tuple-element.24.slide_ref.refs_0_, bf16[192,1024]{1,0:T(8,128)(2,1)S(1)} %copy-done, bf16[192,1024]{1,0:T(8,128)(2,1)S(1)} %copy-done.1, bf16[192,1024]{1,0:T(8,128)(2,1)S(1)} %copy-done.2), custom_call_target="tpu_custom_call" | custom-call | flops 1000000 | bytes 1000 | tf_op jit(solution)/shard_map/local/pallas_call | solution.py:453
  17.7 0.0 collective-permute-done.3.one_ref.refs_4_
  17.7 0.9 %near.1.near_ref = f32[200,1024]{1,0:T(8,128)S(1)} custom-call(bf16[240,1024]{1,0:T(8,128)(2,1)S(1)} %get-tuple-element.22.q_ref, bf16[48,1024]{1,0:T(8,128)(2,1)S(1)} %get-tuple-element.23.k_mask_ref, f32[1,56,1024]{2,1,0:T(8,128)S(1)} %local.3.local_a, f32[1,56,1024]{2,1,0:T(8,128)S(1)} %local.4.local_c, f32[2,56,1024]{2,1,0:T(8,128)S(1)} %local.5.local_d, ...), custom_call_target="tpu_custom_call" | custom-call | flops 1000000 | bytes 10000 | tf_op jit(solution)/shard_map/near/pallas_call | solution.py:498
  18.6 0.0 collective-permute-done.4.from_one.refs_6_
  18.6 0.0 collective-permute-done.5.from_two.refs_7_
  18.6 0.6 %far.1.near_ref = f32[200,1024]{1,0:T(8,128)S(1)} custom-call(bf16[240,1024]{1,0:T(8,128)(2,1)S(1)} %get-tuple-element.22.q_ref, bf16[48,1024]{1,0:T(8,128)(2,1)S(1)} %get-tuple-element.23.k_mask_ref, f32[200,1024]{1,0:T(8,128)S(1)} %near.1.near_ref, bf16[192,256]{1,0:T(8,128)(2,1)S(1)} %collective-permute-done.4.from_one.refs_6_, ...), custom_call_target="tpu_custom_call" | custom-call | flops 1000000 | bytes 10000 | tf_op jit(solution)/shard_map/far/pallas_call | solution.py:509
  19.2 0.3 %collective-permute-done.6.from_beyond = bf16[192,256]{1,0:T(8,128)(2,1)S(1)} collective-permute-done((bf16[192,256]{1,0:T(8,128)(2,1)S(1)}, bf16[192,256]{1,0:T(8,128)(2,1)S(1)}, u32[]{:S(2)}, u32[]{:S(2)}) %collective-permute-start.6) | collective-permute-done | bytes 98336 | tf_op jit(solution)/shard_map/ppermute | solution.py:31
  19.5 8.8 %last.1 = (f32[192,1024]{1,0:T(8,128)S(1)}, f32[8,256]{1,0:T(8,128)S(1)}) custom-call(bf16[240,1024]{1,0:T(8,128)(2,1)S(1)} %get-tuple-element.22.q_ref, bf16[48,1024]{1,0:T(8,128)(2,1)S(1)} %get-tuple-element.23.k_mask_ref, f32[200,1024]{1,0:T(8,128)S(1)} %far.1.near_ref, bf16[192,256]{1,0:T(8,128)(2,1)S(1)} %collective-permute-done.6.from_beyond, ...), custom_call_target="tpu_custom_call" | custom-call | flops 402653184 | bytes 100000 | tf_op jit(solution)/shard_map/last/pallas_call | solution.py:521
  28.3 0.1 collective-permute-start.9
  28.4 1.6 %collective-permute-start.8 = (f32[8,256]{1,0:T(8,128)S(1)}, f32[8,256]{1,0:T(8,128)S(1)}, u32[]{:S(2)}, u32[]{:S(2)}) collective-permute-start(f32[8,256]{1,0:T(8,128)S(1)} %get-tuple-element.38.refs_0_), channel_id=1, source_target_pairs={{0,2},{1,3},{2,0},{3,1},{4,6},{5,7},{6,4},{7,5},{8,10},{9,11},{10,... | collective-permute-start | bytes 24584 | tf_op jit(solution)/shard_map/ppermute | solution.py:31
  30.0 0.3 collective-permute-start.7
  30.2 1.2 %collective-permute-done.9.refs_3_ = f32[8,256]{1,0:T(8,128)S(1)} collective-permute-done((f32[8,256]{1,0:T(8,128)S(1)}, f32[8,256]{1,0:T(8,128)S(1)}, u32[]{:S(2)}, u32[]{:S(2)}) %collective-permute-start.9) | collective-permute-done | bytes 8224 | tf_op jit(solution)/shard_map/ppermute | solution.py:31
  31.5 0.6 %collective-permute-done.8.refs_2_ = f32[8,256]{1,0:T(8,128)S(1)} collective-permute-done((f32[8,256]{1,0:T(8,128)S(1)}, f32[8,256]{1,0:T(8,128)S(1)}, u32[]{:S(2)}, u32[]{:S(2)}) %collective-permute-start.8) | collective-permute-done | bytes 8224 | tf_op jit(solution)/shard_map/ppermute | solution.py:31
  32.1 0.0 collective-permute-done.7.refs_1_
  32.1 0.9 %norm.1 = bf16[192,1024]{1,0:T(8,128)(2,1)} custom-call(f32[192,1024]{1,0:T(8,128)S(1)} %get-tuple-element.36.att_ref, f32[2,192,128]{2,1,0:T(8,128)S(1)} %get-tuple-element.37.affine_ref, f32[8,256]{1,0:T(8,128)S(1)} %get-tuple-element.38.refs_0_, f32[8,256]{1,0:T(8,128)S(1)} %collective-permute-done.7.refs_1_, ...), custom_call_target="tpu_custom_call" | custom-call | tf_op jit(solution)/shard_map/norm/pallas_call | solution.py:536
  (11 shorter events, 0.0 us)
Async XLA Ops:
  0.0 9.5 %copy-start = (bf16[192,1024]{1,0:T(8,128)(2,1)S(1)}, bf16[192,1024]{1,0:T(8,128)(2,1)}, u32[]{:S(2)}) copy-start(bf16[192,1024]{1,0:T(8,128)(2,1)} %refs_1_.1) | copy-start | bytes 1179652
  0.0 9.5 %copy-start.3 = (f32[192]{0:T(256)S(1)}, f32[192]{0:T(256)}, u32[]{:S(2)}) copy-start(f32[192]{0:T(256)} %param.10) | copy-start | bytes 2308
  0.0 9.5 %copy-start.4 = (f32[192]{0:T(256)S(1)}, f32[192]{0:T(256)}, u32[]{:S(2)}) copy-start(f32[192]{0:T(256)} %param.11) | copy-start | bytes 2308
  0.0 9.5 %copy-start.5 = (s32[8]{0:T(128)S(1)}, s32[8]{0:T(128)}, u32[]{:S(2)}) copy-start(s32[8]{0:T(128)} %lengths_ref.1) | copy-start | bytes 100
  0.0 10.3 %copy-start.2 = (bf16[192,1024]{1,0:T(8,128)(2,1)S(1)}, bf16[192,1024]{1,0:T(8,128)(2,1)}, u32[]{:S(2)}) copy-start(bf16[192,1024]{1,0:T(8,128)(2,1)} %refs_3_.1) | copy-start | bytes 1179652
  2.0 8.3 %copy-start.1 = (bf16[192,1024]{1,0:T(8,128)(2,1)S(1)}, bf16[192,1024]{1,0:T(8,128)(2,1)}, u32[]{:S(2)}) copy-start(bf16[192,1024]{1,0:T(8,128)(2,1)} %refs_2_.1) | copy-start | bytes 1179652
  2.0 9.4 %collective-permute-start = (bf16[384,256]{1,0:T(8,128)(2,1)S(1)}, bf16[384,256]{1,0:T(8,128)(2,1)S(1)}, u32[]{:S(2)}, u32[]{:S(2)}) collective-permute-start(bf16[384,256]{1,0:T(8,128)(2,1)S(1)} %get-tuple-element.25), channel_id=1, source_target_pairs={{0,8},{4,12},{8,0},{12,4},{16,24},{20,28},{24,16},{28,20},{1,9},{5... | collective-permute-start | bytes 589832 | tf_op jit(solution)/shard_map/ppermute | solution.py:31
  5.1 12.6 %collective-permute-start.3 = (bf16[384,256]{1,0:T(8,128)(2,1)S(1)}, bf16[384,256]{1,0:T(8,128)(2,1)S(1)}, u32[]{:S(2)}, u32[]{:S(2)}) collective-permute-start(bf16[384,256]{1,0:T(8,128)(2,1)S(1)} %get-tuple-element.25), channel_id=1, source_target_pairs={{0,4},{4,0},{8,12},{12,8},{16,20},{20,16},{24,28},{28,24},{1,5},{5... | collective-permute-start | bytes 589832 | tf_op jit(solution)/shard_map/ppermute | solution.py:31
  6.6 8.0 %collective-permute-start.2 = (bf16[192,128]{1,0:T(8,128)(2,1)S(1)}, bf16[192,128]{1,0:T(8,128)(2,1)S(1)}, u32[]{:S(2)}, u32[]{:S(2)}) collective-permute-start(bf16[192,128]{1,0:T(8,128)(2,1)S(1)} %get-tuple-element.27), channel_id=1, source_target_pairs={{0,20},{4,16},{8,28},{12,24},{16,4},{20,0},{24,12},{28,8},{1,21},{... | collective-permute-start | bytes 147464 | tf_op jit(solution)/shard_map/ppermute | solution.py:31
  9.1 5.7 %collective-permute-start.1 = (bf16[192,128]{1,0:T(8,128)(2,1)S(1)}, bf16[192,128]{1,0:T(8,128)(2,1)S(1)}, u32[]{:S(2)}, u32[]{:S(2)}) collective-permute-start(bf16[192,128]{1,0:T(8,128)(2,1)S(1)} %get-tuple-element.27), channel_id=1, source_target_pairs={{0,16},{4,20},{8,24},{12,28},{16,0},{20,4},{24,8},{28,12},{1,17},{... | collective-permute-start | bytes 147464 | tf_op jit(solution)/shard_map/ppermute | solution.py:31
  11.4 7.2 %collective-permute-start.4 = (bf16[192,256]{1,0:T(8,128)(2,1)S(1)}, bf16[192,256]{1,0:T(8,128)(2,1)S(1)}, u32[]{:S(2)}, u32[]{:S(2)}) collective-permute-start(bf16[192,256]{1,0:T(8,128)(2,1)S(1)} %get-tuple-element.29), channel_id=1, source_target_pairs={{0,4},{4,0},{8,12},{12,8},{16,20},{20,16},{24,28},{28,24},{1,5},{5... | collective-permute-start | bytes 294920 | tf_op jit(solution)/shard_map/ppermute | solution.py:31
  12.9 5.6 %collective-permute-start.5 = (bf16[192,256]{1,0:T(8,128)(2,1)S(1)}, bf16[192,256]{1,0:T(8,128)(2,1)S(1)}, u32[]{:S(2)}, u32[]{:S(2)}) collective-permute-start(bf16[192,256]{1,0:T(8,128)(2,1)S(1)} %get-tuple-element.30), channel_id=1, source_target_pairs={{0,4},{4,0},{8,12},{12,8},{16,20},{20,16},{24,28},{28,24},{1,5},{5... | collective-permute-start | bytes 294920 | tf_op jit(solution)/shard_map/ppermute | solution.py:31
  14.8 4.7 %collective-permute-start.6 = (bf16[192,256]{1,0:T(8,128)(2,1)S(1)}, bf16[192,256]{1,0:T(8,128)(2,1)S(1)}, u32[]{:S(2)}, u32[]{:S(2)}) collective-permute-start(bf16[192,256]{1,0:T(8,128)(2,1)S(1)} %pass_on.1), channel_id=1, source_target_pairs={{0,8},{4,12},{8,0},{12,4},{16,24},{20,28},{24,16},{28,20},{1,9},{5... | collective-permute-start | bytes 294920 | tf_op jit(solution)/shard_map/ppermute | solution.py:31
  28.3 3.2 %collective-permute-start.9 = (f32[8,256]{1,0:T(8,128)S(1)}, f32[8,256]{1,0:T(8,128)S(1)}, u32[]{:S(2)}, u32[]{:S(2)}) collective-permute-start(f32[8,256]{1,0:T(8,128)S(1)} %get-tuple-element.38.refs_0_), channel_id=1, source_target_pairs={{0,3},{1,2},{2,1},{3,0},{4,7},{5,6},{6,5},{7,4},{8,11},{9,10},{10,... | collective-permute-start | bytes 24584 | tf_op jit(solution)/shard_map/ppermute | solution.py:31
  28.4 3.7 %collective-permute-start.8 = (f32[8,256]{1,0:T(8,128)S(1)}, f32[8,256]{1,0:T(8,128)S(1)}, u32[]{:S(2)}, u32[]{:S(2)}) collective-permute-start(f32[8,256]{1,0:T(8,128)S(1)} %get-tuple-element.38.refs_0_), channel_id=1, source_target_pairs={{0,2},{1,3},{2,0},{3,1},{4,6},{5,7},{6,4},{7,5},{8,10},{9,11},{10,... | collective-permute-start | bytes 24584 | tf_op jit(solution)/shard_map/ppermute | solution.py:31
  30.0 2.1 %collective-permute-start.7 = (f32[8,256]{1,0:T(8,128)S(1)}, f32[8,256]{1,0:T(8,128)S(1)}, u32[]{:S(2)}, u32[]{:S(2)}) collective-permute-start(f32[8,256]{1,0:T(8,128)S(1)} %get-tuple-element.38.refs_0_), channel_id=1, source_target_pairs={{0,1},{1,0},{2,3},{3,2},{4,5},{5,4},{6,7},{7,6},{8,9},{9,8},{10,11... | collective-permute-start | bytes 24584 | tf_op jit(solution)/shard_map/ppermute | solution.py:31
